TPU v7x, 256 devices: a whole 4x4x8 slice. The times are simulated.
256 devices in a mesh: dp: 128 (over z, x_lo, y, core), mp: 2 (over x_hi).
Axes of the slice: x: 4 (x_hi: 2, x_lo: 2; x = x_hi * 2 + x_lo), y: 4, z: 8, core: 2. Of those that a mesh axis runs over, the one named last changes fastest.
Arguments:
- tokens: bfloat16 [131072, 1024], P('dp', 'mp'), may hold values from -6 to 6
- norm_gain: float32 [1024], replicated, may hold values from 0.25 to 1.75
- fc_in: bfloat16 [1024, 4096], P(None, 'mp'), may hold values from -0.1875 to 0.1875
- fc_out: bfloat16 [4096, 1024], P('mp'), may hold values from -0.09375 to 0.09375
- projection: bfloat16 [1024, 1024], P(None, 'mp'), may hold values from -0.1875 to 0.1875
- slots: int32 [128, 1024], P('dp'), may hold values from 0 to 31, never falling along the last dimension, each value on 1 to 64 neighbouring positions
- images: bfloat16 [32768, 1024], P(('dp', 'mp')), may hold values from -6 to 6
- labels: int32 [32768], P(('dp', 'mp')), may hold values from 0 to 4095
- logit_scale: float32 [1], replicated, may hold values from 5 to 15
- logit_bias: float32 [1], replicated, may hold values from -12 to -4
Outputs:
- text_embedding: bfloat16 [4096, 1024], P('dp', 'mp')
- grad_image: float32 [32768, 1024], P(('dp', 'mp'))
- grad_text: float32 [4096, 1024], P('dp', 'mp')
Inputs may be any that keep to these rules, and one draw needn't show every extreme that they name: Within each row the slot numbers never fall; every one of the 32 slots has 1 to 64 tokens, and some slot has exactly 64.
All inputs are finite; a program needn't handle non-finite values.
Results may differ from a plain program's by a relative error of at most 0.0053.
Values may be sent and summed in bfloat16 or wider, within the bound.
No kernel may reach another device: no remote copies, remote signals or barrier semaphores. Data moves between devices by JAX's collectives and lax.ppermute only.
A program may use at most 128 MiB of HBM per device.

v0:
```python
import jax
import jax.numpy as jnp
from jax import lax
from jax.sharding import PartitionSpec as P

CAP_DEV = 32


def on_device(
    tokens, norm_gain, fc_in, fc_out, projection, slots, images, labels, logit_scale, logit_bias
):
    whole = lax.all_gather(tokens, "mp", axis=1, tiled=True)
    states = whole.astype(jnp.float32)
    center = states - jnp.mean(states, axis=1, keepdims=True)
    spread = jnp.mean(center * center, axis=1, keepdims=True)
    normed = (center * lax.rsqrt(spread + 1e-06) * norm_gain[None, :]).astype(jnp.bfloat16)
    hidden = jax.nn.gelu(
        jnp.dot(normed, fc_in, preferred_element_type=jnp.float32), approximate=True
    ).astype(jnp.bfloat16)
    partial_out = jnp.dot(hidden, fc_out, preferred_element_type=jnp.float32)
    slot_row = slots[0]
    members = (slot_row[None, :] == jnp.arange(CAP_DEV, dtype=jnp.int32)[:, None]).astype(
        jnp.float32
    )
    counts = jnp.sum(members, axis=1)
    summed = lax.psum(partial_out, "mp")
    totals = jnp.dot(members, states + summed, precision=lax.Precision.HIGHEST)
    pooled = (totals / counts[:, None]).astype(jnp.bfloat16)
    emb = jnp.dot(pooled, projection, preferred_element_type=jnp.float32)
    squares = lax.psum(jnp.sum(emb * emb, axis=1), "mp")
    text_part = (emb * lax.rsqrt(squares + 1e-06)[:, None]).astype(jnp.bfloat16)
    text_full = lax.all_gather(text_part, "mp", axis=1, tiled=True)
    imgs = images.astype(jnp.float32)
    img = (imgs * lax.rsqrt(jnp.sum(imgs * imgs, axis=1, keepdims=True) + 1e-06)).astype(
        jnp.bfloat16
    )
    scale = logit_scale[0]
    bias = logit_bias[0]
    score_rows, score_marks = (img, labels)
    all_texts = lax.all_gather(text_full, "dp", axis=0, tiled=True)
    columns = jnp.arange(all_texts.shape[0], dtype=jnp.int32)
    logit = (
        scale * jnp.einsum("ie,je->ij", score_rows, all_texts, preferred_element_type=jnp.float32)
        + bias
    )
    sign = jnp.where(score_marks[:, None] == columns[None, :], 1.0, -1.0).astype(jnp.float32)
    weight_all = (-scale * sign * jax.nn.sigmoid(-sign * logit)).astype(jnp.bfloat16)
    grad_image = jnp.dot(weight_all, all_texts, preferred_element_type=jnp.float32)
    lane_grad = lax.psum_scatter(
        jnp.einsum("ij,ie->je", weight_all, img, preferred_element_type=jnp.float32),
        "dp",
        scatter_dimension=0,
        tiled=True,
    )
    grad_text = lax.psum_scatter(lane_grad, "mp", scatter_dimension=1, tiled=True)
    return (text_part, grad_image, grad_text)


def solution(mesh):
    placed = (
        P("dp", "mp"),
        P(),
        P(None, "mp"),
        P("mp", None),
        P(None, "mp"),
        P("dp", None),
        P(("dp", "mp"), None),
        P(("dp", "mp")),
        P(),
        P(),
    )
    return jax.shard_map(
        on_device,
        mesh=mesh,
        in_specs=placed,
        out_specs=(P("dp", "mp"), P(("dp", "mp"), None), P("dp", "mp")),
        check_vma=False,
    )
```

profile of v0, /device:TPU:1, one launch (start us, length us, event | category | flops | bytes accessed | tf_op | source)
XLA Modules:
  0.0 1056.2 jit_solution(6540110498742174289)
XLA Ops:
  7.2 0.0 copy-start
  7.2 0.0 copy-start.5
  7.2 0.0 all-gather.3.cloned.1.call-start
  7.2 0.7 all-gather.3.cloned.1.call-update
  7.9 0.0 all-reduce.2.cloned.1.call-start
  8.0 45.4 %all-gather.3.cloned.1.call-done = bf16[1024,1024]{1,0:T(8,128)(2,1)} async-done(((bf16[1024,512]{1,0:T(8,128)(2,1)}), bf16[1024,1024]{1,0:T(8,128)(2,1)}) %all-gather.3.cloned.1.call-update) | async-done | bytes 2097168 | tf_op jit(solution)/shard_map/all_gather | solution.py:12
  53.4 0.0 copy-start.1
  53.4 2.1 convert_reduce_fusion
  55.4 2.3 fusion.18
  57.7 0.0 copy-done.5
  57.8 0.0 copy-done.1
  57.8 14.5 %fusion.22 = f32[1024,1024]{1,0:T(8,128)} fusion(bf16[2048,1024]{1,0:T(8,128)(2,1)} %param.13, bf16[1024,2048]{1,0:T(8,128)(2,1)} %param.12, bf16[1024,1024]{1,0:T(8,128)(2,1)S(1)} %copy-done.1, f32[1024]{0:T(1024)S(1)} %copy-done.5, f32[1024]{0:T(1024)S(1)} %add_rsqrt_fusion, f32[1024]{0:T(1024)S(1)} %broadcast_multiply_fusion), kind=kOutput, calls=%fused_computation.27 | convolution fusion | flops 8614051840 | bytes 14692352 | tf_op jit(solution)/shard_map/dot_general | solution.py:20
  72.3 0.0 copy-start.4
  72.3 0.0 all-reduce.2.cloned.1.call-update
  72.3 0.0 copy-start.2
  72.3 0.0 copy-start.6
  72.3 0.0 all-gather.5.cloned.1.call-start
  72.4 0.6 copy-done.4
  73.0 0.1 convert_reduce_fusion.1
  73.1 119.9 %all-reduce.2.cloned.1.call-done = f32[1024,1024]{1,0:T(8,128)} async-done(((f32[1024,1024]{1,0:T(8,128)}), f32[1024,1024]{1,0:T(8,128)}) %all-reduce.2.cloned.1.call-update) | async-done | bytes 4194320 | tf_op jit(solution)/shard_map/psum | solution.py:26
  193.0 4.0 fusion.34
  197.1 0.0 copy-done
  197.1 0.4 multiply_reduce_fusion
  197.5 5.3 psum.15
  202.8 0.1 multiply_convert_fusion
  202.8 0.0 copy-start.3
  202.9 5.0 all_gather.10
  207.9 0.0 all-gather.5.cloned.1.call-update
  207.9 0.2 reduce-scatter.3.cloned.1.call-start
  209.4 0.0 copy-done.2
  209.5 0.1 fusion.35
  209.6 219.6 %all-gather.5.cloned.1.call-done = bf16[4096,1024]{1,0:T(8,128)(2,1)} async-done(((bf16[32,1024]{1,0:T(8,128)(2,1)}), bf16[4096,1024]{1,0:T(8,128)(2,1)}) %all-gather.5.cloned.1.call-update) | async-done | bytes 8388624 | tf_op jit(solution)/shard_map/all_gather | solution.py:40
  429.2 0.0 copy-done.6
  429.2 6.7 fusion.17
  435.9 0.0 copy-done.3
  435.9 8.1 fusion.37
  444.0 0.0 reduce-scatter.3.cloned.1.call-update
  444.1 0.0 reduce-scatter.5.cloned.1.call-start
  444.1 583.9 %reduce-scatter.3.cloned.1.call-done = f32[32,1024]{1,0:T(8,128)} async-done(((f32[4096,1024]{1,0:T(8,128)}), f32[32,1024]{1,0:T(8,128)}) %reduce-scatter.3.cloned.1.call-update) | async-done | bytes 131088 | tf_op jit(solution)/shard_map/reduce_scatter | solution.py:49
  1028.0 0.0 reduce-scatter.5.cloned.1.call-update
  1028.1 5.4 fusion.45
  1033.5 16.2 %reduce-scatter.5.cloned.1.call-done = f32[32,512]{1,0:T(8,128)} async-done(((f32[32,1024]{1,0:T(8,128)}), f32[32,512]{1,0:T(8,128)}) %reduce-scatter.5.cloned.1.call-update) | async-done | bytes 65552 | tf_op jit(solution)/shard_map/reduce_scatter | solution.py:55
  (4 shorter events, 0.0 us)
Async XLA Ops:
  7.2 189.9 %copy-start = (bf16[1024,512]{1,0:T(8,128)(2,1)S(1)}, bf16[1024,512]{1,0:T(8,128)(2,1)}, u32[]{:S(2)}) copy-start(bf16[1024,512]{1,0:T(8,128)(2,1)} %param.14) | copy-start | bytes 3145732
  7.2 50.6 %copy-start.5 = (f32[1024]{0:T(1024)S(1)}, f32[1024]{0:T(1024)}, u32[]{:S(2)}) copy-start(f32[1024]{0:T(1024)} %param.11) | copy-start | bytes 12292
  7.2 46.2 %all-gather.3.cloned.1.call-start = ((), (), s32[]{:S(2)}) async-start(), calls=%async_computation.2 | async-start | bytes 3145728 | tf_op jit(solution)/shard_map/all_gather | solution.py:12
  7.9 185.1 %all-reduce.2.cloned.1.call-start = ((), (), s32[]{:S(2)}) async-start(), calls=%async_computation.3 | async-start | bytes 8388608 | tf_op jit(solution)/shard_map/psum | solution.py:26
  53.4 4.4 copy-start.1
  72.3 0.7 copy-start.4
  72.3 137.2 %copy-start.2 = (bf16[128,1024]{1,0:T(8,128)(2,1)S(1)}, bf16[128,1024]{1,0:T(8,128)(2,1)}, u32[]{:S(2)}) copy-start(bf16[128,1024]{1,0:T(8,128)(2,1)} %param.16) | copy-start | bytes 786436
  72.3 356.9 %copy-start.6 = (s32[128]{0:T(128)S(1)}, s32[128]{0:T(128)}, u32[]{:S(2)}) copy-start(s32[128]{0:T(128)} %param.17) | copy-start | bytes 1540
  72.3 356.9 %all-gather.5.cloned.1.call-start = ((), (), s32[]{:S(2)}) async-start(), calls=%async_computation.4 | async-start | bytes 8454144 | tf_op jit(solution)/shard_map/all_gather | solution.py:40
  202.8 233.0 %copy-start.3 = (bf16[32,512]{1,0:T(8,128)(2,1)}, bf16[32,512]{1,0:T(8,128)(2,1)S(1)}, u32[]{:S(2)}) copy-start(bf16[32,512]{1,0:T(8,128)(2,1)S(1)} %multiply_convert_fusion) | copy-start | bytes 98308
  207.9 820.1 %reduce-scatter.3.cloned.1.call-start = ((), (), s32[]{:S(2)}) async-start(), calls=%async_computation.5 | async-start | bytes 16908288 | tf_op jit(solution)/shard_map/reduce_scatter | solution.py:49
  444.1 605.7 %reduce-scatter.5.cloned.1.call-start = ((), (), s32[]{:S(2)}) async-start(), calls=%async_computation.6 | async-start | bytes 196608 | tf_op jit(solution)/shard_map/reduce_scatter | solution.py:55
Sparse Core Ops, SparseCore 0:
  9.8 43.4 all-gather.2
  72.4 120.5 all-reduce.1
  208.0 221.0 all-gather.4
  444.2 583.8 reduce-scatter.2
  1031.1 18.5 reduce-scatter.4
where the time goes:
time: 1060 us
  waiting for transfers between devices  986 us (93%)
  matrix products  39.2 us (4%)
  between operations  15.2 us (1%)
    reduce_scatter x1, waiting for transfers between devices, on_device(): lax.psum_scatter(jnp.einsum('ij,ie->je', weight_all, img, preferred_eleme...  584 us
    all_gather x1, waiting for transfers between devices, on_device(): all_texts = lax.all_gather(text_full, 'dp', axis=0, tiled=True)  220 us
    psum x1, waiting for transfers between devices, on_device(): summed = lax.psum(partial_out, 'mp')  120 us
    all_gather x1, waiting for transfers between devices, on_device(): whole = lax.all_gather(tokens, 'mp', axis=1, tiled=True)  45.4 us
  transfers between devices with their start and end apart: 5, of which 5 were waited for; matrix products, arithmetic and copies ran while one was open for 1% of the time, Pallas kernels for 0%

commit v1 on v0

v1 whole, which is shorter than its diff:
```python
import functools
import jax
import jax.numpy as jnp
from jax import lax
from jax.experimental import pallas as pl
from jax.experimental.pallas import tpu as pltpu
from jax.sharding import Mesh, PartitionSpec as P

CAP_DEV = 32
CHUNKS = 4
FF_TILE = 512
IMG_TILE = 256
IMG_ROWS = 128
PAD = 128
AXES = ("zh", "zl", "xl", "y", "core", "xh")
SIZES = (4, 2, 2, 4, 2, 2)
DP = ("zh", "zl", "xl", "y", "core")
MP = "xh"
BF = jnp.bfloat16
F32 = jnp.float32
SWAP = [(0, 1), (1, 0)]
SMALL = pl.CostEstimate(flops=1000, bytes_accessed=1000, transcendentals=0)


def dot(a, b):
    return jnp.dot(a, b, preferred_element_type=F32)


def shift(n, k):
    return [(i, (i + k) % n) for i in range(n)]


def ring_x(k):
    place = lambda x: (x % 2) * 2 + x // 2
    return [(place(x), place((x + k) % 4)) for x in range(4)]


def mlp_kernel(last, low, slot, own, other, gain, w_in, *refs):
    if last:
        w_out, hid_in, st_in, out, st_out, normed, acc = refs
    else:
        hid_in, st_in, hid_out, st_out, normed = refs
    step = pl.program_id(0)
    half = own.shape[1]
    captions = lax.broadcasted_iota(jnp.int32, (CAP_DEV, own.shape[0]), 0)
    members = (captions == slot[...]).astype(F32).astype(BF)

    @pl.when(step == 0)
    def _():
        is_low = low[0] == 1
        mine = own[...].astype(F32)
        theirs = other[...].astype(F32)
        lo = jnp.where(is_low, mine, theirs)
        hi = jnp.where(is_low, theirs, mine)
        size = 1.0 / (2 * half)
        mean = (jnp.sum(lo, axis=1, keepdims=True) + jnp.sum(hi, axis=1, keepdims=True)) * size
        st_out[:, :half] = st_in[:, :half] + dot(members, lo.astype(BF))
        st_out[:, half:] = st_in[:, half:] + dot(members, hi.astype(BF))
        lo = lo - mean
        hi = hi - mean
        spread = (
            jnp.sum(lo * lo, axis=1, keepdims=True) + jnp.sum(hi * hi, axis=1, keepdims=True)
        ) * size
        inverse = lax.rsqrt(spread + 1e-06)
        normed[:, :half] = (lo * inverse * gain[:, :half]).astype(BF)
        normed[:, half:] = (hi * inverse * gain[:, half:]).astype(BF)

    hidden = jax.nn.gelu(dot(normed[...], w_in[...]), approximate=True).astype(BF)
    total = hid_in[...] + dot(members, hidden)
    if not last:
        hid_out[...] = total
        return
    coarse = total.astype(BF)
    fine = (total - coarse.astype(F32)).astype(BF)
    terms = dot(jnp.concatenate([coarse, fine], axis=0), w_out[...])
    terms = terms[:CAP_DEV] + terms[CAP_DEV:]

    @pl.when(step == 0)
    def _():
        acc[...] = terms

    @pl.when(step > 0)
    def _():
        acc[...] += terms

    @pl.when(step == pl.num_programs(0) - 1)
    def _():
        out[...] = acc[...]


def mlp_chunk(i, last, low, slots, tokens, other, gain, fc_in, fc_out, hidden, states):
    rows, half = other.shape
    d, ff = fc_in.shape
    e = fc_out.shape[1]
    tile_in = pl.BlockSpec((CAP_DEV, FF_TILE), lambda j: (0, j))
    whole = pl.BlockSpec((CAP_DEV, d), lambda j: (0, 0))
    in_specs = [
        pl.BlockSpec(memory_space=pltpu.SMEM),
        pl.BlockSpec((1, rows), lambda j: (0, i)),
        pl.BlockSpec((rows, half), lambda j: (i, 0)),
        pl.BlockSpec((rows, half), lambda j: (0, 0)),
        pl.BlockSpec((1, d), lambda j: (0, 0)),
        pl.BlockSpec((d, FF_TILE), lambda j: (0, j)),
    ]
    args = [low, slots, tokens, other, gain, fc_in]
    scratch = [pltpu.VMEM((rows, d), BF)]
    if last:
        in_specs.append(pl.BlockSpec((FF_TILE, e), lambda j: (j, 0)))
        args.append(fc_out)
        first_shape = jax.ShapeDtypeStruct((CAP_DEV, e), F32)
        first_spec = pl.BlockSpec((CAP_DEV, e), lambda j: (0, 0))
        scratch.append(pltpu.VMEM((CAP_DEV, e), F32))
    else:
        first_shape = jax.ShapeDtypeStruct((CAP_DEV, ff), F32)
        first_spec = tile_in
    return pl.pallas_call(
        functools.partial(mlp_kernel, last),
        grid=(ff // FF_TILE,),
        in_specs=in_specs + [tile_in, whole],
        out_specs=[first_spec, whole],
        out_shape=[first_shape, jax.ShapeDtypeStruct((CAP_DEV, d), F32)],
        scratch_shapes=scratch,
        compiler_params=pltpu.CompilerParams(vmem_limit_bytes=52 << 20),
        cost_estimate=SMALL,
    )(*args, hidden, states)


def loss_kernel(last, scal, columns, texts, img, *refs):
    if last:
        gt_in, gi_out, gt_out, acc = refs
    else:
        gi_out, acc = refs
    step = pl.program_id(0)
    e = texts.shape[1]
    scale, bias = scal[0], scal[1]
    rows = img[:, :e]
    code = img[:, e:].astype(F32)
    marks = (code[:, 0:1] * 64.0 + code[:, 1:2]).astype(jnp.int32)
    logit = lax.dot_general(
        rows, texts[...], (((1,), (1,)), ((), ())), preferred_element_type=F32
    )
    logit = scale * logit + bias
    sign = jnp.where(marks == columns[...], 1.0, -1.0).astype(F32)
    weight = (-scale * sign * jax.nn.sigmoid(-sign * logit)).astype(BF)
    gi_out[...] = dot(weight, texts[...]).astype(gi_out.dtype)
    part = lax.dot_general(weight, rows, (((0,), (0,)), ((), ())), preferred_element_type=F32)

    @pl.when(step == 0)
    def _():
        acc[...] = gt_in[...] + part if last else part

    @pl.when(step > 0)
    def _():
        acc[...] += part

    if last:
        half = e // 2

        @pl.when(step == pl.num_programs(0) - 1)
        def _():
            for g in range(texts.shape[0] // CAP_DEV):
                for h in range(2):
                    gt_out[2 * g + h] = acc[
                        g * CAP_DEV : (g + 1) * CAP_DEV, h * half : (h + 1) * half
                    ].astype(BF)


def loss(last, scal, columns, texts, img, *gt_in):
    n, e = texts.shape
    total = img.shape[0]
    fixed = lambda shape: pl.BlockSpec(shape, lambda j: (0,) * len(shape))
    in_specs = [
        pl.BlockSpec(memory_space=pltpu.SMEM),
        fixed((1, n)),
        fixed((n, e)),
        pl.BlockSpec((IMG_TILE, img.shape[1]), lambda j: (j, 0)),
    ]
    gi_spec = pl.BlockSpec((IMG_TILE, e), lambda j: (j, 0))
    if last:
        in_specs.append(fixed((n, e)))
        shape = (2 * n // CAP_DEV, CAP_DEV, e // 2)
        out_specs = [gi_spec, fixed(shape)]
        out_shape = [
            jax.ShapeDtypeStruct((total, e), F32),
            jax.ShapeDtypeStruct(shape, BF),
        ]
        scratch = [pltpu.VMEM((n, e), F32)]
    else:
        out_specs = [gi_spec, fixed((n, e))]
        out_shape = [
            jax.ShapeDtypeStruct((total, e), BF),
            jax.ShapeDtypeStruct((n, e), F32),
        ]
        scratch = []
    return pl.pallas_call(
        functools.partial(loss_kernel, last),
        grid=(total // IMG_TILE,),
        in_specs=in_specs,
        out_specs=out_specs,
        out_shape=out_shape,
        scratch_shapes=scratch,
        compiler_params=pltpu.CompilerParams(vmem_limit_bytes=52 << 20),
        cost_estimate=SMALL,
    )(scal, columns, texts, img, *gt_in)


def on_device(
    tokens, norm_gain, fc_in, fc_out, projection, slots, images, labels, logit_scale, logit_bias
):
    zh, xl, core, xh = (lax.axis_index(a) for a in ("zh", "xl", "core", "xh"))
    low = xh == 0

    rows = tokens.shape[0] // CHUNKS
    others = [
        lax.ppermute(tokens[i * rows : (i + 1) * rows], MP, SWAP) for i in range(CHUNKS)
    ]

    imgs = images.astype(F32)
    img = (imgs * lax.rsqrt(jnp.sum(imgs * imgs, axis=1, keepdims=True) + 1e-06)).astype(BF)
    code = jnp.stack([labels // 64, labels % 64], axis=1).astype(F32).astype(BF)
    img = jnp.concatenate([img, jnp.pad(code, ((0, 0), (0, PAD - 2)))], axis=1)
    img_mine = jnp.concatenate(
        [img] + [lax.ppermute(img, "zh", shift(4, k)) for k in (1, 2, 3)], axis=0
    )

    members = slots[0][None, :] == jnp.arange(CAP_DEV, dtype=jnp.int32)[:, None]
    counts = jnp.sum(members.astype(F32), axis=1)
    hidden = jnp.zeros((CAP_DEV, fc_in.shape[1]), F32)
    states = jnp.zeros((CAP_DEV, fc_in.shape[0]), F32)
    flag = low.astype(jnp.int32).reshape(1)
    for i, other in enumerate(others):
        last = i == CHUNKS - 1
        if last:
            other, _ = lax.optimization_barrier((other, img_mine))
        hidden, states = mlp_chunk(
            i, last, flag, slots, tokens, other, norm_gain[None, :], fc_in, fc_out, hidden, states
        )
    partial_out, img_sent = lax.optimization_barrier((hidden, img_mine))
    img_other = lax.ppermute(img_sent, "core", SWAP)
    summed = partial_out + lax.ppermute(partial_out, MP, SWAP)
    pooled = ((states + summed) / counts[:, None]).astype(BF)

    emb = dot(pooled, projection)
    emb, img_other = lax.optimization_barrier((emb, img_other))
    before, across, after = [
        lax.ppermute(emb, ("xl", "xh"), ring_x(k)) for k in (1, 2, 3)
    ]
    near_low = xl == xh
    other_low = jnp.where(near_low, after, before)
    other_high = jnp.where(near_low, before, after)
    mine_low = jnp.where(low, emb, across)
    mine_high = jnp.where(low, across, emb)

    def normalised(lo, hi):
        squares = jnp.sum(lo * lo, axis=1, keepdims=True) + jnp.sum(hi * hi, axis=1, keepdims=True)
        inverse = lax.rsqrt(squares + 1e-06)
        return (lo * inverse).astype(BF), (hi * inverse).astype(BF)

    mine_low, mine_high = normalised(mine_low, mine_high)
    other_low, other_high = normalised(other_low, other_high)
    text_part = jnp.where(low, mine_low, mine_high)
    mine = jnp.concatenate([mine_low, mine_high], axis=1)
    other = jnp.concatenate([other_low, other_high], axis=1)
    first = xl == 0
    pair = jnp.concatenate([jnp.where(first, mine, other), jnp.where(first, other, mine)], axis=0)

    texts = lax.all_to_all(
        jnp.broadcast_to(pair[None], (8,) + pair.shape), ("zl", "y"), split_axis=0, concat_axis=0,
        tiled=True,
    ).reshape(16 * CAP_DEV, -1)
    zl_i, y_i, xl_i, cap_i = (
        lax.broadcasted_iota(jnp.int32, (2, 4, 2, CAP_DEV), d) for d in range(4)
    )
    columns = (((((zh * 2 + zl_i) * 2 + xl_i) * 4 + y_i) * 2 + core) * CAP_DEV + cap_i).reshape(1, -1)

    scal = jnp.concatenate([logit_scale, logit_bias])
    gi_send, gt = loss(False, scal, columns, texts, img_other)
    gi_got = lax.ppermute(gi_send, "core", SWAP)
    gi, gt = loss(True, scal, columns, texts, img_mine, gt)

    gi = gi + gi_got.astype(F32)
    grad_image = gi[:IMG_ROWS]
    for k in (1, 2, 3):
        back = gi[k * IMG_ROWS : (k + 1) * IMG_ROWS].astype(BF)
        grad_image += lax.ppermute(back, "zh", shift(4, -k)).astype(F32)

    got = lax.all_to_all(gt, ("zl", "y", "xl", "xh"), split_axis=0, concat_axis=0, tiled=True)
    grad_text = jnp.sum(got.astype(F32), axis=0)
    return (text_part, grad_image, grad_text)


def solution(mesh):
    fine = Mesh(mesh.devices.reshape(SIZES), AXES)
    every = DP + (MP,)
    placed = (
        P(DP, MP),
        P(),
        P(None, MP),
        P(MP, None),
        P(None, MP),
        P(DP, None),
        P(every, None),
        P(every),
        P(),
        P(),
    )
    return jax.shard_map(
        on_device,
        mesh=fine,
        in_specs=placed,
        out_specs=(P(DP, MP), P(every, None), P(DP, MP)),
        check_vma=False,
    )
```

time: 1060 us -> 143 us (0.13)
  waiting for transfers between devices: 986 us -> 41.2 us
  starting transfers between devices: 0.38 us -> 49.6 us
  matrix products: 39.2 us -> 0.33 us
  Pallas kernels: 0 us -> 33.9 us
  between operations: 15.2 us -> 2.26 us
    reduce_scatter x2 -> x0, waiting for transfers between devices: 600 us -> none  [the longest x1 584 us: on_device(): lax.psum_scatter(jnp.einsum('ij,ie->je', weight_all, img, preferred_eleme...]
    all_gather x2 -> x0, waiting for transfers between devices: 265 us -> none  [the longest x1 220 us: on_device(): all_texts = lax.all_gather(text_full, 'dp', axis=0, tiled=True)]
    psum x1 -> x0, waiting for transfers between devices: 120 us -> none  [on_device(): summed = lax.psum(partial_out, 'mp')]
    ppermute x0 -> x16, starting transfers between devices: none -> 40.1 us  [the longest x3 9.35 us: on_device(): lax.ppermute(img, 'zh', shift(4, k))]
    dot_general x6 -> x1, matrix products: 39.2 us -> 0.33 us  [dot(): return jnp.dot(a, b, preferred_element_type=F32)]
    pallas_call x0 -> x6, Pallas kernels: none -> 33.9 us  [the longest x4 22.2 us: mlp_chunk(): pl.pallas_call(functools.partial(mlp_kernel, last), grid=(ff // FF_TILE,)...]
    ppermute x0 -> x16, waiting for transfers between devices: none -> 31.8 us  [the longest x3 25.1 us: on_device(): grad_image += lax.ppermute(back, 'zh', shift(4, -k)).astype(F32)]
  transfers between devices with their start and end apart: 5 -> 18, of which waited for: 5 -> 7; matrix products, arithmetic and copies ran while one was open for 1% -> 3% of each run, Pallas kernels for 0% -> 16%
where the time goes in v1:
time: 143 us; the launch traced here: 140 us
  starting transfers between devices  49.6 us (35%)
  waiting for transfers between devices  41.2 us (29%)
  Pallas kernels  33.9 us (24%)
  local copies, waits for them, and re-layouts  7.11 us (5%)
  other arithmetic  5.74 us (4%)
  between operations  2.26 us (2%)
    ppermute x3, waiting for transfers between devices, on_device(): grad_image += lax.ppermute(back, 'zh', shift(4, -k)).astype(F32)  25.1 us
    pallas_call x4, Pallas kernels, mlp_chunk(): pl.pallas_call(functools.partial(mlp_kernel, last), grid=(ff // FF_TILE,)...  22.2 us
    pallas_call x2, Pallas kernels, loss(): pl.pallas_call(functools.partial(loss_kernel, last), grid=(total // IMG_T...  11.7 us
    all_to_all x1, waiting for transfers between devices, on_device(): lax.all_to_all(jnp.broadcast_to(pair[None], (8,) + pair.shape), ('zl', 'y...  9.38 us
    ppermute x3, starting transfers between devices, on_device(): lax.ppermute(img, 'zh', shift(4, k))  9.35 us
    ppermute x3, starting transfers between devices, on_device(): grad_image += lax.ppermute(back, 'zh', shift(4, -k)).astype(F32)  7.32 us
    ppermute x4, starting transfers between devices, on_device(): lax.ppermute(tokens[i * rows:(i + 1) * rows], MP, SWAP)  6.85 us
    all_to_all x1, starting transfers between devices, on_device(): lax.all_to_all(jnp.broadcast_to(pair[None], (8,) + pair.shape), ('zl', 'y...  5.22 us
  transfers between devices with their start and end apart: 18, of which 7 were waited for; matrix products, arithmetic and copies ran while one was open for 3% of the time, Pallas kernels for 16%

profile of v1, /device:TPU:1, one launch (start us, length us, event | category | flops | bytes accessed | tf_op | source)
XLA Modules:
  0.0 140.2 jit_solution(18025283751051081476)
XLA Ops:
  0.7 2.2 %fusion.11 = (bf16[256,512]{1,0:T(8,128)(2,1)S(1)}, bf16[256,512]{1,0:T(8,128)(2,1)}, bf16[256,512]{1,0:T(8,128)(2,1)}, bf16[256,512]{1,0:T(8,128)(2,1)}) fusion(bf16[1024,512]{1,0:T(8,128)(2,1)} %own.7), kind=kLoop, calls=%fused_computation.51 | loop fusion | bytes 2097152 | tf_op jit(solution)/shard_map/slice | solution.py:215
  2.9 3.6 %collective-permute-start.6 = (bf16[256,512]{1,0:T(8,128)(2,1)S(1)}, bf16[256,512]{1,0:T(8,128)(2,1)S(1)}, u32[]{:S(2)}, u32[]{:S(2)}) collective-permute-start(bf16[256,512]{1,0:T(8,128)(2,1)S(1)} %get-tuple-element.49), channel_id=1, source_target_pairs={{0,1},{1,0},{2,3},{3,2},{4,5},{5,4},{6,7},{7,6},{8,9},{9,8},{10,11... | collective-permute-start | bytes 786440 | tf_op jit(solution)/shard_map/ppermute | solution.py:215
  6.4 0.1 fusion
  6.6 0.1 copy.17
  6.8 0.1 fusion.1
  6.9 6.1 %collective-permute-start.3 = (bf16[128,1152]{1,0:T(8,128)(2,1)S(1)}, bf16[128,1152]{1,0:T(8,128)(2,1)S(1)}, u32[]{:S(2)}, u32[]{:S(2)}) collective-permute-start(bf16[128,1152]{1,0:T(8,128)(2,1)S(1)} %pad_maximum_fusion.1), channel_id=1, source_target_pairs={{0,192},{64,0},{128,64},{192,128},{1,193},{65,1},{129,65},{193,129... | collective-permute-start | bytes 884744 | tf_op jit(solution)/shard_map/ppermute | solution.py:223
  13.0 1.0 collective-permute-start.2
  14.0 2.3 %collective-permute-start.1 = (bf16[128,1152]{1,0:T(8,128)(2,1)S(1)}, bf16[128,1152]{1,0:T(8,128)(2,1)S(1)}, u32[]{:S(2)}, u32[]{:S(2)}) collective-permute-start(bf16[128,1152]{1,0:T(8,128)(2,1)S(1)} %pad_maximum_fusion.1), channel_id=1, source_target_pairs={{0,64},{64,128},{128,192},{192,0},{1,65},{65,129},{129,193},{193,1... | collective-permute-start | bytes 884744 | tf_op jit(solution)/shard_map/ppermute | solution.py:223
  16.3 0.2 collective-permute-start.5
  16.5 2.7 %collective-permute-start.4 = (bf16[256,512]{1,0:T(8,128)(2,1)}, bf16[256,512]{1,0:T(8,128)(2,1)S(1)}, u32[]{:S(2)}, u32[]{:S(2)}) collective-permute-start(bf16[256,512]{1,0:T(8,128)(2,1)} %get-tuple-element.51), channel_id=1, source_target_pairs={{0,1},{1,0},{2,3},{3,2},{4,5},{5,4},{6,7},{7,6},{8,9},{9,8},{10,11... | collective-permute-start | bytes 786440 | tf_op jit(solution)/shard_map/ppermute | solution.py:215
  19.3 5.2 %shard_map.121 = (f32[32,2048]{1,0:T(8,128)S(1)}, f32[32,1024]{1,0:T(8,128)S(1)}) custom-call(s32[1]{0:T(128)} %bitcast.low, s32[1,1024]{1,0:T(1,128)S(1)} %copy-done.2, bf16[1024,512]{1,0:T(8,128)(2,1)} %own.7, bf16[256,512]{1,0:T(8,128)(2,1)S(1)} %collective-permute-done.6.other, f32[1,1024]{1,0:T(1,128)S(1)} %bitcast.10, bf16[1024,2048]{1,0:T(8,128)(2,1)} %w_in.7, ...), custom_call_target="tpu_custom_call" | custom-call | flops 1000 | bytes 1000 | tf_op jit(solution)/shard_map/pallas_call | solution.py:116
  24.6 0.3 collective-permute-start
  24.9 5.2 %shard_map.122 = (f32[32,2048]{1,0:T(8,128)S(1)}, f32[32,1024]{1,0:T(8,128)S(1)}) custom-call(s32[1]{0:T(128)} %bitcast.low, s32[1,1024]{1,0:T(1,128)S(1)} %copy-done.2, bf16[1024,512]{1,0:T(8,128)(2,1)} %own.7, bf16[256,512]{1,0:T(8,128)(2,1)S(1)} %collective-permute-done.5.other, f32[1,1024]{1,0:T(1,128)S(1)} %bitcast.11, bf16[1024,2048]{1,0:T(8,128)(2,1)} %w_in.7, ...), custom_call_target="tpu_custom_call" | custom-call | flops 1000 | bytes 1000 | tf_op jit(solution)/shard_map/pallas_call | solution.py:116
  30.1 5.2 %shard_map.123 = (f32[32,2048]{1,0:T(8,128)S(1)}, f32[32,1024]{1,0:T(8,128)S(1)}) custom-call(s32[1]{0:T(128)} %bitcast.low, s32[1,1024]{1,0:T(1,128)S(1)} %copy-done.2, bf16[1024,512]{1,0:T(8,128)(2,1)} %own.7, bf16[256,512]{1,0:T(8,128)(2,1)S(1)} %collective-permute-done.4.other, f32[1,1024]{1,0:T(1,128)S(1)} %bitcast.12, bf16[1024,2048]{1,0:T(8,128)(2,1)} %w_in.7, ...), custom_call_target="tpu_custom_call" | custom-call | flops 1000 | bytes 1000 | tf_op jit(solution)/shard_map/pallas_call | solution.py:116
  35.3 0.1 pad_maximum_fusion.img
  35.4 1.4 %copy-done.1 = bf16[1024,512]{1,0:T(8,128)(2,1)S(1)} copy-done((bf16[1024,512]{1,0:T(8,128)(2,1)S(1)}, bf16[1024,512]{1,0:T(8,128)(2,1)}, u32[]{:S(2)}) %copy-start.1) | copy-done | bytes 1048600
  36.9 6.6 %shard_map.124 = (f32[32,1024]{1,0:T(8,128)S(1)}, f32[32,1024]{1,0:T(8,128)S(1)}) custom-call(s32[1]{0:T(128)} %bitcast.low, s32[1,1024]{1,0:T(1,128)S(1)} %copy-done.2, bf16[1024,512]{1,0:T(8,128)(2,1)S(1)} %copy-done.1, bf16[256,512]{1,0:T(8,128)(2,1)S(1)} %collective-permute-done.other, f32[1,1024]{1,0:T(1,128)S(1)} %bitcast.13, bf16[1024,2048]{1,0:T(8,128)(2,1)} %w_in.7, ...), custom_call_target="tpu_custom_call" | custom-call | flops 1000 | bytes 1000 | tf_op jit(solution)/shard_map/pallas_call | solution.py:116
  43.5 4.8 %collective-permute-start.8 = (bf16[512,1152]{1,0:T(8,128)(2,1)S(1)}, bf16[512,1152]{1,0:T(8,128)(2,1)S(1)}, u32[]{:S(2)}, u32[]{:S(2)}) collective-permute-start(bf16[512,1152]{1,0:T(8,128)(2,1)S(1)} %pad_maximum_fusion.img), channel_id=1, source_target_pairs={{0,2},{2,0},{1,3},{3,1},{4,6},{6,4},{5,7},{7,5},{8,10},{10,8},{9,1... | collective-permute-start | bytes 3538952 | tf_op jit(solution)/shard_map/ppermute | solution.py:239
  48.2 2.8 %collective-permute-start.7 = (f32[32,1024]{1,0:T(8,128)S(1)}, f32[32,1024]{1,0:T(8,128)S(1)}, u32[]{:S(2)}, u32[]{:S(2)}) collective-permute-start(f32[32,1024]{1,0:T(8,128)S(1)} %get-tuple-element.29), channel_id=1, source_target_pairs={{0,1},{1,0},{2,3},{3,2},{4,5},{5,4},{6,7},{7,6},{8,9},{9,8},{10,11... | collective-permute-start | bytes 393224 | tf_op jit(solution)/shard_map/ppermute | solution.py:240
  51.0 0.1 convert_reduce_fusion.1
  51.1 3.7 %collective-permute-done.7 = f32[32,1024]{1,0:T(8,128)S(1)} collective-permute-done((f32[32,1024]{1,0:T(8,128)S(1)}, f32[32,1024]{1,0:T(8,128)S(1)}, u32[]{:S(2)}, u32[]{:S(2)}) %collective-permute-start.7) | collective-permute-done | bytes 131104 | tf_op jit(solution)/shard_map/ppermute | solution.py:240
  54.8 0.3 fusion.4
  55.2 1.0 copy-done.6
  56.2 1.2 collective-permute-start.11
  57.4 1.5 %collective-permute-start.10 = (f32[32,512]{1,0:T(8,128)S(1)}, f32[32,512]{1,0:T(8,128)S(1)}, u32[]{:S(2)}, u32[]{:S(2)}) collective-permute-start(f32[32,512]{1,0:T(8,128)S(1)} %fusion.4), channel_id=1, source_target_pairs={{0,17},{16,0},{1,16},{17,1},{2,19},{18,2},{3,18},{19,3},{4,21},{20... | collective-permute-start | bytes 196616 | tf_op jit(solution)/shard_map/ppermute | solution.py:246
  58.9 1.5 %collective-permute-start.9 = (f32[32,512]{1,0:T(8,128)S(1)}, f32[32,512]{1,0:T(8,128)S(1)}, u32[]{:S(2)}, u32[]{:S(2)}) collective-permute-start(f32[32,512]{1,0:T(8,128)S(1)} %fusion.4), channel_id=1, source_target_pairs={{0,1},{16,17},{1,0},{17,16},{2,3},{18,19},{3,2},{19,18},{4,5},{20,... | collective-permute-start | bytes 196616 | tf_op jit(solution)/shard_map/ppermute | solution.py:246
  60.4 0.1 collective-permute-done.11
  60.5 0.1 multiply_reduce_fusion
  60.6 2.9 %collective-permute-done.9 = f32[32,512]{1,0:T(8,128)S(1)} collective-permute-done((f32[32,512]{1,0:T(8,128)S(1)}, f32[32,512]{1,0:T(8,128)S(1)}, u32[]{:S(2)}, u32[]{:S(2)}) %collective-permute-start.9) | collective-permute-done | bytes 65568 | tf_op jit(solution)/shard_map/ppermute | solution.py:246
  63.5 0.1 multiply_reduce_fusion.2
  63.7 0.7 broadcast_select_fusion.4
  64.5 1.1 broadcast_in_dim.11
  65.6 5.2 %all-to-all-start = ((bf16[8,64,1024]{2,1,0:T(8,128)(2,1)}), bf16[8,64,1024]{2,1,0:T(8,128)(2,1)S(1)}, u32[]{:S(2)}, u32[]{:S(2)}) async-start(bf16[8,64,1024]{2,1,0:T(8,128)(2,1)} %broadcast_in_dim.11), calls=%async_computation | async-start | bytes 2097152 | tf_op jit(solution)/shard_map/all_to_all | solution.py:267
  72.2 0.1 reshape.120.columns
  72.4 9.4 %all-to-all-done = bf16[8,64,1024]{2,1,0:T(8,128)(2,1)S(1)} async-done(((bf16[8,64,1024]{2,1,0:T(8,128)(2,1)}), bf16[8,64,1024]{2,1,0:T(8,128)(2,1)S(1)}, u32[]{:S(2)}, u32[]{:S(2)}) %all-to-all-start) | async-done | bytes 1048608 | tf_op jit(solution)/shard_map/all_to_all | solution.py:267
  81.8 1.0 copy-done.4
  82.7 5.4 %shard_map.125 = (bf16[512,1024]{1,0:T(8,128)(2,1)S(1)}, f32[512,1024]{1,0:T(8,128)}) custom-call(f32[2]{0:T(128)S(1)} %pad_maximum_fusion.5.scal, s32[1,512]{1,0:T(1,128)S(1)} %reshape.120.columns, bf16[512,1024]{1,0:T(8,128)(2,1)} %bitcast.14, bf16[512,1152]{1,0:T(8,128)(2,1)} %copy-done.6), custom_call_target="tpu_custom_call" | custom-call | flops 1000 | bytes 1000 | tf_op jit(solution)/shard_map/pallas_call | solution.py:195
  88.2 4.8 %collective-permute-start.12 = (bf16[512,1024]{1,0:T(8,128)(2,1)S(1)}, bf16[512,1024]{1,0:T(8,128)(2,1)}, u32[]{:S(2)}, u32[]{:S(2)}) collective-permute-start(bf16[512,1024]{1,0:T(8,128)(2,1)S(1)} %get-tuple-element.35), channel_id=1, source_target_pairs={{0,2},{2,0},{1,3},{3,1},{4,6},{6,4},{5,7},{7,5},{8,10},{10,8},{9,1... | collective-permute-start | bytes 3145736 | tf_op jit(solution)/shard_map/ppermute | solution.py:278
  93.0 6.3 %shard_map.126 = (f32[512,1024]{1,0:T(8,128)}, bf16[32,32,512]{2,1,0:T(8,128)(2,1)}) custom-call(f32[2]{0:T(128)S(1)} %pad_maximum_fusion.5.scal, s32[1,512]{1,0:T(1,128)S(1)} %reshape.120.columns, bf16[512,1024]{1,0:T(8,128)(2,1)} %bitcast.15, bf16[512,1152]{1,0:T(8,128)(2,1)} %copy-done.5, f32[512,1024]{1,0:T(8,128)} %get-tuple-element.33.refs_0_), custom_call_target="tpu_custom_call" | custom-call | flops 1000 | bytes 1000 | tf_op jit(solution)/shard_map/pallas_call | solution.py:195
  99.3 4.4 %all-to-all-start.1 = ((bf16[32,32,512]{2,1,0:T(8,128)(2,1)}), bf16[32,32,512]{2,1,0:T(8,128)(2,1)S(1)}, u32[]{:S(2)}, u32[]{:S(2)}) async-start(bf16[32,32,512]{2,1,0:T(8,128)(2,1)} %get-tuple-element.36), calls=%async_computation.1 | async-start | bytes 2097152 | tf_op jit(solution)/shard_map/all_to_all | solution.py:287
  103.7 2.3 %fusion.9 = (bf16[512,1024]{1,0:T(8,128)(2,1)S(1)}, f32[512,1024]{1,0:T(8,128)S(1)}) fusion(f32[512,1024]{1,0:T(8,128)} %get-tuple-element.34, bf16[512,1024]{1,0:T(8,128)(2,1)} %collective-permute-done.12), kind=kLoop, calls=%fused_computation.49 | loop fusion | flops 1572864 | bytes 6291456 | tf_op jit(solution)/shard_map/convert.3
  106.0 3.8 %collective-permute-start.13 = (bf16[128,1024]{1,0:T(8,128)(2,1)S(1)}, bf16[128,1024]{1,0:T(8,128)(2,1)S(1)}, u32[]{:S(2)}, u32[]{:S(2)}) collective-permute-start(bf16[128,1024]{1,0:T(8,128)(2,1)S(1)} %get-tuple-element.46), channel_id=1, source_target_pairs={{0,192},{64,0},{128,64},{192,128},{1,193},{65,1},{129,65},{193,129... | collective-permute-start | bytes 786440 | tf_op jit(solution)/shard_map/ppermute | solution.py:285
  109.8 3.5 %collective-permute-start.14 = (bf16[128,1024]{1,0:T(8,128)(2,1)S(1)}, bf16[128,1024]{1,0:T(8,128)(2,1)S(1)}, u32[]{:S(2)}, u32[]{:S(2)}) collective-permute-start(bf16[128,1024]{1,0:T(8,128)(2,1)S(1)} %get-tuple-element.48), channel_id=1, source_target_pairs={{0,128},{64,192},{128,0},{192,64},{1,129},{65,193},{129,1},{193,65... | collective-permute-start | bytes 786440 | tf_op jit(solution)/shard_map/ppermute | solution.py:285
  113.4 1.9 %collective-permute-done.13 = bf16[128,1024]{1,0:T(8,128)(2,1)S(1)} collective-permute-done((bf16[128,1024]{1,0:T(8,128)(2,1)S(1)}, bf16[128,1024]{1,0:T(8,128)(2,1)S(1)}, u32[]{:S(2)}, u32[]{:S(2)}) %collective-permute-start.13) | collective-permute-done | bytes 262176 | tf_op jit(solution)/shard_map/ppermute | solution.py:285
  115.3 15.4 %collective-permute-done.15 = bf16[128,1024]{1,0:T(8,128)(2,1)S(1)} collective-permute-done((bf16[128,1024]{1,0:T(8,128)(2,1)S(1)}, bf16[128,1024]{1,0:T(8,128)(2,1)S(1)}, u32[]{:S(2)}, u32[]{:S(2)}) %collective-permute-start.15) | collective-permute-done | bytes 262176 | tf_op jit(solution)/shard_map/ppermute | solution.py:285
  130.7 7.7 %collective-permute-done.14 = bf16[128,1024]{1,0:T(8,128)(2,1)S(1)} collective-permute-done((bf16[128,1024]{1,0:T(8,128)(2,1)S(1)}, bf16[128,1024]{1,0:T(8,128)(2,1)S(1)}, u32[]{:S(2)}, u32[]{:S(2)}) %collective-permute-start.14) | collective-permute-done | bytes 262176 | tf_op jit(solution)/shard_map/ppermute | solution.py:285
  138.5 0.9 fusion.3
  139.4 0.8 convert_reduce_fusion
  (45 shorter events, 0.5 us)
Async XLA Ops:
  0.6 54.2 %copy-start = (bf16[1024,512]{1,0:T(8,128)(2,1)S(1)}, bf16[1024,512]{1,0:T(8,128)(2,1)}, u32[]{:S(2)}) copy-start(bf16[1024,512]{1,0:T(8,128)(2,1)} %param.14) | copy-start | bytes 3145732
  0.6 5.8 %copy-start.7 = (bf16[128,1024]{1,0:T(8,128)(2,1)S(1)}, bf16[128,1024]{1,0:T(8,128)(2,1)}, u32[]{:S(2)}) copy-start(bf16[128,1024]{1,0:T(8,128)(2,1)} %param.16) | copy-start | bytes 786436
  0.7 5.9 %copy-start.9 = (s32[128]{0:T(128)S(1)}, s32[128]{0:T(128)}, u32[]{:S(2)}) copy-start(s32[128]{0:T(128)} %param.17) | copy-start | bytes 1540
  0.7 18.6 %copy-start.2 = (s32[1,1024]{1,0:T(1,128)S(1)}, s32[1,1024]{1,0:T(1,128)}, u32[]{:S(2)}) copy-start(s32[1,1024]{1,0:T(1,128)} %slot.7) | copy-start | bytes 12292
  0.7 18.6 %copy-start.3 = (f32[1024]{0:T(1024)S(1)}, f32[1024]{0:T(1024)}, u32[]{:S(2)}) copy-start(f32[1024]{0:T(1024)} %param.11) | copy-start | bytes 12292
  2.9 13.6 %collective-permute-start.6 = (bf16[256,512]{1,0:T(8,128)(2,1)S(1)}, bf16[256,512]{1,0:T(8,128)(2,1)S(1)}, u32[]{:S(2)}, u32[]{:S(2)}) collective-permute-start(bf16[256,512]{1,0:T(8,128)(2,1)S(1)} %get-tuple-element.49), channel_id=1, source_target_pairs={{0,1},{1,0},{2,3},{3,2},{4,5},{5,4},{6,7},{7,6},{8,9},{9,8},{10,11... | collective-permute-start | bytes 786440 | tf_op jit(solution)/shard_map/ppermute | solution.py:215
  6.9 28.3 %collective-permute-start.3 = (bf16[128,1152]{1,0:T(8,128)(2,1)S(1)}, bf16[128,1152]{1,0:T(8,128)(2,1)S(1)}, u32[]{:S(2)}, u32[]{:S(2)}) collective-permute-start(bf16[128,1152]{1,0:T(8,128)(2,1)S(1)} %pad_maximum_fusion.1), channel_id=1, source_target_pairs={{0,192},{64,0},{128,64},{192,128},{1,193},{65,1},{129,65},{193,129... | collective-permute-start | bytes 884744 | tf_op jit(solution)/shard_map/ppermute | solution.py:223
  13.0 22.2 %collective-permute-start.2 = (bf16[128,1152]{1,0:T(8,128)(2,1)S(1)}, bf16[128,1152]{1,0:T(8,128)(2,1)S(1)}, u32[]{:S(2)}, u32[]{:S(2)}) collective-permute-start(bf16[128,1152]{1,0:T(8,128)(2,1)S(1)} %pad_maximum_fusion.1), channel_id=1, source_target_pairs={{0,128},{64,192},{128,0},{192,64},{1,129},{65,193},{129,1},{193,65... | collective-permute-start | bytes 884744 | tf_op jit(solution)/shard_map/ppermute | solution.py:223
  14.0 21.3 %collective-permute-start.1 = (bf16[128,1152]{1,0:T(8,128)(2,1)S(1)}, bf16[128,1152]{1,0:T(8,128)(2,1)S(1)}, u32[]{:S(2)}, u32[]{:S(2)}) collective-permute-start(bf16[128,1152]{1,0:T(8,128)(2,1)S(1)} %pad_maximum_fusion.1), channel_id=1, source_target_pairs={{0,64},{64,128},{128,192},{192,0},{1,65},{65,129},{129,193},{193,1... | collective-permute-start | bytes 884744 | tf_op jit(solution)/shard_map/ppermute | solution.py:223
  16.3 8.3 %collective-permute-start.5 = (bf16[256,512]{1,0:T(8,128)(2,1)}, bf16[256,512]{1,0:T(8,128)(2,1)S(1)}, u32[]{:S(2)}, u32[]{:S(2)}) collective-permute-start(bf16[256,512]{1,0:T(8,128)(2,1)} %get-tuple-element.50), channel_id=1, source_target_pairs={{0,1},{1,0},{2,3},{3,2},{4,5},{5,4},{6,7},{7,6},{8,9},{9,8},{10,11... | collective-permute-start | bytes 786440 | tf_op jit(solution)/shard_map/ppermute | solution.py:215
  16.5 13.5 %collective-permute-start.4 = (bf16[256,512]{1,0:T(8,128)(2,1)}, bf16[256,512]{1,0:T(8,128)(2,1)S(1)}, u32[]{:S(2)}, u32[]{:S(2)}) collective-permute-start(bf16[256,512]{1,0:T(8,128)(2,1)} %get-tuple-element.51), channel_id=1, source_target_pairs={{0,1},{1,0},{2,3},{3,2},{4,5},{5,4},{6,7},{7,6},{8,9},{9,8},{10,11... | collective-permute-start | bytes 786440 | tf_op jit(solution)/shard_map/ppermute | solution.py:215
  19.3 5.2 %copy-start.8 = (bf16[256,512]{1,0:T(8,128)(2,1)S(1)}, bf16[256,512]{1,0:T(8,128)(2,1)}, u32[]{:S(2)}) copy-start(bf16[256,512]{1,0:T(8,128)(2,1)} %get-tuple-element.52) | copy-start | bytes 786436
  24.6 10.8 %collective-permute-start = (bf16[256,512]{1,0:T(8,128)(2,1)S(1)}, bf16[256,512]{1,0:T(8,128)(2,1)S(1)}, u32[]{:S(2)}, u32[]{:S(2)}) collective-permute-start(bf16[256,512]{1,0:T(8,128)(2,1)S(1)} %copy-done.8), channel_id=1, source_target_pairs={{0,1},{1,0},{2,3},{3,2},{4,5},{5,4},{6,7},{7,6},{8,9},{9,8},{10,11... | collective-permute-start | bytes 786440 | tf_op jit(solution)/shard_map/ppermute | solution.py:215
  35.3 1.6 %copy-start.1 = (bf16[1024,512]{1,0:T(8,128)(2,1)S(1)}, bf16[1024,512]{1,0:T(8,128)(2,1)}, u32[]{:S(2)}) copy-start(bf16[1024,512]{1,0:T(8,128)(2,1)} %own.7) | copy-start | bytes 3145732
  35.4 8.1 %copy-start.5 = (bf16[512,1152]{1,0:T(8,128)(2,1)}, bf16[512,1152]{1,0:T(8,128)(2,1)S(1)}, u32[]{:S(2)}) copy-start(bf16[512,1152]{1,0:T(8,128)(2,1)S(1)} %pad_maximum_fusion.img) | copy-start | bytes 3538948
  43.5 11.6 %collective-permute-start.8 = (bf16[512,1152]{1,0:T(8,128)(2,1)S(1)}, bf16[512,1152]{1,0:T(8,128)(2,1)S(1)}, u32[]{:S(2)}, u32[]{:S(2)}) collective-permute-start(bf16[512,1152]{1,0:T(8,128)(2,1)S(1)} %pad_maximum_fusion.img), channel_id=1, source_target_pairs={{0,2},{2,0},{1,3},{3,1},{4,6},{6,4},{5,7},{7,5},{8,10},{10,8},{9,1... | collective-permute-start | bytes 3538952 | tf_op jit(solution)/shard_map/ppermute | solution.py:239
  48.2 6.6 %collective-permute-start.7 = (f32[32,1024]{1,0:T(8,128)S(1)}, f32[32,1024]{1,0:T(8,128)S(1)}, u32[]{:S(2)}, u32[]{:S(2)}) collective-permute-start(f32[32,1024]{1,0:T(8,128)S(1)} %get-tuple-element.29), channel_id=1, source_target_pairs={{0,1},{1,0},{2,3},{3,2},{4,5},{5,4},{6,7},{7,6},{8,9},{9,8},{10,11... | collective-permute-start | bytes 393224 | tf_op jit(solution)/shard_map/ppermute | solution.py:240
  55.1 1.0 copy-start.6
  56.2 4.3 %collective-permute-start.11 = (f32[32,512]{1,0:T(8,128)S(1)}, f32[32,512]{1,0:T(8,128)S(1)}, u32[]{:S(2)}, u32[]{:S(2)}) collective-permute-start(f32[32,512]{1,0:T(8,128)S(1)} %fusion.4), channel_id=1, source_target_pairs={{0,16},{16,1},{1,17},{17,0},{2,18},{18,3},{3,19},{19,2},{4,20},{20... | collective-permute-start | bytes 196616 | tf_op jit(solution)/shard_map/ppermute | solution.py:246
  57.4 3.1 %collective-permute-start.10 = (f32[32,512]{1,0:T(8,128)S(1)}, f32[32,512]{1,0:T(8,128)S(1)}, u32[]{:S(2)}, u32[]{:S(2)}) collective-permute-start(f32[32,512]{1,0:T(8,128)S(1)} %fusion.4), channel_id=1, source_target_pairs={{0,17},{16,0},{1,16},{17,1},{2,19},{18,2},{3,18},{19,3},{4,21},{20... | collective-permute-start | bytes 196616 | tf_op jit(solution)/shard_map/ppermute | solution.py:246
  58.9 4.7 %collective-permute-start.9 = (f32[32,512]{1,0:T(8,128)S(1)}, f32[32,512]{1,0:T(8,128)S(1)}, u32[]{:S(2)}, u32[]{:S(2)}) collective-permute-start(f32[32,512]{1,0:T(8,128)S(1)} %fusion.4), channel_id=1, source_target_pairs={{0,1},{16,17},{1,0},{17,16},{2,3},{18,19},{3,2},{19,18},{4,5},{20,... | collective-permute-start | bytes 196616 | tf_op jit(solution)/shard_map/ppermute | solution.py:246
  65.6 16.2 %all-to-all-start = ((bf16[8,64,1024]{2,1,0:T(8,128)(2,1)}), bf16[8,64,1024]{2,1,0:T(8,128)(2,1)S(1)}, u32[]{:S(2)}, u32[]{:S(2)}) async-start(bf16[8,64,1024]{2,1,0:T(8,128)(2,1)} %broadcast_in_dim.11), calls=%async_computation | async-start | bytes 2097152 | tf_op jit(solution)/shard_map/all_to_all | solution.py:267
  81.8 1.0 copy-start.4
  88.2 15.5 %collective-permute-start.12 = (bf16[512,1024]{1,0:T(8,128)(2,1)S(1)}, bf16[512,1024]{1,0:T(8,128)(2,1)}, u32[]{:S(2)}, u32[]{:S(2)}) collective-permute-start(bf16[512,1024]{1,0:T(8,128)(2,1)S(1)} %get-tuple-element.35), channel_id=1, source_target_pairs={{0,2},{2,0},{1,3},{3,1},{4,6},{6,4},{5,7},{7,5},{8,10},{10,8},{9,1... | collective-permute-start | bytes 3145736 | tf_op jit(solution)/shard_map/ppermute | solution.py:278
  99.3 40.1 %all-to-all-start.1 = ((bf16[32,32,512]{2,1,0:T(8,128)(2,1)}), bf16[32,32,512]{2,1,0:T(8,128)(2,1)S(1)}, u32[]{:S(2)}, u32[]{:S(2)}) async-start(bf16[32,32,512]{2,1,0:T(8,128)(2,1)} %get-tuple-element.36), calls=%async_computation.1 | async-start | bytes 2097152 | tf_op jit(solution)/shard_map/all_to_all | solution.py:287
  106.0 9.3 %collective-permute-start.13 = (bf16[128,1024]{1,0:T(8,128)(2,1)S(1)}, bf16[128,1024]{1,0:T(8,128)(2,1)S(1)}, u32[]{:S(2)}, u32[]{:S(2)}) collective-permute-start(bf16[128,1024]{1,0:T(8,128)(2,1)S(1)} %get-tuple-element.46), channel_id=1, source_target_pairs={{0,192},{64,0},{128,64},{192,128},{1,193},{65,1},{129,65},{193,129... | collective-permute-start | bytes 786440 | tf_op jit(solution)/shard_map/ppermute | solution.py:285
  109.8 20.9 %collective-permute-start.15 = (bf16[128,1024]{1,0:T(8,128)(2,1)S(1)}, bf16[128,1024]{1,0:T(8,128)(2,1)S(1)}, u32[]{:S(2)}, u32[]{:S(2)}) collective-permute-start(bf16[128,1024]{1,0:T(8,128)(2,1)S(1)} %get-tuple-element.47), channel_id=1, source_target_pairs={{0,64},{64,128},{128,192},{192,0},{1,65},{65,129},{129,193},{193,1... | collective-permute-start | bytes 786440 | tf_op jit(solution)/shard_map/ppermute | solution.py:285
  109.8 28.6 %collective-permute-start.14 = (bf16[128,1024]{1,0:T(8,128)(2,1)S(1)}, bf16[128,1024]{1,0:T(8,128)(2,1)S(1)}, u32[]{:S(2)}, u32[]{:S(2)}) collective-permute-start(bf16[128,1024]{1,0:T(8,128)(2,1)S(1)} %get-tuple-element.48), channel_id=1, source_target_pairs={{0,128},{64,192},{128,0},{192,64},{1,129},{65,193},{129,1},{193,65... | collective-permute-start | bytes 786440 | tf_op jit(solution)/shard_map/ppermute | solution.py:285

commit v2 on v0

v2 whole, which is shorter than its diff:
```python
import functools
import jax
import jax.numpy as jnp
from jax import lax
from jax.experimental import pallas as pl
from jax.experimental.pallas import tpu as pltpu
from jax.sharding import Mesh, PartitionSpec as P

CAP_DEV = 32
ROW_TILE = 512
FF_TILE = 1024
IMG_ROWS = 128
GELU_A = 0.7978845608028654
GELU_B = GELU_A * 0.044715
PAD = 128
AXES = ("zh", "zl", "xl", "y", "core", "xh")
SIZES = (4, 2, 2, 4, 2, 2)
DP = ("zh", "zl", "xl", "y", "core")
MP = "xh"
BF = jnp.bfloat16
F32 = jnp.float32
SWAP = [(0, 1), (1, 0)]
LARGE = pl.CostEstimate(flops=10**10, bytes_accessed=1000, transcendentals=0)
SMALL = pl.CostEstimate(flops=1000, bytes_accessed=1000, transcendentals=0)


def dot(a, b):
    return jnp.dot(a, b, preferred_element_type=F32)


def shift(n, k):
    return [(i, (i + k) % n) for i in range(n)]


def mlp_kernel(row_tile, ff_tile, low, slot, own, other, gain, fc_in, fc_out, out, st_out, w_in, w_out, sems):
    rows, half = own.shape
    ff = w_in.shape[1]
    tiles = [pl.ds(j * ff_tile, ff_tile) for j in range(ff // ff_tile)]
    loads = [
        pltpu.make_async_copy(fc_in.at[:, t], w_in.at[:, t], sems.at[j])
        for j, t in enumerate(tiles)
    ]
    loads.append(pltpu.make_async_copy(fc_out, w_out, sems.at[len(tiles)]))
    for load in loads:
        load.start()
    size = 1.0 / (2 * half)
    is_low = low[0] == 1
    pooled = [jnp.zeros((CAP_DEV, ff_tile), F32) for _ in range(ff // ff_tile)]
    states = [jnp.zeros((CAP_DEV, half), F32) for _ in range(2)]
    for r in range(0, rows, row_tile):
        block = slice(r, r + row_tile)
        captions = lax.broadcasted_iota(jnp.int32, (CAP_DEV, row_tile), 0)
        members = (captions == slot[:, block]).astype(F32).astype(BF)
        mine = own[block, :]
        theirs = other[block, :]
        lo = jnp.where(is_low, mine, theirs)
        hi = jnp.where(is_low, theirs, mine)
        states[0] += dot(members, lo)
        states[1] += dot(members, hi)
        lo = lo.astype(F32)
        hi = hi.astype(F32)
        mean = (jnp.sum(lo, axis=1, keepdims=True) + jnp.sum(hi, axis=1, keepdims=True)) * size
        lo = lo - mean
        hi = hi - mean
        spread = (
            jnp.sum(lo * lo, axis=1, keepdims=True) + jnp.sum(hi * hi, axis=1, keepdims=True)
        ) * size
        inverse = lax.rsqrt(spread + 1e-06)
        normed = jnp.concatenate(
            [
                (lo * inverse * gain[:, :half]).astype(BF),
                (hi * inverse * gain[:, half:]).astype(BF),
            ],
            axis=1,
        )
        for j in range(ff // ff_tile):
            if r == 0:
                loads[j].wait()
            pre = dot(normed, w_in[:, j * ff_tile : (j + 1) * ff_tile])
            pre_half = 0.5 * pre
            bend = jnp.tanh(pre * (GELU_A + GELU_B * (pre * pre)))
            hidden = (pre_half + pre_half * bend).astype(BF)
            pooled[j] += dot(members, hidden)
    st_out[:, :half] = states[0]
    st_out[:, half:] = states[1]
    loads[-1].wait()
    terms = jnp.zeros((2 * CAP_DEV, w_out.shape[1]), F32)
    for j in range(ff // ff_tile):
        coarse = pooled[j].astype(BF)
        fine = (pooled[j] - coarse.astype(F32)).astype(BF)
        terms += dot(
            jnp.concatenate([coarse, fine], axis=0), w_out[j * ff_tile : (j + 1) * ff_tile, :]
        )
    out[...] = terms[:CAP_DEV] + terms[CAP_DEV:]


def weights_of(scal, columns, texts, img):
    e = texts.shape[1]
    scale, bias = scal[0], scal[1]
    code = img[:, e:].astype(F32)
    marks = (code[:, 0:1] * 64.0 + code[:, 1:2]).astype(jnp.int32)
    logit = lax.dot_general(
        img[:, :e], texts, (((1,), (1,)), ((), ())), preferred_element_type=F32
    )
    logit = scale * logit + bias
    sign = jnp.where(marks == columns[...], 1.0, -1.0).astype(F32)
    return (-scale * sign * jax.nn.sigmoid(-sign * logit)).astype(BF)


def first_kernel(scal, columns, emb, img, texts, weight, gi):
    half = emb.shape[3]
    for g in range(emb.shape[0]):
        lo = emb[g, 0].astype(F32)
        hi = emb[g, 1].astype(F32)
        squares = jnp.sum(lo * lo, axis=1, keepdims=True) + jnp.sum(hi * hi, axis=1, keepdims=True)
        inverse = lax.rsqrt(squares + 1e-06)
        rows = slice(g * CAP_DEV, (g + 1) * CAP_DEV)
        texts[rows, :half] = (lo * inverse).astype(BF)
        texts[rows, half:] = (hi * inverse).astype(BF)
    w = weights_of(scal, columns, texts[...], img)
    weight[...] = w
    gi[...] = dot(w, texts[...]).astype(BF)


def second_kernel(scal, columns, texts, img, weight):
    weight[...] = weights_of(scal, columns, texts[...], img)


def image_kernel(place, weight, texts, got, own, first, second, third, total):
    total[...] = dot(weight[...], texts[...]) + got[...].astype(F32)
    rows = own.shape[0]
    for k, out in enumerate((own, first, second, third)):
        slot = lax.rem(place[0] + (4 - k), 4)
        out[...] = total[pl.ds(pl.multiple_of(slot * rows, rows), rows), :].astype(out.dtype)


def text_kernel(weight_a, img_a, weight_b, img_b, out):
    half = out.shape[3]
    e = 2 * half
    turned = (((0,), (0,)), ((), ()))
    gt = lax.dot_general(weight_a[...], img_a[:, :e], turned, preferred_element_type=F32)
    gt += lax.dot_general(weight_b[...], img_b[:, :e], turned, preferred_element_type=F32)
    groups = out.shape[0] // 2
    for z in range(2):
        for g in range(groups):
            row = (z * groups + g) * CAP_DEV
            for h in range(2):
                out[2 * g + h, z] = gt[row : row + CAP_DEV, h * half : (h + 1) * half].astype(BF)


def call(kernel, args, outs, scalars=0, far=(), scratch=(), cost=SMALL):
    in_specs = [
        pl.BlockSpec(
            memory_space=pltpu.SMEM if i < scalars else pltpu.HBM if i in far else pltpu.VMEM
        )
        for i in range(len(args))
    ]
    return pl.pallas_call(
        kernel,
        in_specs=in_specs,
        out_specs=[pl.BlockSpec(memory_space=pltpu.VMEM) for _ in outs],
        out_shape=[jax.ShapeDtypeStruct(shape, dtype) for shape, dtype in outs],
        scratch_shapes=list(scratch),
        compiler_params=pltpu.CompilerParams(vmem_limit_bytes=54 << 20),
        cost_estimate=cost,
    )(*args)


def on_device(
    tokens, norm_gain, fc_in, fc_out, projection, slots, images, labels, logit_scale, logit_bias
):
    zh, core, xh = (lax.axis_index(a) for a in ("zh", "core", "xh"))
    low = xh == 0

    other = lax.ppermute(tokens, MP, SWAP)

    imgs = images.astype(F32)
    img = (imgs * lax.rsqrt(jnp.sum(imgs * imgs, axis=1, keepdims=True) + 1e-06)).astype(BF)
    code = jnp.stack([labels // 64, labels % 64], axis=1).astype(F32).astype(BF)
    img = jnp.concatenate([img, jnp.pad(code, ((0, 0), (0, PAD - 2)))], axis=1)
    img_mine = lax.all_to_all(
        jnp.broadcast_to(img[None], (4,) + img.shape), "zh", split_axis=0, concat_axis=0, tiled=True
    ).reshape(4 * IMG_ROWS, -1)

    members = slots[0][None, :] == jnp.arange(CAP_DEV, dtype=jnp.int32)[:, None]
    counts = jnp.sum(members.astype(F32), axis=1)
    flag = low.astype(jnp.int32).reshape(1)
    partial_out, states = call(
        functools.partial(mlp_kernel, ROW_TILE, FF_TILE),
        (flag, slots, tokens, other, norm_gain[None, :], fc_in, fc_out),
        [((CAP_DEV, fc_out.shape[1]), F32), ((CAP_DEV, fc_in.shape[0]), F32)],
        1,
        (5, 6),
        (
            pltpu.VMEM(fc_in.shape, BF),
            pltpu.VMEM(fc_out.shape, BF),
            pltpu.SemaphoreType.DMA((fc_in.shape[1] // FF_TILE + 1,)),
        ),
        LARGE,
    )
    summed = partial_out + lax.ppermute(partial_out, MP, SWAP)
    pooled = ((states + summed) / counts[:, None]).astype(BF)
    emb = dot(pooled, projection)

    group = ("zl", "y", "xl", "xh")
    sent = jnp.broadcast_to(emb.astype(BF)[None], (32,) + emb.shape)
    embs = lax.all_to_all(sent, group, split_axis=0, concat_axis=0, tiled=True)
    embs = embs.reshape((16, 2) + emb.shape)
    img_sent, _ = lax.optimization_barrier((img_mine, emb))
    img_other = lax.ppermute(img_sent, "core", SWAP)

    zl_i, y_i, xl_i, cap_i = (
        lax.broadcasted_iota(jnp.int32, (2, 4, 2, CAP_DEV), d) for d in range(4)
    )
    columns = (((((zh * 2 + zl_i) * 2 + xl_i) * 4 + y_i) * 2 + core) * CAP_DEV + cap_i).reshape(1, -1)
    scal = jnp.concatenate([logit_scale, logit_bias])
    n, e = 16 * CAP_DEV, fc_in.shape[0]
    images_half = img_mine.shape[0]
    texts, weight_other, gi_send = call(
        first_kernel,
        (scal, columns, embs, img_other),
        [((n, e), BF), ((images_half, n), BF), ((images_half, e), BF)],
        1,
    )
    gi_got = lax.ppermute(gi_send, "core", SWAP)
    (weight_mine,) = call(
        second_kernel, (scal, columns, texts, img_mine), [((images_half, n), BF)], 1
    )

    gi_got, weight_mine = lax.optimization_barrier((gi_got, weight_mine))
    grad_image, *rest = call(
        image_kernel,
        (zh.astype(jnp.int32).reshape(1), weight_mine, texts, gi_got),
        [((IMG_ROWS, e), F32)] + [((IMG_ROWS, e), BF)] * 3,
        1,
        scratch=(pltpu.VMEM((images_half, e), F32),),
    )
    for k, part in enumerate(rest):
        grad_image += lax.ppermute(part, "zh", shift(4, -k - 1)).astype(F32)

    weight_mine, _ = lax.optimization_barrier((weight_mine, rest[0]))
    (gt,) = call(
        text_kernel,
        (weight_other, img_other, weight_mine, img_mine),
        [((16, 2, CAP_DEV, e // 2), BF)],
    )
    got = lax.all_to_all(gt, ("y", "xl", "xh"), split_axis=0, concat_axis=0, tiled=True)
    gathered = jnp.sum(got.astype(F32), axis=0)
    front = lax.axis_index("zl") == 0
    keep = jnp.where(front, gathered[0], gathered[1])
    give = jnp.where(front, gathered[1], gathered[0])
    grad_text = keep + lax.ppermute(give, "zl", SWAP)

    own_emb = lax.dynamic_index_in_dim(
        embs, (lax.axis_index("zl") * 4 + lax.axis_index("y")) * 2 + lax.axis_index("xl"), 0, False
    ).astype(F32)
    squares = jnp.sum(own_emb * own_emb, axis=(0, 2))
    text_part = (emb * lax.rsqrt(squares + 1e-06)[:, None]).astype(BF)
    return (text_part, grad_image, grad_text)


def solution(mesh):
    fine = Mesh(mesh.devices.reshape(SIZES), AXES)
    every = DP + (MP,)
    placed = (
        P(DP, MP),
        P(),
        P(None, MP),
        P(MP, None),
        P(None, MP),
        P(DP, None),
        P(every, None),
        P(every),
        P(),
        P(),
    )
    return jax.shard_map(
        on_device,
        mesh=fine,
        in_specs=placed,
        out_specs=(P(DP, MP), P(every, None), P(DP, MP)),
        check_vma=False,
    )
```

time: 1060 us -> 129 us (0.12)
  waiting for transfers between devices: 986 us -> 41.8 us
  starting transfers between devices: 0.38 us -> 43.9 us
  matrix products: 39.2 us -> 1.3 us
  Pallas kernels: 0 us -> 27 us
  between operations: 15.2 us -> 2.06 us
    reduce_scatter x2 -> x0, waiting for transfers between devices: 600 us -> none  [the longest x1 584 us: on_device(): lax.psum_scatter(jnp.einsum('ij,ie->je', weight_all, img, preferred_eleme...]
    all_gather x2 -> x0, waiting for transfers between devices: 265 us -> none  [the longest x1 220 us: on_device(): all_texts = lax.all_gather(text_full, 'dp', axis=0, tiled=True)]
    psum x1 -> x0, waiting for transfers between devices: 120 us -> none  [on_device(): summed = lax.psum(partial_out, 'mp')]
    dot_general x6 -> x1, matrix products: 39.2 us -> 1.3 us  [dot(): return jnp.dot(a, b, preferred_element_type=F32)]
    ppermute x0 -> x8, waiting for transfers between devices: none -> 27.5 us  [the longest x3 13.3 us: on_device(): grad_image += lax.ppermute(part, 'zh', shift(4, -k - 1)).astype(F32)]
    pallas_call x0 -> x5, Pallas kernels: none -> 27 us  [call(): pl.pallas_call(kernel, in_specs=in_specs, out_specs=[pl.BlockSpec(memory_...]
    ppermute x0 -> x8, starting transfers between devices: none -> 23.5 us  [the longest x3 8.34 us: on_device(): grad_image += lax.ppermute(part, 'zh', shift(4, -k - 1)).astype(F32)]
    all_to_all x0 -> x3, starting transfers between devices: none -> 20.4 us  [the longest x1 8.48 us: on_device(): embs = lax.all_to_all(sent, group, split_axis=0, concat_axis=0, tiled=True)]
  transfers between devices with their start and end apart: 5 -> 11, of which waited for: 5 -> 7; matrix products, arithmetic and copies ran while one was open for 1% -> 8% of each run, Pallas kernels for 0% -> 12%
where the time goes in v2:
time: 129 us; the launch traced here: 128 us
  starting transfers between devices  43.9 us (34%)
  waiting for transfers between devices  41.8 us (32%)
  Pallas kernels  27 us (21%)
  other arithmetic  7.12 us (6%)
  local copies, waits for them, and re-layouts  5.1 us (4%)
  between operations  2.06 us (2%)
  matrix products  1.3 us (1%)
    pallas_call x5, Pallas kernels, call(): pl.pallas_call(kernel, in_specs=in_specs, out_specs=[pl.BlockSpec(memory_...  27 us
    ppermute x3, waiting for transfers between devices, on_device(): grad_image += lax.ppermute(part, 'zh', shift(4, -k - 1)).astype(F32)  13.3 us
    ppermute x1, waiting for transfers between devices, on_device(): other = lax.ppermute(tokens, MP, SWAP)  9.83 us
    all_to_all x1, starting transfers between devices, on_device(): embs = lax.all_to_all(sent, group, split_axis=0, concat_axis=0, tiled=True)  8.48 us
    all_to_all x1, waiting for transfers between devices, on_device(): embs = lax.all_to_all(sent, group, split_axis=0, concat_axis=0, tiled=True)  8.42 us
    ppermute x3, starting transfers between devices, on_device(): grad_image += lax.ppermute(part, 'zh', shift(4, -k - 1)).astype(F32)  8.34 us
    all_to_all x1, starting transfers between devices, on_device(): lax.all_to_all(jnp.broadcast_to(img[None], (4,) + img.shape), 'zh', split...  8.18 us
    all_to_all x1, waiting for transfers between devices, on_device(): lax.all_to_all(gt, ('y', 'xl', 'xh'), split_axis=0, concat_axis=0, tiled=...  5.85 us
  transfers between devices with their start and end apart: 11, of which 7 were waited for; matrix products, arithmetic and copies ran while one was open for 8% of the time, Pallas kernels for 12%

profile of v2, /device:TPU:1, one launch (start us, length us, event | category | flops | bytes accessed | tf_op | source)
XLA Modules:
  0.0 128.3 jit_solution(3083170113601217004)
XLA Ops:
  0.6 0.0 copy-start
  0.6 3.7 %collective-permute-start = (bf16[1024,512]{1,0:T(8,128)(2,1)}, bf16[1024,512]{1,0:T(8,128)(2,1)S(1)}, u32[]{:S(2)}, u32[]{:S(2)}) collective-permute-start(bf16[1024,512]{1,0:T(8,128)(2,1)} %own.1), channel_id=1, source_target_pairs={{0,1},{1,0},{2,3},{3,2},{4,5},{5,4},{6,7},{7,6},{8,9},{9,8},{10,11... | collective-permute-start | bytes 3145736 | tf_op jit(solution)/shard_map/ppermute | solution.py:175
  4.3 1.1 fusion.1
  5.4 0.7 fusion.8
  6.1 0.1 copy.15
  6.2 1.1 fusion.2
  7.3 1.1 broadcast_in_dim.8
  8.4 8.2 %all-to-all-start.1 = ((bf16[4,128,1152]{2,1,0:T(8,128)(2,1)}), bf16[4,128,1152]{2,1,0:T(8,128)(2,1)S(1)}, u32[]{:S(2)}, u32[]{:S(2)}) async-start(bf16[4,128,1152]{2,1,0:T(8,128)(2,1)} %broadcast_in_dim.8), calls=%async_computation.1 | async-start | bytes 2359296 | tf_op jit(solution)/shard_map/all_to_all | solution.py:181
  16.6 9.8 %collective-permute-done.other = bf16[1024,512]{1,0:T(8,128)(2,1)S(1)} collective-permute-done((bf16[1024,512]{1,0:T(8,128)(2,1)}, bf16[1024,512]{1,0:T(8,128)(2,1)S(1)}, u32[]{:S(2)}, u32[]{:S(2)}) %collective-permute-start) | collective-permute-done | bytes 1048608 | tf_op jit(solution)/shard_map/ppermute | solution.py:175
  26.5 1.0 copy-done.6
  27.4 11.5 %shard_map.121 = (f32[32,1024]{1,0:T(8,128)}, f32[32,1024]{1,0:T(8,128)}) custom-call(s32[1]{0:T(128)} %bitcast.low, s32[1,1024]{1,0:T(1,128)} %slot.1, bf16[1024,512]{1,0:T(8,128)(2,1)} %own.1, bf16[1024,512]{1,0:T(8,128)(2,1)} %copy-done.6, f32[1,1024]{1,0:T(1,128)} %bitcast.19, bf16[1024,2048]{1,0:T(8,128)(2,1)} %fc_in.1, bf16[2048,1024]{1,0:T(8,128)(2,1)} %fc_out.1), custom_call_target="tpu_custom_call" | custom-call | flops 10000000000 | bytes 1000 | tf_op jit(solution)/shard_map/pallas_call | solution.py:158
  38.9 3.7 %collective-permute-start.1 = (f32[32,1024]{1,0:T(8,128)}, f32[32,1024]{1,0:T(8,128)S(1)}, u32[]{:S(2)}, u32[]{:S(2)}) collective-permute-start(f32[32,1024]{1,0:T(8,128)} %get-tuple-element.17), channel_id=1, source_target_pairs={{0,1},{1,0},{2,3},{3,2},{4,5},{5,4},{6,7},{7,6},{8,9},{9,8},{10,11... | collective-permute-start | bytes 393224 | tf_op jit(solution)/shard_map/ppermute | solution.py:201
  42.6 0.0 copy-done.5
  42.6 0.1 convert_reduce_fusion.1
  42.8 2.7 %collective-permute-done.1 = f32[32,1024]{1,0:T(8,128)S(1)} collective-permute-done((f32[32,1024]{1,0:T(8,128)}, f32[32,1024]{1,0:T(8,128)S(1)}, u32[]{:S(2)}, u32[]{:S(2)}) %collective-permute-start.1) | collective-permute-done | bytes 131104 | tf_op jit(solution)/shard_map/ppermute | solution.py:201
  45.5 1.3 %fusion.9 = (bf16[32,512]{1,0:T(8,128)(2,1)S(1)}, f32[32,512]{1,0:T(8,128)S(1)}) fusion(bf16[1024,512]{1,0:T(8,128)(2,1)S(1)} %copy-done, f32[32,1024]{1,0:T(8,128)} %get-tuple-element.16, f32[32,1024]{1,0:T(8,128)} %get-tuple-element.17, f32[32,1024]{1,0:T(8,128)S(1)} %collective-permute-done.1, f32[32]{0:T(128)S(1)} %convert_reduce_fusion.1), kind=kOutput, calls=%fused_computation.32 | convolution fusion | flops 33701888 | bytes 1540224 | tf_op jit(solution)/shard_map/dot_general | solution.py:28
  46.8 0.0 all-to-all-done.1
  46.8 1.2 broadcast_in_dim.7
  48.0 8.5 %all-to-all-start = ((bf16[32,32,512]{2,1,0:T(8,128)(2,1)}), bf16[32,32,512]{2,1,0:T(8,128)(2,1)}, u32[]{:S(2)}, u32[]{:S(2)}) async-start(bf16[32,32,512]{2,1,0:T(8,128)(2,1)} %broadcast_in_dim.7), calls=%async_computation | async-start | bytes 2097152 | tf_op jit(solution)/shard_map/all_to_all | solution.py:207
  56.5 3.0 %collective-permute-start.2 = (bf16[512,1152]{1,0:T(8,128)(2,1)S(1)}, bf16[512,1152]{1,0:T(8,128)(2,1)S(1)}, u32[]{:S(2)}, u32[]{:S(2)}) collective-permute-start(bf16[512,1152]{1,0:T(8,128)(2,1)S(1)} %bitcast.15), channel_id=1, source_target_pairs={{0,2},{2,0},{1,3},{3,1},{4,6},{6,4},{5,7},{7,5},{8,10},{10,8},{9,1... | collective-permute-start | bytes 3538952 | tf_op jit(solution)/shard_map/ppermute | solution.py:210
  60.8 0.1 multiply_add_fusion
  60.9 0.7 reshape.119.columns
  61.6 0.6 pad_maximum_fusion.scal
  62.2 0.0 collective-permute-done.2.img.img_a
  62.2 8.4 %all-to-all-done = bf16[32,32,512]{2,1,0:T(8,128)(2,1)} async-done(((bf16[32,32,512]{2,1,0:T(8,128)(2,1)}), bf16[32,32,512]{2,1,0:T(8,128)(2,1)}, u32[]{:S(2)}, u32[]{:S(2)}) %all-to-all-start) | async-done | bytes 1048608 | tf_op jit(solution)/shard_map/all_to_all | solution.py:207
  70.6 4.3 %shard_map.122 = (bf16[512,1024]{1,0:T(8,128)(2,1)}, bf16[512,512]{1,0:T(8,128)(2,1)}, bf16[512,1024]{1,0:T(8,128)(2,1)}) custom-call(f32[2]{0:T(128)} %pad_maximum_fusion.scal, s32[1,512]{1,0:T(1,128)} %reshape.119.columns, bf16[16,2,32,512]{3,2,1,0:T(8,128)(2,1)} %bitcast.3.emb, bf16[512,1152]{1,0:T(8,128)(2,1)} %copy-done.2), custom_call_target="tpu_custom_call" | custom-call | flops 1000 | bytes 1000 | tf_op jit(solution)/shard_map/pallas_call | solution.py:158
  74.9 4.4 %collective-permute-start.3 = (bf16[512,1024]{1,0:T(8,128)(2,1)}, bf16[512,1024]{1,0:T(8,128)(2,1)S(1)}, u32[]{:S(2)}, u32[]{:S(2)}) collective-permute-start(bf16[512,1024]{1,0:T(8,128)(2,1)} %get-tuple-element.19), channel_id=1, source_target_pairs={{0,2},{2,0},{1,3},{3,1},{4,6},{6,4},{5,7},{7,5},{8,10},{10,8},{9,1... | collective-permute-start | bytes 3145736 | tf_op jit(solution)/shard_map/ppermute | solution.py:225
  79.3 3.3 %shard_map.123.weight.weight_b = bf16[512,512]{1,0:T(8,128)(2,1)} custom-call(f32[2]{0:T(128)} %pad_maximum_fusion.scal, s32[1,512]{1,0:T(1,128)} %reshape.119.columns, bf16[512,1024]{1,0:T(8,128)(2,1)} %get-tuple-element.20.texts, bf16[512,1152]{1,0:T(8,128)(2,1)} %bitcast.16), custom_call_target="tpu_custom_call" | custom-call | flops 1000 | bytes 1000 | tf_op jit(solution)/shard_map/pallas_call | solution.py:158
  82.7 0.0 collective-permute-done.3.got
  82.7 1.0 copy-done.3
  83.7 3.7 %shard_map.124 = (f32[128,1024]{1,0:T(8,128)}, bf16[128,1024]{1,0:T(8,128)(2,1)}, bf16[128,1024]{1,0:T(8,128)(2,1)}, bf16[128,1024]{1,0:T(8,128)(2,1)}) custom-call(s32[1]{0:T(128)} %bitcast.4.place, bf16[512,512]{1,0:T(8,128)(2,1)} %shard_map.123.weight.weight_b, bf16[512,1024]{1,0:T(8,128)(2,1)} %get-tuple-element.20.texts, bf16[512,1024]{1,0:T(8,128)(2,1)} %copy-done.3), custom_call_target="tpu_custom_call" | custom-call | flops 1000 | bytes 1000 | tf_op jit(solution)/shard_map/pallas_call | solution.py:158
  87.4 4.2 %shard_map.125 = bf16[16,2,32,512]{3,2,1,0:T(8,128)(2,1)} custom-call(bf16[512,512]{1,0:T(8,128)(2,1)} %get-tuple-element.27.weight_a, bf16[512,1152]{1,0:T(8,128)(2,1)} %copy-done.2, bf16[512,512]{1,0:T(8,128)(2,1)} %shard_map.123.weight.weight_b, bf16[512,1152]{1,0:T(8,128)(2,1)} %bitcast.17), custom_call_target="tpu_custom_call" | custom-call | flops 1000 | bytes 1000 | tf_op jit(solution)/shard_map/pallas_call | solution.py:158
  91.6 3.8 %all-to-all-start.2 = ((bf16[16,2,32,512]{3,2,1,0:T(8,128)(2,1)}), bf16[16,2,32,512]{3,2,1,0:T(8,128)(2,1)S(1)}, u32[]{:S(2)}, u32[]{:S(2)}) async-start(bf16[16,2,32,512]{3,2,1,0:T(8,128)(2,1)} %shard_map.125), calls=%async_computation.2 | async-start | bytes 2097152 | tf_op jit(solution)/shard_map/all_to_all | solution.py:247
  95.4 1.0 multiply_reduce_fusion
  96.4 0.7 multiply_convert_fusion
  97.1 5.1 %collective-permute-start.4 = (bf16[128,1024]{1,0:T(8,128)(2,1)}, bf16[128,1024]{1,0:T(8,128)(2,1)S(1)}, u32[]{:S(2)}, u32[]{:S(2)}) collective-permute-start(bf16[128,1024]{1,0:T(8,128)(2,1)} %get-tuple-element.24), channel_id=1, source_target_pairs={{0,192},{64,0},{128,64},{192,128},{1,193},{65,1},{129,65},{193,129... | collective-permute-start | bytes 786440 | tf_op jit(solution)/shard_map/ppermute | solution.py:239
  102.1 1.2 collective-permute-start.5
  103.3 2.1 %collective-permute-start.6 = (bf16[128,1024]{1,0:T(8,128)(2,1)}, bf16[128,1024]{1,0:T(8,128)(2,1)S(1)}, u32[]{:S(2)}, u32[]{:S(2)}) collective-permute-start(bf16[128,1024]{1,0:T(8,128)(2,1)} %get-tuple-element.26), channel_id=1, source_target_pairs={{0,64},{64,128},{128,192},{192,0},{1,65},{65,129},{129,193},{193,1... | collective-permute-start | bytes 786440 | tf_op jit(solution)/shard_map/ppermute | solution.py:239
  105.4 5.9 %all-to-all-done.2 = bf16[16,2,32,512]{3,2,1,0:T(8,128)(2,1)S(1)} async-done(((bf16[16,2,32,512]{3,2,1,0:T(8,128)(2,1)}), bf16[16,2,32,512]{3,2,1,0:T(8,128)(2,1)S(1)}, u32[]{:S(2)}, u32[]{:S(2)}) %all-to-all-start.2) | async-done | bytes 1048608 | tf_op jit(solution)/shard_map/all_to_all | solution.py:247
  111.2 0.1 convert_reduce_fusion
  111.4 0.4 collective-permute-start.7
  111.8 9.3 %collective-permute-done.5 = bf16[128,1024]{1,0:T(8,128)(2,1)S(1)} collective-permute-done((bf16[128,1024]{1,0:T(8,128)(2,1)}, bf16[128,1024]{1,0:T(8,128)(2,1)S(1)}, u32[]{:S(2)}, u32[]{:S(2)}) %collective-permute-start.5) | collective-permute-done | bytes 262176 | tf_op jit(solution)/shard_map/ppermute | solution.py:239
  121.1 4.0 %collective-permute-done.6 = bf16[128,1024]{1,0:T(8,128)(2,1)S(1)} collective-permute-done((bf16[128,1024]{1,0:T(8,128)(2,1)}, bf16[128,1024]{1,0:T(8,128)(2,1)S(1)}, u32[]{:S(2)}, u32[]{:S(2)}) %collective-permute-start.6) | collective-permute-done | bytes 262176 | tf_op jit(solution)/shard_map/ppermute | solution.py:239
  125.0 0.0 collective-permute-done.4
  125.0 0.0 copy-done.4
  125.0 0.9 convert_add_fusion
  126.0 1.7 %collective-permute-done.7 = f32[32,512]{1,0:T(8,128)S(1)} collective-permute-done((f32[32,512]{1,0:T(8,128)S(1)}, f32[32,512]{1,0:T(8,128)S(1)}, u32[]{:S(2)}, u32[]{:S(2)}) %collective-permute-start.7) | collective-permute-done | bytes 65568 | tf_op jit(solution)/shard_map/ppermute | solution.py:252
  127.7 0.6 bitcast_add_fusion
  (15 shorter events, 0.1 us)
Async XLA Ops:
  0.6 44.9 %copy-start = (bf16[1024,512]{1,0:T(8,128)(2,1)S(1)}, bf16[1024,512]{1,0:T(8,128)(2,1)}, u32[]{:S(2)}) copy-start(bf16[1024,512]{1,0:T(8,128)(2,1)} %param.14) | copy-start | bytes 3145732
  0.6 25.8 %collective-permute-start = (bf16[1024,512]{1,0:T(8,128)(2,1)}, bf16[1024,512]{1,0:T(8,128)(2,1)S(1)}, u32[]{:S(2)}, u32[]{:S(2)}) collective-permute-start(bf16[1024,512]{1,0:T(8,128)(2,1)} %own.1), channel_id=1, source_target_pairs={{0,1},{1,0},{2,3},{3,2},{4,5},{5,4},{6,7},{7,6},{8,9},{9,8},{10,11... | collective-permute-start | bytes 3145736 | tf_op jit(solution)/shard_map/ppermute | solution.py:175
  8.4 38.3 %all-to-all-start.1 = ((bf16[4,128,1152]{2,1,0:T(8,128)(2,1)}), bf16[4,128,1152]{2,1,0:T(8,128)(2,1)S(1)}, u32[]{:S(2)}, u32[]{:S(2)}) async-start(bf16[4,128,1152]{2,1,0:T(8,128)(2,1)} %broadcast_in_dim.8), calls=%async_computation.1 | async-start | bytes 2359296 | tf_op jit(solution)/shard_map/all_to_all | solution.py:181
  26.4 1.0 copy-start.6
  27.4 15.2 %copy-start.5 = (s32[1,1024]{1,0:T(1,128)S(1)}, s32[1,1024]{1,0:T(1,128)}, u32[]{:S(2)}) copy-start(s32[1,1024]{1,0:T(1,128)} %slot.1) | copy-start | bytes 12292
  38.9 6.5 %collective-permute-start.1 = (f32[32,1024]{1,0:T(8,128)}, f32[32,1024]{1,0:T(8,128)S(1)}, u32[]{:S(2)}, u32[]{:S(2)}) collective-permute-start(f32[32,1024]{1,0:T(8,128)} %get-tuple-element.17), channel_id=1, source_target_pairs={{0,1},{1,0},{2,3},{3,2},{4,5},{5,4},{6,7},{7,6},{8,9},{9,8},{10,11... | collective-permute-start | bytes 393224 | tf_op jit(solution)/shard_map/ppermute | solution.py:201
  46.8 28.1 %copy-start.1 = (bf16[4,128,1152]{2,1,0:T(8,128)(2,1)}, bf16[4,128,1152]{2,1,0:T(8,128)(2,1)S(1)}, u32[]{:S(2)}) copy-start(bf16[4,128,1152]{2,1,0:T(8,128)(2,1)S(1)} %all-to-all-done.1) | copy-start | bytes 3538948
  48.0 22.6 %all-to-all-start = ((bf16[32,32,512]{2,1,0:T(8,128)(2,1)}), bf16[32,32,512]{2,1,0:T(8,128)(2,1)}, u32[]{:S(2)}, u32[]{:S(2)}) async-start(bf16[32,32,512]{2,1,0:T(8,128)(2,1)} %broadcast_in_dim.7), calls=%async_computation | async-start | bytes 2097152 | tf_op jit(solution)/shard_map/all_to_all | solution.py:207
  56.5 5.7 %collective-permute-start.2 = (bf16[512,1152]{1,0:T(8,128)(2,1)S(1)}, bf16[512,1152]{1,0:T(8,128)(2,1)S(1)}, u32[]{:S(2)}, u32[]{:S(2)}) collective-permute-start(bf16[512,1152]{1,0:T(8,128)(2,1)S(1)} %bitcast.15), channel_id=1, source_target_pairs={{0,2},{2,0},{1,3},{3,1},{4,6},{6,4},{5,7},{7,5},{8,10},{10,8},{9,1... | collective-permute-start | bytes 3538952 | tf_op jit(solution)/shard_map/ppermute | solution.py:210
  62.2 8.4 %copy-start.2 = (bf16[512,1152]{1,0:T(8,128)(2,1)}, bf16[512,1152]{1,0:T(8,128)(2,1)S(1)}, u32[]{:S(2)}) copy-start(bf16[512,1152]{1,0:T(8,128)(2,1)S(1)} %collective-permute-done.2.img.img_a) | copy-start | bytes 3538948
  74.9 7.7 %collective-permute-start.3 = (bf16[512,1024]{1,0:T(8,128)(2,1)}, bf16[512,1024]{1,0:T(8,128)(2,1)S(1)}, u32[]{:S(2)}, u32[]{:S(2)}) collective-permute-start(bf16[512,1024]{1,0:T(8,128)(2,1)} %get-tuple-element.19), channel_id=1, source_target_pairs={{0,2},{2,0},{1,3},{3,1},{4,6},{6,4},{5,7},{7,5},{8,10},{10,8},{9,1... | collective-permute-start | bytes 3145736 | tf_op jit(solution)/shard_map/ppermute | solution.py:225
  82.7 1.0 copy-start.3
  91.6 33.5 %copy-start.4 = (f32[128,1024]{1,0:T(8,128)S(1)}, f32[128,1024]{1,0:T(8,128)}, u32[]{:S(2)}) copy-start(f32[128,1024]{1,0:T(8,128)} %get-tuple-element.23) | copy-start | bytes 1572868
  91.6 19.7 %all-to-all-start.2 = ((bf16[16,2,32,512]{3,2,1,0:T(8,128)(2,1)}), bf16[16,2,32,512]{3,2,1,0:T(8,128)(2,1)S(1)}, u32[]{:S(2)}, u32[]{:S(2)}) async-start(bf16[16,2,32,512]{3,2,1,0:T(8,128)(2,1)} %shard_map.125), calls=%async_computation.2 | async-start | bytes 2097152 | tf_op jit(solution)/shard_map/all_to_all | solution.py:247
  97.1 28.0 %collective-permute-start.4 = (bf16[128,1024]{1,0:T(8,128)(2,1)}, bf16[128,1024]{1,0:T(8,128)(2,1)S(1)}, u32[]{:S(2)}, u32[]{:S(2)}) collective-permute-start(bf16[128,1024]{1,0:T(8,128)(2,1)} %get-tuple-element.24), channel_id=1, source_target_pairs={{0,192},{64,0},{128,64},{192,128},{1,193},{65,1},{129,65},{193,129... | collective-permute-start | bytes 786440 | tf_op jit(solution)/shard_map/ppermute | solution.py:239
  102.1 18.9 %collective-permute-start.5 = (bf16[128,1024]{1,0:T(8,128)(2,1)}, bf16[128,1024]{1,0:T(8,128)(2,1)S(1)}, u32[]{:S(2)}, u32[]{:S(2)}) collective-permute-start(bf16[128,1024]{1,0:T(8,128)(2,1)} %get-tuple-element.25), channel_id=1, source_target_pairs={{0,128},{64,192},{128,0},{192,64},{1,129},{65,193},{129,1},{193,65... | collective-permute-start | bytes 786440 | tf_op jit(solution)/shard_map/ppermute | solution.py:239
  103.3 21.7 %collective-permute-start.6 = (bf16[128,1024]{1,0:T(8,128)(2,1)}, bf16[128,1024]{1,0:T(8,128)(2,1)S(1)}, u32[]{:S(2)}, u32[]{:S(2)}) collective-permute-start(bf16[128,1024]{1,0:T(8,128)(2,1)} %get-tuple-element.26), channel_id=1, source_target_pairs={{0,64},{64,128},{128,192},{192,0},{1,65},{65,129},{129,193},{193,1... | collective-permute-start | bytes 786440 | tf_op jit(solution)/shard_map/ppermute | solution.py:239
  111.4 16.3 %collective-permute-start.7 = (f32[32,512]{1,0:T(8,128)S(1)}, f32[32,512]{1,0:T(8,128)S(1)}, u32[]{:S(2)}, u32[]{:S(2)}) collective-permute-start(f32[32,512]{1,0:T(8,128)S(1)} %select_bitcast_fusion), channel_id=1, source_target_pairs={{0,32},{32,0},{1,33},{33,1},{2,34},{34,2},{3,35},{35,3},{4,36},{36... | collective-permute-start | bytes 196616 | tf_op jit(solution)/shard_map/ppermute | solution.py:252

commit v3 on v2

--- a/solution.py
+++ b/solution.py
@@ -32,23 +32,51 @@
     return [(i, (i + k) % n) for i in range(n)]
 
 
-def mlp_kernel(row_tile, ff_tile, low, slot, own, other, gain, fc_in, fc_out, out, st_out, w_in, w_out, sems):
+def head_kernel(mine, got, states, counts, projection, emb, sent, block, sems):
+    pooled = ((states[...] + (mine[...] + got[...])) / counts[...]).astype(BF)
+    result = dot(pooled, projection[...])
+    block[...] = jnp.broadcast_to(result.astype(BF)[None], block.shape)
+    n = block.shape[0]
+    stores = [
+        pltpu.make_async_copy(block, sent.at[pl.ds(i * n, n)], sems.at[i])
+        for i in range(sent.shape[0] // n)
+    ]
+    for store in stores:
+        store.start()
+    emb[...] = result
+    for store in stores:
+        store.wait()
+
+
+def mlp_kernel(
+    row_tile, ff_tile, low, slot, tokens, arrived, gain, fc_in, fc_out, out, st_out,
+    own, other, w_in, w_out, sems
+):
     rows, half = own.shape
     ff = w_in.shape[1]
-    tiles = [pl.ds(j * ff_tile, ff_tile) for j in range(ff // ff_tile)]
+    blocks = [slice(r, r + row_tile) for r in range(0, rows, row_tile)]
+    tiles = [slice(j, j + ff_tile) for j in range(0, ff, ff_tile)]
+    pairs = []
+    for block in blocks:
+        pairs.append([(tokens.at[block, :], own.at[block, :])])
+        pairs[-1].append((arrived.at[block, :], other.at[block, :]))
+    for j, tile in enumerate(tiles):
+        pairs.insert(2 * j + 1, [(fc_in.at[:, tile], w_in.at[:, tile])])
+    pairs.append([(fc_out, w_out)])
     loads = [
-        pltpu.make_async_copy(fc_in.at[:, t], w_in.at[:, t], sems.at[j])
-        for j, t in enumerate(tiles)
+        [pltpu.make_async_copy(a, b, sems.at[i, k]) for k, (a, b) in enumerate(pair)]
+        for i, pair in enumerate(pairs)
     ]
-    loads.append(pltpu.make_async_copy(fc_out, w_out, sems.at[len(tiles)]))
-    for load in loads:
-        load.start()
+    for group in loads:
+        for load in group:
+            load.start()
     size = 1.0 / (2 * half)
     is_low = low[0] == 1
     pooled = [jnp.zeros((CAP_DEV, ff_tile), F32) for _ in range(ff // ff_tile)]
     states = [jnp.zeros((CAP_DEV, half), F32) for _ in range(2)]
-    for r in range(0, rows, row_tile):
-        block = slice(r, r + row_tile)
+    for i, block in enumerate(blocks):
+        for load in loads[2 * i]:
+            load.wait()
         captions = lax.broadcasted_iota(jnp.int32, (CAP_DEV, row_tile), 0)
         members = (captions == slot[:, block]).astype(F32).astype(BF)
         mine = own[block, :]
@@ -74,8 +102,8 @@
             axis=1,
         )
         for j in range(ff // ff_tile):
-            if r == 0:
-                loads[j].wait()
+            if i == 0:
+                loads[2 * j + 1][0].wait()
             pre = dot(normed, w_in[:, j * ff_tile : (j + 1) * ff_tile])
             pre_half = 0.5 * pre
             bend = jnp.tanh(pre * (GELU_A + GELU_B * (pre * pre)))
@@ -83,7 +111,7 @@
             pooled[j] += dot(members, hidden)
     st_out[:, :half] = states[0]
     st_out[:, half:] = states[1]
-    loads[-1].wait()
+    loads[-1][0].wait()
     terms = jnp.zeros((2 * CAP_DEV, w_out.shape[1]), F32)
     for j in range(ff // ff_tile):
         coarse = pooled[j].astype(BF)
@@ -107,7 +135,7 @@
     return (-scale * sign * jax.nn.sigmoid(-sign * logit)).astype(BF)
 
 
-def first_kernel(scal, columns, emb, img, texts, weight, gi):
+def first_kernel(scal, place, columns, emb, exact, img, own_text, texts, weight, gi):
     half = emb.shape[3]
     for g in range(emb.shape[0]):
         lo = emb[g, 0].astype(F32)
@@ -117,6 +145,10 @@
         rows = slice(g * CAP_DEV, (g + 1) * CAP_DEV)
         texts[rows, :half] = (lo * inverse).astype(BF)
         texts[rows, half:] = (hi * inverse).astype(BF)
+    lo = emb[place[0], 0].astype(F32)
+    hi = emb[place[0], 1].astype(F32)
+    squares = jnp.sum(lo * lo, axis=1, keepdims=True) + jnp.sum(hi * hi, axis=1, keepdims=True)
+    own_text[...] = (exact[...] * lax.rsqrt(squares + 1e-06)).astype(BF)
     w = weights_of(scal, columns, texts[...], img)
     weight[...] = w
     gi[...] = dot(w, texts[...]).astype(BF)
@@ -148,20 +180,25 @@
                 out[2 * g + h, z] = gt[row : row + CAP_DEV, h * half : (h + 1) * half].astype(BF)
 
 
-def call(kernel, args, outs, scalars=0, far=(), scratch=(), cost=SMALL):
+def call(kernel, args, outs, scalars=0, far=(), free=(), far_out=(), scratch=(), cost=SMALL, limit=20):
     in_specs = [
         pl.BlockSpec(
-            memory_space=pltpu.SMEM if i < scalars else pltpu.HBM if i in far else pltpu.VMEM
+            memory_space=pltpu.SMEM
+            if i < scalars
+            else pltpu.HBM if i in far else pl.ANY if i in free else pltpu.VMEM
         )
         for i in range(len(args))
     ]
     return pl.pallas_call(
         kernel,
         in_specs=in_specs,
-        out_specs=[pl.BlockSpec(memory_space=pltpu.VMEM) for _ in outs],
+        out_specs=[
+            pl.BlockSpec(memory_space=pltpu.HBM if i in far_out else pltpu.VMEM)
+            for i in range(len(outs))
+        ],
         out_shape=[jax.ShapeDtypeStruct(shape, dtype) for shape, dtype in outs],
         scratch_shapes=list(scratch),
-        compiler_params=pltpu.CompilerParams(vmem_limit_bytes=54 << 20),
+        compiler_params=pltpu.CompilerParams(vmem_limit_bytes=limit << 20),
         cost_estimate=cost,
     )(*args)
 
@@ -190,20 +227,31 @@
         (flag, slots, tokens, other, norm_gain[None, :], fc_in, fc_out),
         [((CAP_DEV, fc_out.shape[1]), F32), ((CAP_DEV, fc_in.shape[0]), F32)],
         1,
-        (5, 6),
-        (
+        far=(2, 5, 6),
+        free=(3,),
+        scratch=(
+            pltpu.VMEM(tokens.shape, BF),
+            pltpu.VMEM(tokens.shape, BF),
             pltpu.VMEM(fc_in.shape, BF),
             pltpu.VMEM(fc_out.shape, BF),
-            pltpu.SemaphoreType.DMA((fc_in.shape[1] // FF_TILE + 1,)),
+            pltpu.SemaphoreType.DMA((5, 2)),
         ),
-        LARGE,
-    )
-    summed = partial_out + lax.ppermute(partial_out, MP, SWAP)
-    pooled = ((states + summed) / counts[:, None]).astype(BF)
-    emb = dot(pooled, projection)
+        cost=LARGE,
+        limit=48,
+    )
+    emb, sent = call(
+        head_kernel,
+        (partial_out, lax.ppermute(partial_out, MP, SWAP), states, counts[:, None], projection),
+        [((CAP_DEV, projection.shape[1]), F32), ((32, CAP_DEV, projection.shape[1]), BF)],
+        far_out=(1,),
+        limit=60,
+        scratch=(
+            pltpu.VMEM((8, CAP_DEV, projection.shape[1]), BF),
+            pltpu.SemaphoreType.DMA((4,)),
+        ),
+    )
 
     group = ("zl", "y", "xl", "xh")
-    sent = jnp.broadcast_to(emb.astype(BF)[None], (32,) + emb.shape)
     embs = lax.all_to_all(sent, group, split_axis=0, concat_axis=0, tiled=True)
     embs = embs.reshape((16, 2) + emb.shape)
     img_sent, _ = lax.optimization_barrier((img_mine, emb))
@@ -216,11 +264,13 @@
     scal = jnp.concatenate([logit_scale, logit_bias])
     n, e = 16 * CAP_DEV, fc_in.shape[0]
     images_half = img_mine.shape[0]
-    texts, weight_other, gi_send = call(
+    zl, y, xl = (lax.axis_index(a) for a in ("zl", "y", "xl"))
+    place = ((zl * 4 + y) * 2 + xl).astype(jnp.int32).reshape(1)
+    text_part, texts, weight_other, gi_send = call(
         first_kernel,
-        (scal, columns, embs, img_other),
-        [((n, e), BF), ((images_half, n), BF), ((images_half, e), BF)],
-        1,
+        (scal, place, columns, embs, emb, img_other),
+        [(emb.shape, BF), ((n, e), BF), ((images_half, n), BF), ((images_half, e), BF)],
+        2,
     )
     gi_got = lax.ppermute(gi_send, "core", SWAP)
     (weight_mine,) = call(
@@ -246,16 +296,11 @@
     )
     got = lax.all_to_all(gt, ("y", "xl", "xh"), split_axis=0, concat_axis=0, tiled=True)
     gathered = jnp.sum(got.astype(F32), axis=0)
-    front = lax.axis_index("zl") == 0
+    front = zl == 0
     keep = jnp.where(front, gathered[0], gathered[1])
     give = jnp.where(front, gathered[1], gathered[0])
     grad_text = keep + lax.ppermute(give, "zl", SWAP)
 
-    own_emb = lax.dynamic_index_in_dim(
-        embs, (lax.axis_index("zl") * 4 + lax.axis_index("y")) * 2 + lax.axis_index("xl"), 0, False
-    ).astype(F32)
-    squares = jnp.sum(own_emb * own_emb, axis=(0, 2))
-    text_part = (emb * lax.rsqrt(squares + 1e-06)[:, None]).astype(BF)
     return (text_part, grad_image, grad_text)
 
 

time: 129 us -> 119 us (0.922)
  Pallas kernels: 27 us -> 20.8 us
  other arithmetic: 7.12 us -> 4.87 us
  waiting for transfers between devices: 41.8 us -> 43.3 us
  matrix products: 1.3 us -> 0 us
    pallas_call x5 -> x6, Pallas kernels: 27 us -> 20.8 us  [call(): pl.pallas_call(kernel, in_specs=in_specs, out_specs=[pl.BlockSpec(memory_...]
    ppermute x3, waiting for transfers between devices: 13.3 us -> 11.4 us  [on_device(): grad_image += lax.ppermute(part, 'zh', shift(4, -k - 1)).astype(F32)]
    all_to_all x1, waiting for transfers between devices: 5.85 us -> 7.24 us  [on_device(): lax.all_to_all(gt, ('y', 'xl', 'xh'), split_axis=0, concat_axis=0, tiled=...]
    dot_general x1 -> x0, matrix products: 1.3 us -> none  [dot(): return jnp.dot(a, b, preferred_element_type=F32)]
  transfers between devices with their start and end apart: 11 -> 11, of which waited for: 7 -> 9; matrix products, arithmetic and copies ran while one was open for 8% -> 5% of each run, Pallas kernels for 12% -> 13%
where the time goes in v3:
time: 119 us; the launch traced here: 118 us
  waiting for transfers between devices  43.3 us (36%)
  starting transfers between devices  43.2 us (36%)
  Pallas kernels  20.8 us (17%)
  other arithmetic  4.87 us (4%)
  local copies, waits for them, and re-layouts  4.05 us (3%)
  between operations  2.09 us (2%)
    pallas_call x6, Pallas kernels, call(): pl.pallas_call(kernel, in_specs=in_specs, out_specs=[pl.BlockSpec(memory_...  20.8 us
    ppermute x3, waiting for transfers between devices, on_device(): grad_image += lax.ppermute(part, 'zh', shift(4, -k - 1)).astype(F32)  11.4 us
    ppermute x1, waiting for transfers between devices, on_device(): other = lax.ppermute(tokens, MP, SWAP)  9.79 us
    all_to_all x1, waiting for transfers between devices, on_device(): embs = lax.all_to_all(sent, group, split_axis=0, concat_axis=0, tiled=True)  9.25 us
    all_to_all x1, starting transfers between devices, on_device(): embs = lax.all_to_all(sent, group, split_axis=0, concat_axis=0, tiled=True)  8.6 us
    all_to_all x1, starting transfers between devices, on_device(): lax.all_to_all(jnp.broadcast_to(img[None], (4,) + img.shape), 'zh', split...  8.18 us
    ppermute x3, starting transfers between devices, on_device(): grad_image += lax.ppermute(part, 'zh', shift(4, -k - 1)).astype(F32)  8.16 us
    all_to_all x1, waiting for transfers between devices, on_device(): lax.all_to_all(gt, ('y', 'xl', 'xh'), split_axis=0, concat_axis=0, tiled=...  7.24 us
  transfers between devices with their start and end apart: 11, of which 9 were waited for; matrix products, arithmetic and copies ran while one was open for 5% of the time, Pallas kernels for 13%

profile of v3, /device:TPU:1, one launch (start us, length us, event | category | flops | bytes accessed | tf_op | source)
XLA Modules:
  0.0 118.3 jit_solution(2743915670698579101)
XLA Ops:
  0.6 3.7 %collective-permute-start = (bf16[1024,512]{1,0:T(8,128)(2,1)}, bf16[1024,512]{1,0:T(8,128)(2,1)S(1)}, u32[]{:S(2)}, u32[]{:S(2)}) collective-permute-start(bf16[1024,512]{1,0:T(8,128)(2,1)} %tokens.1), channel_id=1, source_target_pairs={{0,1},{1,0},{2,3},{3,2},{4,5},{5,4},{6,7},{7,6},{8,9},{9,8},{10,11... | collective-permute-start | bytes 3145736 | tf_op jit(solution)/shard_map/ppermute | solution.py:212
  4.3 1.1 fusion.1
  5.4 0.7 fusion.6
  6.1 1.1 fusion.2
  7.1 0.1 copy.17
  7.3 0.0 copy-start.4
  7.3 0.0 copy-start.7
  7.3 1.1 broadcast_in_dim.16
  8.5 8.2 %all-to-all-start.1 = ((bf16[4,128,1152]{2,1,0:T(8,128)(2,1)}), bf16[4,128,1152]{2,1,0:T(8,128)(2,1)S(1)}, u32[]{:S(2)}, u32[]{:S(2)}) async-start(bf16[4,128,1152]{2,1,0:T(8,128)(2,1)} %broadcast_in_dim.16), calls=%async_computation.1 | async-start | bytes 2359296 | tf_op jit(solution)/shard_map/all_to_all | solution.py:218
  16.6 9.8 %collective-permute-done.arrived = bf16[1024,512]{1,0:T(8,128)(2,1)S(1)} collective-permute-done((bf16[1024,512]{1,0:T(8,128)(2,1)}, bf16[1024,512]{1,0:T(8,128)(2,1)S(1)}, u32[]{:S(2)}, u32[]{:S(2)}) %collective-permute-start) | collective-permute-done | bytes 1048608 | tf_op jit(solution)/shard_map/ppermute | solution.py:212
  26.4 9.9 %shard_map.121 = (f32[32,1024]{1,0:T(8,128)S(1)}, f32[32,1024]{1,0:T(8,128)S(1)}) custom-call(s32[1]{0:T(128)} %bitcast.1.low, s32[1,1024]{1,0:T(1,128)S(1)} %copy-done.3, bf16[1024,512]{1,0:T(8,128)(2,1)S(1)} %copy-done.4, bf16[1024,512]{1,0:T(8,128)(2,1)S(1)} %collective-permute-done.arrived, f32[1,1024]{1,0:T(1,128)S(1)} %bitcast.21, ...), custom_call_target="tpu_custom_call" | custom-call | flops 10000000000 | bytes 1000 | tf_op jit(solution)/shard_map/pallas_call | solution.py:192
  36.4 0.6 copy-done.1
  37.0 3.6 %collective-permute-start.1 = (f32[32,1024]{1,0:T(8,128)S(1)}, f32[32,1024]{1,0:T(8,128)S(1)}, u32[]{:S(2)}, u32[]{:S(2)}) collective-permute-start(f32[32,1024]{1,0:T(8,128)S(1)} %get-tuple-element.19.mine), channel_id=1, source_target_pairs={{0,1},{1,0},{2,3},{3,2},{4,5},{5,4},{6,7},{7,6},{8,9},{9,8},{10,11... | collective-permute-start | bytes 393224 | tf_op jit(solution)/shard_map/ppermute | solution.py:244
  40.7 0.1 convert_reduce_fusion.1
  40.8 0.7 copy.15.counts
  41.5 1.8 %collective-permute-done.1.got = f32[32,1024]{1,0:T(8,128)S(1)} collective-permute-done((f32[32,1024]{1,0:T(8,128)S(1)}, f32[32,1024]{1,0:T(8,128)S(1)}, u32[]{:S(2)}, u32[]{:S(2)}) %collective-permute-start.1) | collective-permute-done | bytes 131104 | tf_op jit(solution)/shard_map/ppermute | solution.py:244
  43.3 0.6 copy-done.8
  44.0 3.4 %shard_map.122 = (f32[32,512]{1,0:T(8,128)}, bf16[32,32,512]{2,1,0:T(8,128)(2,1)}) custom-call(f32[32,1024]{1,0:T(8,128)} %copy-done, f32[32,1024]{1,0:T(8,128)} %copy-done.8, f32[32,1024]{1,0:T(8,128)} %copy-done.1, f32[32,1]{1,0:T(8,128)} %copy.15.counts, bf16[1024,512]{1,0:T(8,128)(2,1)} %projection.1), custom_call_target="tpu_custom_call" | custom-call | flops 1000 | bytes 1000 | tf_op jit(solution)/shard_map/pallas_call | solution.py:192
  47.4 0.0 copy-start.2
  47.4 0.0 all-to-all-done.1
  47.4 8.6 %all-to-all-start = ((bf16[32,32,512]{2,1,0:T(8,128)(2,1)}), bf16[32,32,512]{2,1,0:T(8,128)(2,1)S(1)}, u32[]{:S(2)}, u32[]{:S(2)}) async-start(bf16[32,32,512]{2,1,0:T(8,128)(2,1)} %get-tuple-element.21), calls=%async_computation | async-start | bytes 2097152 | tf_op jit(solution)/shard_map/all_to_all | solution.py:255
  56.0 2.8 %collective-permute-start.2 = (bf16[512,1152]{1,0:T(8,128)(2,1)S(1)}, bf16[512,1152]{1,0:T(8,128)(2,1)S(1)}, u32[]{:S(2)}, u32[]{:S(2)}) collective-permute-start(bf16[512,1152]{1,0:T(8,128)(2,1)S(1)} %bitcast.16), channel_id=1, source_target_pairs={{0,2},{2,0},{1,3},{3,1},{4,6},{6,4},{5,7},{7,5},{8,10},{10,8},{9,1... | collective-permute-start | bytes 3538952 | tf_op jit(solution)/shard_map/ppermute | solution.py:258
  60.1 0.1 multiply_add_fusion
  60.2 0.1 reshape.115.columns
  60.3 0.1 pad_maximum_fusion.scal
  60.3 0.9 collective-permute-done.2.img.img_a
  61.2 9.3 %all-to-all-done = bf16[32,32,512]{2,1,0:T(8,128)(2,1)S(1)} async-done(((bf16[32,32,512]{2,1,0:T(8,128)(2,1)}), bf16[32,32,512]{2,1,0:T(8,128)(2,1)S(1)}, u32[]{:S(2)}, u32[]{:S(2)}) %all-to-all-start) | async-done | bytes 1048608 | tf_op jit(solution)/shard_map/all_to_all | solution.py:255
  70.5 2.8 %shard_map.123 = (bf16[32,512]{1,0:T(8,128)(2,1)}, bf16[512,1024]{1,0:T(8,128)(2,1)S(1)}, bf16[512,512]{1,0:T(8,128)(2,1)S(1)}, bf16[512,1024]{1,0:T(8,128)(2,1)S(1)}) custom-call(f32[2]{0:T(128)S(1)} %pad_maximum_fusion.scal, s32[1]{0:T(128)} %bitcast.place, s32[1,512]{1,0:T(1,128)S(1)} %reshape.115.columns, bf16[16,2,32,512]{3,2,1,0:T(8,128)(2,1)S(1)} %bitcast.19, ...), custom_call_target="tpu_custom_call" | custom-call | flops 1000 | bytes 1000 | tf_op jit(solution)/shard_map/pallas_call | solution.py:192
  73.3 4.1 %collective-permute-start.3 = (bf16[512,1024]{1,0:T(8,128)(2,1)S(1)}, bf16[512,1024]{1,0:T(8,128)(2,1)S(1)}, u32[]{:S(2)}, u32[]{:S(2)}) collective-permute-start(bf16[512,1024]{1,0:T(8,128)(2,1)S(1)} %get-tuple-element.25), channel_id=1, source_target_pairs={{0,2},{2,0},{1,3},{3,1},{4,6},{6,4},{5,7},{7,5},{8,10},{10,8},{9,1... | collective-permute-start | bytes 3145736 | tf_op jit(solution)/shard_map/ppermute | solution.py:275
  77.4 1.5 %shard_map.124.weight.weight_b = bf16[512,512]{1,0:T(8,128)(2,1)S(1)} custom-call(f32[2]{0:T(128)S(1)} %pad_maximum_fusion.scal, s32[1,512]{1,0:T(1,128)S(1)} %reshape.115.columns, bf16[512,1024]{1,0:T(8,128)(2,1)S(1)} %get-tuple-element.26.texts, bf16[512,1152]{1,0:T(8,128)(2,1)S(1)} %bitcast.17), custom_call_target="tpu_custom_call" | custom-call | flops 1000 | bytes 1000 | tf_op jit(solution)/shard_map/pallas_call | solution.py:192
  78.8 0.8 collective-permute-done.3.got
  79.6 0.9 shard_map.125
  80.6 0.0 copy-start.5
  80.6 0.7 copy-done.5
  81.3 2.3 %shard_map.126 = bf16[16,2,32,512]{3,2,1,0:T(8,128)(2,1)} custom-call(bf16[512,512]{1,0:T(8,128)(2,1)S(1)} %get-tuple-element.33.weight_a, bf16[512,1152]{1,0:T(8,128)(2,1)S(1)} %collective-permute-done.2.img.img_a, bf16[512,512]{1,0:T(8,128)(2,1)S(1)} %shard_map.124.weight.weight_b, bf16[512,1152]{1,0:T(8,128)(2,1)S(1)} %bitcast.18), custom_call_target="tpu_custom_call" | custom-call | flops 1000 | bytes 1000 | tf_op jit(solution)/shard_map/pallas_call | solution.py:192
  83.5 3.8 %all-to-all-start.2 = ((bf16[16,2,32,512]{3,2,1,0:T(8,128)(2,1)}), bf16[16,2,32,512]{3,2,1,0:T(8,128)(2,1)S(1)}, u32[]{:S(2)}, u32[]{:S(2)}) async-start(bf16[16,2,32,512]{3,2,1,0:T(8,128)(2,1)} %shard_map.126), calls=%async_computation.2 | async-start | bytes 2097152 | tf_op jit(solution)/shard_map/all_to_all | solution.py:297
  87.3 4.9 %collective-permute-start.4 = (bf16[128,1024]{1,0:T(8,128)(2,1)S(1)}, bf16[128,1024]{1,0:T(8,128)(2,1)S(1)}, u32[]{:S(2)}, u32[]{:S(2)}) collective-permute-start(bf16[128,1024]{1,0:T(8,128)(2,1)S(1)} %get-tuple-element.30), channel_id=1, source_target_pairs={{0,192},{64,0},{128,64},{192,128},{1,193},{65,1},{129,65},{193,129... | collective-permute-start | bytes 786440 | tf_op jit(solution)/shard_map/ppermute | solution.py:289
  92.3 1.1 collective-permute-start.5
  93.4 2.1 %collective-permute-start.6 = (bf16[128,1024]{1,0:T(8,128)(2,1)S(1)}, bf16[128,1024]{1,0:T(8,128)(2,1)S(1)}, u32[]{:S(2)}, u32[]{:S(2)}) collective-permute-start(bf16[128,1024]{1,0:T(8,128)(2,1)S(1)} %get-tuple-element.32), channel_id=1, source_target_pairs={{0,64},{64,128},{128,192},{192,0},{1,65},{65,129},{129,193},{193,1... | collective-permute-start | bytes 786440 | tf_op jit(solution)/shard_map/ppermute | solution.py:289
  95.5 7.2 %all-to-all-done.2 = bf16[16,2,32,512]{3,2,1,0:T(8,128)(2,1)S(1)} async-done(((bf16[16,2,32,512]{3,2,1,0:T(8,128)(2,1)}), bf16[16,2,32,512]{3,2,1,0:T(8,128)(2,1)S(1)}, u32[]{:S(2)}, u32[]{:S(2)}) %all-to-all-start.2) | async-done | bytes 1048608 | tf_op jit(solution)/shard_map/all_to_all | solution.py:297
  102.8 0.1 convert_reduce_fusion
  102.9 0.4 collective-permute-start.7
  103.3 7.3 %collective-permute-done.5 = bf16[128,1024]{1,0:T(8,128)(2,1)S(1)} collective-permute-done((bf16[128,1024]{1,0:T(8,128)(2,1)S(1)}, bf16[128,1024]{1,0:T(8,128)(2,1)S(1)}, u32[]{:S(2)}, u32[]{:S(2)}) %collective-permute-start.5) | collective-permute-done | bytes 262176 | tf_op jit(solution)/shard_map/ppermute | solution.py:289
  110.5 4.1 %collective-permute-done.6 = bf16[128,1024]{1,0:T(8,128)(2,1)S(1)} collective-permute-done((bf16[128,1024]{1,0:T(8,128)(2,1)S(1)}, bf16[128,1024]{1,0:T(8,128)(2,1)S(1)}, u32[]{:S(2)}, u32[]{:S(2)}) %collective-permute-start.6) | collective-permute-done | bytes 262176 | tf_op jit(solution)/shard_map/ppermute | solution.py:289
  114.6 0.0 collective-permute-done.4
  114.6 0.9 convert_add_fusion
  115.6 2.1 %collective-permute-done.7 = f32[32,512]{1,0:T(8,128)S(1)} collective-permute-done((f32[32,512]{1,0:T(8,128)S(1)}, f32[32,512]{1,0:T(8,128)S(1)}, u32[]{:S(2)}, u32[]{:S(2)}) %collective-permute-start.7) | collective-permute-done | bytes 65568 | tf_op jit(solution)/shard_map/ppermute | solution.py:302
  117.7 0.6 bitcast_add_fusion
  (16 shorter events, 0.1 us)
Async XLA Ops:
  0.6 25.8 %collective-permute-start = (bf16[1024,512]{1,0:T(8,128)(2,1)}, bf16[1024,512]{1,0:T(8,128)(2,1)S(1)}, u32[]{:S(2)}, u32[]{:S(2)}) collective-permute-start(bf16[1024,512]{1,0:T(8,128)(2,1)} %tokens.1), channel_id=1, source_target_pairs={{0,1},{1,0},{2,3},{3,2},{4,5},{5,4},{6,7},{7,6},{8,9},{9,8},{10,11... | collective-permute-start | bytes 3145736 | tf_op jit(solution)/shard_map/ppermute | solution.py:212
  7.3 19.2 %copy-start.3 = (s32[1,1024]{1,0:T(1,128)S(1)}, s32[1,1024]{1,0:T(1,128)}, u32[]{:S(2)}) copy-start(s32[1,1024]{1,0:T(1,128)} %slot.1) | copy-start | bytes 12292
  7.3 19.2 %copy-start.4 = (bf16[1024,512]{1,0:T(8,128)(2,1)S(1)}, bf16[1024,512]{1,0:T(8,128)(2,1)}, u32[]{:S(2)}) copy-start(bf16[1024,512]{1,0:T(8,128)(2,1)} %tokens.1) | copy-start | bytes 3145732
  7.3 19.2 %copy-start.7 = (f32[1024]{0:T(1024)S(1)}, f32[1024]{0:T(1024)}, u32[]{:S(2)}) copy-start(f32[1024]{0:T(1024)} %param.11) | copy-start | bytes 12292
  8.5 38.9 %all-to-all-start.1 = ((bf16[4,128,1152]{2,1,0:T(8,128)(2,1)}), bf16[4,128,1152]{2,1,0:T(8,128)(2,1)S(1)}, u32[]{:S(2)}, u32[]{:S(2)}) async-start(bf16[4,128,1152]{2,1,0:T(8,128)(2,1)} %broadcast_in_dim.16), calls=%async_computation.1 | async-start | bytes 2359296 | tf_op jit(solution)/shard_map/all_to_all | solution.py:218
  36.4 0.6 copy-start.1
  37.0 6.3 %copy-start = (f32[32,1024]{1,0:T(8,128)}, f32[32,1024]{1,0:T(8,128)S(1)}, u32[]{:S(2)}) copy-start(f32[32,1024]{1,0:T(8,128)S(1)} %get-tuple-element.19.mine) | copy-start | bytes 393220
  37.0 6.3 %collective-permute-start.1 = (f32[32,1024]{1,0:T(8,128)S(1)}, f32[32,1024]{1,0:T(8,128)S(1)}, u32[]{:S(2)}, u32[]{:S(2)}) collective-permute-start(f32[32,1024]{1,0:T(8,128)S(1)} %get-tuple-element.19.mine), channel_id=1, source_target_pairs={{0,1},{1,0},{2,3},{3,2},{4,5},{5,4},{6,7},{7,6},{8,9},{9,8},{10,11... | collective-permute-start | bytes 393224 | tf_op jit(solution)/shard_map/ppermute | solution.py:244
  43.3 0.6 copy-start.8
  47.4 23.1 %copy-start.2 = (f32[32,512]{1,0:T(8,128)S(1)}, f32[32,512]{1,0:T(8,128)}, u32[]{:S(2)}) copy-start(f32[32,512]{1,0:T(8,128)} %get-tuple-element.22.exact) | copy-start | bytes 196612
  47.4 23.1 %all-to-all-start = ((bf16[32,32,512]{2,1,0:T(8,128)(2,1)}), bf16[32,32,512]{2,1,0:T(8,128)(2,1)S(1)}, u32[]{:S(2)}, u32[]{:S(2)}) async-start(bf16[32,32,512]{2,1,0:T(8,128)(2,1)} %get-tuple-element.21), calls=%async_computation | async-start | bytes 2097152 | tf_op jit(solution)/shard_map/all_to_all | solution.py:255
  56.0 5.2 %collective-permute-start.2 = (bf16[512,1152]{1,0:T(8,128)(2,1)S(1)}, bf16[512,1152]{1,0:T(8,128)(2,1)S(1)}, u32[]{:S(2)}, u32[]{:S(2)}) collective-permute-start(bf16[512,1152]{1,0:T(8,128)(2,1)S(1)} %bitcast.16), channel_id=1, source_target_pairs={{0,2},{2,0},{1,3},{3,1},{4,6},{6,4},{5,7},{7,5},{8,10},{10,8},{9,1... | collective-permute-start | bytes 3538952 | tf_op jit(solution)/shard_map/ppermute | solution.py:258
  73.3 6.4 %collective-permute-start.3 = (bf16[512,1024]{1,0:T(8,128)(2,1)S(1)}, bf16[512,1024]{1,0:T(8,128)(2,1)S(1)}, u32[]{:S(2)}, u32[]{:S(2)}) collective-permute-start(bf16[512,1024]{1,0:T(8,128)(2,1)S(1)} %get-tuple-element.25), channel_id=1, source_target_pairs={{0,2},{2,0},{1,3},{3,1},{4,6},{6,4},{5,7},{7,5},{8,10},{10,8},{9,1... | collective-permute-start | bytes 3145736 | tf_op jit(solution)/shard_map/ppermute | solution.py:275
  80.6 0.7 copy-start.5
  83.5 8.7 %copy-start.6 = (bf16[128,1024]{1,0:T(8,128)(2,1)S(1)}, bf16[128,1024]{1,0:T(8,128)(2,1)}, u32[]{:S(2)}) copy-start(bf16[128,1024]{1,0:T(8,128)(2,1)} %copy-done.5) | copy-start | bytes 786436
  83.5 19.2 %all-to-all-start.2 = ((bf16[16,2,32,512]{3,2,1,0:T(8,128)(2,1)}), bf16[16,2,32,512]{3,2,1,0:T(8,128)(2,1)S(1)}, u32[]{:S(2)}, u32[]{:S(2)}) async-start(bf16[16,2,32,512]{3,2,1,0:T(8,128)(2,1)} %shard_map.126), calls=%async_computation.2 | async-start | bytes 2097152 | tf_op jit(solution)/shard_map/all_to_all | solution.py:297
  87.3 27.3 %collective-permute-start.4 = (bf16[128,1024]{1,0:T(8,128)(2,1)S(1)}, bf16[128,1024]{1,0:T(8,128)(2,1)S(1)}, u32[]{:S(2)}, u32[]{:S(2)}) collective-permute-start(bf16[128,1024]{1,0:T(8,128)(2,1)S(1)} %get-tuple-element.30), channel_id=1, source_target_pairs={{0,192},{64,0},{128,64},{192,128},{1,193},{65,1},{129,65},{193,129... | collective-permute-start | bytes 786440 | tf_op jit(solution)/shard_map/ppermute | solution.py:289
  92.3 18.3 %collective-permute-start.5 = (bf16[128,1024]{1,0:T(8,128)(2,1)S(1)}, bf16[128,1024]{1,0:T(8,128)(2,1)S(1)}, u32[]{:S(2)}, u32[]{:S(2)}) collective-permute-start(bf16[128,1024]{1,0:T(8,128)(2,1)S(1)} %copy-done.6), channel_id=1, source_target_pairs={{0,128},{64,192},{128,0},{192,64},{1,129},{65,193},{129,1},{193,65... | collective-permute-start | bytes 786440 | tf_op jit(solution)/shard_map/ppermute | solution.py:289
  93.4 21.2 %collective-permute-start.6 = (bf16[128,1024]{1,0:T(8,128)(2,1)S(1)}, bf16[128,1024]{1,0:T(8,128)(2,1)S(1)}, u32[]{:S(2)}, u32[]{:S(2)}) collective-permute-start(bf16[128,1024]{1,0:T(8,128)(2,1)S(1)} %get-tuple-element.32), channel_id=1, source_target_pairs={{0,64},{64,128},{128,192},{192,0},{1,65},{65,129},{129,193},{193,1... | collective-permute-start | bytes 786440 | tf_op jit(solution)/shard_map/ppermute | solution.py:289
  102.9 14.7 %collective-permute-start.7 = (f32[32,512]{1,0:T(8,128)S(1)}, f32[32,512]{1,0:T(8,128)S(1)}, u32[]{:S(2)}, u32[]{:S(2)}) collective-permute-start(f32[32,512]{1,0:T(8,128)S(1)} %select_bitcast_fusion), channel_id=1, source_target_pairs={{0,32},{32,0},{1,33},{33,1},{2,34},{34,2},{3,35},{35,3},{4,36},{36... | collective-permute-start | bytes 196616 | tf_op jit(solution)/shard_map/ppermute | solution.py:302

commit v4 on v3

--- a/solution.py
+++ b/solution.py
@@ -13,6 +13,8 @@
 GELU_A = 0.7978845608028654
 GELU_B = GELU_A * 0.044715
 PAD = 128
+IMAGE_LIMIT = 54
+TEXT_LIMIT = 20
 AXES = ("zh", "zl", "xl", "y", "core", "xh")
 SIZES = (4, 2, 2, 4, 2, 2)
 DP = ("zh", "zl", "xl", "y", "core")
@@ -30,22 +32,6 @@
 
 def shift(n, k):
     return [(i, (i + k) % n) for i in range(n)]
-
-
-def head_kernel(mine, got, states, counts, projection, emb, sent, block, sems):
-    pooled = ((states[...] + (mine[...] + got[...])) / counts[...]).astype(BF)
-    result = dot(pooled, projection[...])
-    block[...] = jnp.broadcast_to(result.astype(BF)[None], block.shape)
-    n = block.shape[0]
-    stores = [
-        pltpu.make_async_copy(block, sent.at[pl.ds(i * n, n)], sems.at[i])
-        for i in range(sent.shape[0] // n)
-    ]
-    for store in stores:
-        store.start()
-    emb[...] = result
-    for store in stores:
-        store.wait()
 
 
 def mlp_kernel(
@@ -180,7 +166,7 @@
                 out[2 * g + h, z] = gt[row : row + CAP_DEV, h * half : (h + 1) * half].astype(BF)
 
 
-def call(kernel, args, outs, scalars=0, far=(), free=(), far_out=(), scratch=(), cost=SMALL, limit=20):
+def call(kernel, args, outs, scalars=0, far=(), free=(), scratch=(), cost=SMALL, limit=20):
     in_specs = [
         pl.BlockSpec(
             memory_space=pltpu.SMEM
@@ -192,10 +178,7 @@
     return pl.pallas_call(
         kernel,
         in_specs=in_specs,
-        out_specs=[
-            pl.BlockSpec(memory_space=pltpu.HBM if i in far_out else pltpu.VMEM)
-            for i in range(len(outs))
-        ],
+        out_specs=[pl.BlockSpec(memory_space=pltpu.VMEM) for _ in outs],
         out_shape=[jax.ShapeDtypeStruct(shape, dtype) for shape, dtype in outs],
         scratch_shapes=list(scratch),
         compiler_params=pltpu.CompilerParams(vmem_limit_bytes=limit << 20),
@@ -239,17 +222,10 @@
         cost=LARGE,
         limit=48,
     )
-    emb, sent = call(
-        head_kernel,
-        (partial_out, lax.ppermute(partial_out, MP, SWAP), states, counts[:, None], projection),
-        [((CAP_DEV, projection.shape[1]), F32), ((32, CAP_DEV, projection.shape[1]), BF)],
-        far_out=(1,),
-        limit=60,
-        scratch=(
-            pltpu.VMEM((8, CAP_DEV, projection.shape[1]), BF),
-            pltpu.SemaphoreType.DMA((4,)),
-        ),
-    )
+    summed = partial_out + lax.ppermute(partial_out, MP, SWAP)
+    pooled = ((states + summed) / counts[:, None]).astype(BF)
+    emb = dot(pooled, projection)
+    sent = jnp.broadcast_to(emb.astype(BF)[None], (32,) + emb.shape)
 
     group = ("zl", "y", "xl", "xh")
     embs = lax.all_to_all(sent, group, split_axis=0, concat_axis=0, tiled=True)
@@ -284,6 +260,7 @@
         [((IMG_ROWS, e), F32)] + [((IMG_ROWS, e), BF)] * 3,
         1,
         scratch=(pltpu.VMEM((images_half, e), F32),),
+        limit=IMAGE_LIMIT,
     )
     for k, part in enumerate(rest):
         grad_image += lax.ppermute(part, "zh", shift(4, -k - 1)).astype(F32)
@@ -293,6 +270,7 @@
         text_kernel,
         (weight_other, img_other, weight_mine, img_mine),
         [((16, 2, CAP_DEV, e // 2), BF)],
+        limit=TEXT_LIMIT,
     )
     got = lax.all_to_all(gt, ("y", "xl", "xh"), split_axis=0, concat_axis=0, tiled=True)
     gathered = jnp.sum(got.astype(F32), axis=0)

time: 119 us -> 120 us (level)
    pallas_call x6 -> x5, Pallas kernels: 20.8 us -> 20 us  [call(): pl.pallas_call(kernel, in_specs=in_specs, out_specs=[pl.BlockSpec(memory_...]
    unnamed x19 -> x21, local copies, waits for them, and re-layouts: 2.13 us -> 2.92 us
  transfers between devices with their start and end apart: 11 -> 11, of which waited for: 9 -> 8; matrix products, arithmetic and copies ran while one was open for 5% -> 5% of each run, Pallas kernels for 13% -> 10%
where the time goes in v4:
time: 120 us; the launch traced here: 119 us
  starting transfers between devices  43.5 us (36%)
  waiting for transfers between devices  43.4 us (36%)
  Pallas kernels  20 us (17%)
  local copies, waits for them, and re-layouts  5.24 us (4%)
  other arithmetic  4.87 us (4%)
  between operations  2.09 us (2%)
    pallas_call x5, Pallas kernels, call(): pl.pallas_call(kernel, in_specs=in_specs, out_specs=[pl.BlockSpec(memory_...  20 us
    ppermute x3, waiting for transfers between devices, on_device(): grad_image += lax.ppermute(part, 'zh', shift(4, -k - 1)).astype(F32)  11.7 us
    ppermute x1, waiting for transfers between devices, on_device(): other = lax.ppermute(tokens, MP, SWAP)  9.78 us
    all_to_all x1, waiting for transfers between devices, on_device(): embs = lax.all_to_all(sent, group, split_axis=0, concat_axis=0, tiled=True)  9.23 us
    all_to_all x1, starting transfers between devices, on_device(): embs = lax.all_to_all(sent, group, split_axis=0, concat_axis=0, tiled=True)  8.72 us
    all_to_all x1, starting transfers between devices, on_device(): lax.all_to_all(jnp.broadcast_to(img[None], (4,) + img.shape), 'zh', split...  8.18 us
    ppermute x3, starting transfers between devices, on_device(): grad_image += lax.ppermute(part, 'zh', shift(4, -k - 1)).astype(F32)  8.16 us
    all_to_all x1, waiting for transfers between devices, on_device(): lax.all_to_all(gt, ('y', 'xl', 'xh'), split_axis=0, concat_axis=0, tiled=...  7.25 us
  transfers between devices with their start and end apart: 11, of which 8 were waited for; matrix products, arithmetic and copies ran while one was open for 5% of the time, Pallas kernels for 10%

profile of v4, /device:TPU:1, one launch (start us, length us, event | category | flops | bytes accessed | tf_op | source)
XLA Modules:
  0.0 119.4 jit_solution(5061605112073484386)
XLA Ops:
  0.6 0.0 copy-start
  0.6 3.7 %collective-permute-start = (bf16[1024,512]{1,0:T(8,128)(2,1)}, bf16[1024,512]{1,0:T(8,128)(2,1)}, u32[]{:S(2)}, u32[]{:S(2)}) collective-permute-start(bf16[1024,512]{1,0:T(8,128)(2,1)} %tokens.1), channel_id=1, source_target_pairs={{0,1},{1,0},{2,3},{3,2},{4,5},{5,4},{6,7},{7,6},{8,9},{9,8},{10,11... | collective-permute-start | bytes 3145736 | tf_op jit(solution)/shard_map/ppermute | solution.py:195
  4.3 1.1 fusion.1
  5.4 0.7 fusion.8
  6.1 0.1 copy.15
  6.2 1.1 fusion.2
  7.3 0.0 copy-start.5
  7.3 0.0 copy-start.6
  7.3 0.0 copy-start.7
  7.4 1.1 broadcast_in_dim.8
  8.5 8.2 %all-to-all-start.1 = ((bf16[4,128,1152]{2,1,0:T(8,128)(2,1)}), bf16[4,128,1152]{2,1,0:T(8,128)(2,1)S(1)}, u32[]{:S(2)}, u32[]{:S(2)}) async-start(bf16[4,128,1152]{2,1,0:T(8,128)(2,1)} %broadcast_in_dim.8), calls=%async_computation.1 | async-start | bytes 2359296 | tf_op jit(solution)/shard_map/all_to_all | solution.py:201
  16.7 9.8 %collective-permute-done.arrived = bf16[1024,512]{1,0:T(8,128)(2,1)} collective-permute-done((bf16[1024,512]{1,0:T(8,128)(2,1)}, bf16[1024,512]{1,0:T(8,128)(2,1)}, u32[]{:S(2)}, u32[]{:S(2)}) %collective-permute-start) | collective-permute-done | bytes 1048608 | tf_op jit(solution)/shard_map/ppermute | solution.py:195
  26.5 10.1 %shard_map.121 = (f32[32,1024]{1,0:T(8,128)S(1)}, f32[32,1024]{1,0:T(8,128)S(1)}) custom-call(s32[1]{0:T(128)} %bitcast.1.low, s32[1,1024]{1,0:T(1,128)S(1)} %copy-done.5, bf16[1024,512]{1,0:T(8,128)(2,1)S(1)} %copy-done.6, bf16[1024,512]{1,0:T(8,128)(2,1)} %collective-permute-done.arrived, f32[1,1024]{1,0:T(1,128)S(1)} %bitcast.20, ...), custom_call_target="tpu_custom_call" | custom-call | flops 10000000000 | bytes 1000 | tf_op jit(solution)/shard_map/pallas_call | solution.py:178
  36.5 3.8 %collective-permute-start.1 = (f32[32,1024]{1,0:T(8,128)S(1)}, f32[32,1024]{1,0:T(8,128)S(1)}, u32[]{:S(2)}, u32[]{:S(2)}) collective-permute-start(f32[32,1024]{1,0:T(8,128)S(1)} %get-tuple-element.18), channel_id=1, source_target_pairs={{0,1},{1,0},{2,3},{3,2},{4,5},{5,4},{6,7},{7,6},{8,9},{9,8},{10,11... | collective-permute-start | bytes 393224 | tf_op jit(solution)/shard_map/ppermute | solution.py:225
  40.4 0.1 convert_reduce_fusion.1
  40.5 2.5 %collective-permute-done.1 = f32[32,1024]{1,0:T(8,128)S(1)} collective-permute-done((f32[32,1024]{1,0:T(8,128)S(1)}, f32[32,1024]{1,0:T(8,128)S(1)}, u32[]{:S(2)}, u32[]{:S(2)}) %collective-permute-start.1) | collective-permute-done | bytes 131104 | tf_op jit(solution)/shard_map/ppermute | solution.py:225
  43.0 0.3 fusion.9
  43.4 0.0 all-to-all-done.1
  43.4 1.1 broadcast_in_dim.7
  44.5 8.7 %all-to-all-start = ((bf16[32,32,512]{2,1,0:T(8,128)(2,1)}), bf16[32,32,512]{2,1,0:T(8,128)(2,1)}, u32[]{:S(2)}, u32[]{:S(2)}) async-start(bf16[32,32,512]{2,1,0:T(8,128)(2,1)} %broadcast_in_dim.7), calls=%async_computation | async-start | bytes 2097152 | tf_op jit(solution)/shard_map/all_to_all | solution.py:231
  53.2 2.8 %collective-permute-start.2 = (bf16[512,1152]{1,0:T(8,128)(2,1)S(1)}, bf16[512,1152]{1,0:T(8,128)(2,1)S(1)}, u32[]{:S(2)}, u32[]{:S(2)}) collective-permute-start(bf16[512,1152]{1,0:T(8,128)(2,1)S(1)} %bitcast.16), channel_id=1, source_target_pairs={{0,2},{2,0},{1,3},{3,1},{4,6},{6,4},{5,7},{7,5},{8,10},{10,8},{9,1... | collective-permute-start | bytes 3538952 | tf_op jit(solution)/shard_map/ppermute | solution.py:234
  57.3 0.1 multiply_add_fusion
  57.4 0.1 reshape.117.columns
  57.4 0.1 pad_maximum_fusion.scal
  57.5 0.9 collective-permute-done.2.img.img_a
  58.4 9.2 %all-to-all-done = bf16[32,32,512]{2,1,0:T(8,128)(2,1)} async-done(((bf16[32,32,512]{2,1,0:T(8,128)(2,1)}), bf16[32,32,512]{2,1,0:T(8,128)(2,1)}, u32[]{:S(2)}, u32[]{:S(2)}) %all-to-all-start) | async-done | bytes 1048608 | tf_op jit(solution)/shard_map/all_to_all | solution.py:231
  67.7 3.5 %shard_map.122 = (bf16[32,512]{1,0:T(8,128)(2,1)}, bf16[512,1024]{1,0:T(8,128)(2,1)S(1)}, bf16[512,512]{1,0:T(8,128)(2,1)S(1)}, bf16[512,1024]{1,0:T(8,128)(2,1)S(1)}) custom-call(f32[2]{0:T(128)S(1)} %pad_maximum_fusion.scal, s32[1]{0:T(128)} %bitcast.place, s32[1,512]{1,0:T(1,128)S(1)} %reshape.117.columns, bf16[16,2,32,512]{3,2,1,0:T(8,128)(2,1)} %bitcast.4.emb, ...), custom_call_target="tpu_custom_call" | custom-call | flops 1000 | bytes 1000 | tf_op jit(solution)/shard_map/pallas_call | solution.py:178
  71.1 4.1 %collective-permute-start.3 = (bf16[512,1024]{1,0:T(8,128)(2,1)S(1)}, bf16[512,1024]{1,0:T(8,128)(2,1)S(1)}, u32[]{:S(2)}, u32[]{:S(2)}) collective-permute-start(bf16[512,1024]{1,0:T(8,128)(2,1)S(1)} %get-tuple-element.21), channel_id=1, source_target_pairs={{0,2},{2,0},{1,3},{3,1},{4,6},{6,4},{5,7},{7,5},{8,10},{10,8},{9,1... | collective-permute-start | bytes 3145736 | tf_op jit(solution)/shard_map/ppermute | solution.py:251
  75.2 1.5 %shard_map.123.weight.weight_b = bf16[512,512]{1,0:T(8,128)(2,1)S(1)} custom-call(f32[2]{0:T(128)S(1)} %pad_maximum_fusion.scal, s32[1,512]{1,0:T(1,128)S(1)} %reshape.117.columns, bf16[512,1024]{1,0:T(8,128)(2,1)S(1)} %get-tuple-element.22.texts, bf16[512,1152]{1,0:T(8,128)(2,1)S(1)} %bitcast.17), custom_call_target="tpu_custom_call" | custom-call | flops 1000 | bytes 1000 | tf_op jit(solution)/shard_map/pallas_call | solution.py:178
  76.7 0.0 copy-start.1
  76.7 0.8 copy-done.1
  77.5 0.0 collective-permute-done.3.got
  77.5 1.0 copy-done.8
  78.5 3.7 %shard_map.124 = (f32[128,1024]{1,0:T(8,128)}, bf16[128,1024]{1,0:T(8,128)(2,1)}, bf16[128,1024]{1,0:T(8,128)(2,1)}, bf16[128,1024]{1,0:T(8,128)(2,1)}) custom-call(s32[1]{0:T(128)} %bitcast.8.place, bf16[512,512]{1,0:T(8,128)(2,1)} %copy-done.1, bf16[512,1024]{1,0:T(8,128)(2,1)} %copy-done.4, bf16[512,1024]{1,0:T(8,128)(2,1)} %copy-done.8), custom_call_target="tpu_custom_call" | custom-call | flops 1000 | bytes 1000 | tf_op jit(solution)/shard_map/pallas_call | solution.py:178
  82.2 1.3 %shard_map.125 = bf16[16,2,32,512]{3,2,1,0:T(8,128)(2,1)S(1)} custom-call(bf16[512,512]{1,0:T(8,128)(2,1)S(1)} %get-tuple-element.29.weight_a, bf16[512,1152]{1,0:T(8,128)(2,1)S(1)} %collective-permute-done.2.img.img_a, bf16[512,512]{1,0:T(8,128)(2,1)S(1)} %copy-done.2, bf16[512,1152]{1,0:T(8,128)(2,1)S(1)} %bitcast.18), custom_call_target="tpu_custom_call" | custom-call | flops 1000 | bytes 1000 | tf_op jit(solution)/shard_map/pallas_call | solution.py:178
  83.5 1.0 copy-done.3
  84.4 3.8 %all-to-all-start.2 = ((bf16[16,2,32,512]{3,2,1,0:T(8,128)(2,1)}), bf16[16,2,32,512]{3,2,1,0:T(8,128)(2,1)S(1)}, u32[]{:S(2)}, u32[]{:S(2)}) async-start(bf16[16,2,32,512]{3,2,1,0:T(8,128)(2,1)} %copy-done.3), calls=%async_computation.2 | async-start | bytes 2097152 | tf_op jit(solution)/shard_map/all_to_all | solution.py:275
  88.2 4.9 %collective-permute-start.4 = (bf16[128,1024]{1,0:T(8,128)(2,1)}, bf16[128,1024]{1,0:T(8,128)(2,1)S(1)}, u32[]{:S(2)}, u32[]{:S(2)}) collective-permute-start(bf16[128,1024]{1,0:T(8,128)(2,1)} %get-tuple-element.26), channel_id=1, source_target_pairs={{0,192},{64,0},{128,64},{192,128},{1,193},{65,1},{129,65},{193,129... | collective-permute-start | bytes 786440 | tf_op jit(solution)/shard_map/ppermute | solution.py:266
  93.2 1.1 collective-permute-start.5
  94.3 2.1 %collective-permute-start.6 = (bf16[128,1024]{1,0:T(8,128)(2,1)}, bf16[128,1024]{1,0:T(8,128)(2,1)S(1)}, u32[]{:S(2)}, u32[]{:S(2)}) collective-permute-start(bf16[128,1024]{1,0:T(8,128)(2,1)} %get-tuple-element.28), channel_id=1, source_target_pairs={{0,64},{64,128},{128,192},{192,0},{1,65},{65,129},{129,193},{193,1... | collective-permute-start | bytes 786440 | tf_op jit(solution)/shard_map/ppermute | solution.py:266
  96.4 7.2 %all-to-all-done.2 = bf16[16,2,32,512]{3,2,1,0:T(8,128)(2,1)S(1)} async-done(((bf16[16,2,32,512]{3,2,1,0:T(8,128)(2,1)}), bf16[16,2,32,512]{3,2,1,0:T(8,128)(2,1)S(1)}, u32[]{:S(2)}, u32[]{:S(2)}) %all-to-all-start.2) | async-done | bytes 1048608 | tf_op jit(solution)/shard_map/all_to_all | solution.py:275
  103.7 0.1 convert_reduce_fusion
  103.8 0.4 collective-permute-start.7
  104.2 7.4 %collective-permute-done.5 = bf16[128,1024]{1,0:T(8,128)(2,1)S(1)} collective-permute-done((bf16[128,1024]{1,0:T(8,128)(2,1)}, bf16[128,1024]{1,0:T(8,128)(2,1)S(1)}, u32[]{:S(2)}, u32[]{:S(2)}) %collective-permute-start.5) | collective-permute-done | bytes 262176 | tf_op jit(solution)/shard_map/ppermute | solution.py:266
  111.6 4.2 %collective-permute-done.6 = bf16[128,1024]{1,0:T(8,128)(2,1)S(1)} collective-permute-done((bf16[128,1024]{1,0:T(8,128)(2,1)}, bf16[128,1024]{1,0:T(8,128)(2,1)S(1)}, u32[]{:S(2)}, u32[]{:S(2)}) %collective-permute-start.6) | collective-permute-done | bytes 262176 | tf_op jit(solution)/shard_map/ppermute | solution.py:266
  115.9 0.9 convert_add_fusion
  116.8 2.0 %collective-permute-done.7 = f32[32,512]{1,0:T(8,128)S(1)} collective-permute-done((f32[32,512]{1,0:T(8,128)S(1)}, f32[32,512]{1,0:T(8,128)S(1)}, u32[]{:S(2)}, u32[]{:S(2)}) %collective-permute-start.7) | collective-permute-done | bytes 65568 | tf_op jit(solution)/shard_map/ppermute | solution.py:280
  118.8 0.6 bitcast_add_fusion
  (18 shorter events, 0.1 us)
Async XLA Ops:
  0.6 42.4 %copy-start = (bf16[1024,512]{1,0:T(8,128)(2,1)S(1)}, bf16[1024,512]{1,0:T(8,128)(2,1)}, u32[]{:S(2)}) copy-start(bf16[1024,512]{1,0:T(8,128)(2,1)} %param.14) | copy-start | bytes 3145732
  0.6 25.8 %collective-permute-start = (bf16[1024,512]{1,0:T(8,128)(2,1)}, bf16[1024,512]{1,0:T(8,128)(2,1)}, u32[]{:S(2)}, u32[]{:S(2)}) collective-permute-start(bf16[1024,512]{1,0:T(8,128)(2,1)} %tokens.1), channel_id=1, source_target_pairs={{0,1},{1,0},{2,3},{3,2},{4,5},{5,4},{6,7},{7,6},{8,9},{9,8},{10,11... | collective-permute-start | bytes 3145736 | tf_op jit(solution)/shard_map/ppermute | solution.py:195
  7.3 19.2 %copy-start.5 = (s32[1,1024]{1,0:T(1,128)S(1)}, s32[1,1024]{1,0:T(1,128)}, u32[]{:S(2)}) copy-start(s32[1,1024]{1,0:T(1,128)} %slot.1) | copy-start | bytes 12292
  7.3 19.2 %copy-start.6 = (bf16[1024,512]{1,0:T(8,128)(2,1)S(1)}, bf16[1024,512]{1,0:T(8,128)(2,1)}, u32[]{:S(2)}) copy-start(bf16[1024,512]{1,0:T(8,128)(2,1)} %tokens.1) | copy-start | bytes 3145732
  7.3 19.1 %copy-start.7 = (f32[1024]{0:T(1024)S(1)}, f32[1024]{0:T(1024)}, u32[]{:S(2)}) copy-start(f32[1024]{0:T(1024)} %param.11) | copy-start | bytes 12292
  8.5 34.9 %all-to-all-start.1 = ((bf16[4,128,1152]{2,1,0:T(8,128)(2,1)}), bf16[4,128,1152]{2,1,0:T(8,128)(2,1)S(1)}, u32[]{:S(2)}, u32[]{:S(2)}) async-start(bf16[4,128,1152]{2,1,0:T(8,128)(2,1)} %broadcast_in_dim.8), calls=%async_computation.1 | async-start | bytes 2359296 | tf_op jit(solution)/shard_map/all_to_all | solution.py:201
  36.5 6.5 %collective-permute-start.1 = (f32[32,1024]{1,0:T(8,128)S(1)}, f32[32,1024]{1,0:T(8,128)S(1)}, u32[]{:S(2)}, u32[]{:S(2)}) collective-permute-start(f32[32,1024]{1,0:T(8,128)S(1)} %get-tuple-element.18), channel_id=1, source_target_pairs={{0,1},{1,0},{2,3},{3,2},{4,5},{5,4},{6,7},{7,6},{8,9},{9,8},{10,11... | collective-permute-start | bytes 393224 | tf_op jit(solution)/shard_map/ppermute | solution.py:225
  44.5 23.2 %all-to-all-start = ((bf16[32,32,512]{2,1,0:T(8,128)(2,1)}), bf16[32,32,512]{2,1,0:T(8,128)(2,1)}, u32[]{:S(2)}, u32[]{:S(2)}) async-start(bf16[32,32,512]{2,1,0:T(8,128)(2,1)} %broadcast_in_dim.7), calls=%async_computation | async-start | bytes 2097152 | tf_op jit(solution)/shard_map/all_to_all | solution.py:231
  53.2 5.2 %collective-permute-start.2 = (bf16[512,1152]{1,0:T(8,128)(2,1)S(1)}, bf16[512,1152]{1,0:T(8,128)(2,1)S(1)}, u32[]{:S(2)}, u32[]{:S(2)}) collective-permute-start(bf16[512,1152]{1,0:T(8,128)(2,1)S(1)} %bitcast.16), channel_id=1, source_target_pairs={{0,2},{2,0},{1,3},{3,1},{4,6},{6,4},{5,7},{7,5},{8,10},{10,8},{9,1... | collective-permute-start | bytes 3538952 | tf_op jit(solution)/shard_map/ppermute | solution.py:234
  71.1 6.4 %copy-start.4 = (bf16[512,1024]{1,0:T(8,128)(2,1)}, bf16[512,1024]{1,0:T(8,128)(2,1)S(1)}, u32[]{:S(2)}) copy-start(bf16[512,1024]{1,0:T(8,128)(2,1)S(1)} %get-tuple-element.22.texts) | copy-start | bytes 3145732
  71.1 6.4 %collective-permute-start.3 = (bf16[512,1024]{1,0:T(8,128)(2,1)S(1)}, bf16[512,1024]{1,0:T(8,128)(2,1)S(1)}, u32[]{:S(2)}, u32[]{:S(2)}) collective-permute-start(bf16[512,1024]{1,0:T(8,128)(2,1)S(1)} %get-tuple-element.21), channel_id=1, source_target_pairs={{0,2},{2,0},{1,3},{3,1},{4,6},{6,4},{5,7},{7,5},{8,10},{10,8},{9,1... | collective-permute-start | bytes 3145736 | tf_op jit(solution)/shard_map/ppermute | solution.py:251
  76.7 0.8 copy-start.1
  77.5 1.0 copy-start.8
  77.5 4.7 %copy-start.2 = (bf16[512,512]{1,0:T(8,128)(2,1)S(1)}, bf16[512,512]{1,0:T(8,128)(2,1)}, u32[]{:S(2)}) copy-start(bf16[512,512]{1,0:T(8,128)(2,1)} %copy-done.1) | copy-start | bytes 1572868
  83.5 1.0 copy-start.3
  84.4 31.4 %copy-start.9 = (f32[128,1024]{1,0:T(8,128)S(1)}, f32[128,1024]{1,0:T(8,128)}, u32[]{:S(2)}) copy-start(f32[128,1024]{1,0:T(8,128)} %get-tuple-element.25) | copy-start | bytes 1572868
  84.4 19.2 %all-to-all-start.2 = ((bf16[16,2,32,512]{3,2,1,0:T(8,128)(2,1)}), bf16[16,2,32,512]{3,2,1,0:T(8,128)(2,1)S(1)}, u32[]{:S(2)}, u32[]{:S(2)}) async-start(bf16[16,2,32,512]{3,2,1,0:T(8,128)(2,1)} %copy-done.3), calls=%async_computation.2 | async-start | bytes 2097152 | tf_op jit(solution)/shard_map/all_to_all | solution.py:275
  88.2 27.6 %collective-permute-start.4 = (bf16[128,1024]{1,0:T(8,128)(2,1)}, bf16[128,1024]{1,0:T(8,128)(2,1)S(1)}, u32[]{:S(2)}, u32[]{:S(2)}) collective-permute-start(bf16[128,1024]{1,0:T(8,128)(2,1)} %get-tuple-element.26), channel_id=1, source_target_pairs={{0,192},{64,0},{128,64},{192,128},{1,193},{65,1},{129,65},{193,129... | collective-permute-start | bytes 786440 | tf_op jit(solution)/shard_map/ppermute | solution.py:266
  93.2 18.5 %collective-permute-start.5 = (bf16[128,1024]{1,0:T(8,128)(2,1)}, bf16[128,1024]{1,0:T(8,128)(2,1)S(1)}, u32[]{:S(2)}, u32[]{:S(2)}) collective-permute-start(bf16[128,1024]{1,0:T(8,128)(2,1)} %get-tuple-element.27), channel_id=1, source_target_pairs={{0,128},{64,192},{128,0},{192,64},{1,129},{65,193},{129,1},{193,65... | collective-permute-start | bytes 786440 | tf_op jit(solution)/shard_map/ppermute | solution.py:266
  94.3 21.5 %collective-permute-start.6 = (bf16[128,1024]{1,0:T(8,128)(2,1)}, bf16[128,1024]{1,0:T(8,128)(2,1)S(1)}, u32[]{:S(2)}, u32[]{:S(2)}) collective-permute-start(bf16[128,1024]{1,0:T(8,128)(2,1)} %get-tuple-element.28), channel_id=1, source_target_pairs={{0,64},{64,128},{128,192},{192,0},{1,65},{65,129},{129,193},{193,1... | collective-permute-start | bytes 786440 | tf_op jit(solution)/shard_map/ppermute | solution.py:266
  103.8 14.9 %collective-permute-start.7 = (f32[32,512]{1,0:T(8,128)S(1)}, f32[32,512]{1,0:T(8,128)S(1)}, u32[]{:S(2)}, u32[]{:S(2)}) collective-permute-start(f32[32,512]{1,0:T(8,128)S(1)} %select_bitcast_fusion), channel_id=1, source_target_pairs={{0,32},{32,0},{1,33},{33,1},{2,34},{34,2},{3,35},{35,3},{4,36},{36... | collective-permute-start | bytes 196616 | tf_op jit(solution)/shard_map/ppermute | solution.py:280

commit v5 on v4

--- a/solution.py
+++ b/solution.py
@@ -13,8 +13,10 @@
 GELU_A = 0.7978845608028654
 GELU_B = GELU_A * 0.044715
 PAD = 128
-IMAGE_LIMIT = 54
-TEXT_LIMIT = 20
+FIRST_LIMIT = 20
+SECOND_LIMIT = 20
+IMAGE_LIMIT = 50
+TEXT_LIMIT = 50
 AXES = ("zh", "zl", "xl", "y", "core", "xh")
 SIZES = (4, 2, 2, 4, 2, 2)
 DP = ("zh", "zl", "xl", "y", "core")
@@ -148,8 +150,7 @@
     total[...] = dot(weight[...], texts[...]) + got[...].astype(F32)
     rows = own.shape[0]
     for k, out in enumerate((own, first, second, third)):
-        slot = lax.rem(place[0] + (4 - k), 4)
-        out[...] = total[pl.ds(pl.multiple_of(slot * rows, rows), rows), :].astype(out.dtype)
+        out[...] = total[k * rows : (k + 1) * rows, :].astype(out.dtype)
 
 
 def text_kernel(weight_a, img_a, weight_b, img_b, out):
@@ -198,9 +199,9 @@
     img = (imgs * lax.rsqrt(jnp.sum(imgs * imgs, axis=1, keepdims=True) + 1e-06)).astype(BF)
     code = jnp.stack([labels // 64, labels % 64], axis=1).astype(F32).astype(BF)
     img = jnp.concatenate([img, jnp.pad(code, ((0, 0), (0, PAD - 2)))], axis=1)
-    img_mine = lax.all_to_all(
-        jnp.broadcast_to(img[None], (4,) + img.shape), "zh", split_axis=0, concat_axis=0, tiled=True
-    ).reshape(4 * IMG_ROWS, -1)
+    img_mine = jnp.concatenate(
+        [img] + [lax.ppermute(img, "zh", shift(4, k)) for k in (1, 2, 3)], axis=0
+    )
 
     members = slots[0][None, :] == jnp.arange(CAP_DEV, dtype=jnp.int32)[:, None]
     counts = jnp.sum(members.astype(F32), axis=1)
@@ -220,9 +221,10 @@
             pltpu.SemaphoreType.DMA((5, 2)),
         ),
         cost=LARGE,
-        limit=48,
+        limit=54,
     )
     summed = partial_out + lax.ppermute(partial_out, MP, SWAP)
+    summed, img_mine = lax.optimization_barrier((summed, img_mine))
     pooled = ((states + summed) / counts[:, None]).astype(BF)
     emb = dot(pooled, projection)
     sent = jnp.broadcast_to(emb.astype(BF)[None], (32,) + emb.shape)
@@ -247,10 +249,12 @@
         (scal, place, columns, embs, emb, img_other),
         [(emb.shape, BF), ((n, e), BF), ((images_half, n), BF), ((images_half, e), BF)],
         2,
+        limit=FIRST_LIMIT,
     )
     gi_got = lax.ppermute(gi_send, "core", SWAP)
     (weight_mine,) = call(
-        second_kernel, (scal, columns, texts, img_mine), [((images_half, n), BF)], 1
+        second_kernel, (scal, columns, texts, img_mine), [((images_half, n), BF)], 1,
+        limit=SECOND_LIMIT,
     )
 
     gi_got, weight_mine = lax.optimization_barrier((gi_got, weight_mine))

time: 120 us -> 120 us (level)
  local copies, waits for them, and re-layouts: 5.24 us -> 2.08 us
  starting transfers between devices: 43.5 us -> 45.7 us
  waiting for transfers between devices: 43.4 us -> 41.4 us
  other arithmetic: 4.87 us -> 6.69 us
    ppermute x0 -> x3, starting transfers between devices: none -> 9.35 us  [on_device(): lax.ppermute(img, 'zh', shift(4, k))]
    all_to_all x1 -> x0, starting transfers between devices: 8.18 us -> none  [on_device(): lax.all_to_all(jnp.broadcast_to(img[None], (4,) + img.shape), 'zh', split...]
    unnamed x21 -> x10, local copies, waits for them, and re-layouts: 2.92 us -> 0.72 us
    ppermute x1, waiting for transfers between devices: 1.97 us -> 0.23 us  [on_device(): grad_text = keep + lax.ppermute(give, 'zl', SWAP)]
  transfers between devices with their start and end apart: 11 -> 13, of which waited for: 8 -> 9; matrix products, arithmetic and copies ran while one was open for 5% -> 5% of each run, Pallas kernels for 10% -> 11%
where the time goes in v5:
time: 120 us; the launch traced here: 119 us
  starting transfers between devices  45.7 us (38%)
  waiting for transfers between devices  41.4 us (34%)
  Pallas kernels  20.7 us (17%)
  other arithmetic  6.69 us (6%)
  between operations  2.1 us (2%)
  local copies, waits for them, and re-layouts  2.08 us (2%)
    pallas_call x5, Pallas kernels, call(): pl.pallas_call(kernel, in_specs=in_specs, out_specs=[pl.BlockSpec(memory_...  20.7 us
    ppermute x3, waiting for transfers between devices, on_device(): grad_image += lax.ppermute(part, 'zh', shift(4, -k - 1)).astype(F32)  12.5 us
    ppermute x3, starting transfers between devices, on_device(): lax.ppermute(img, 'zh', shift(4, k))  9.35 us
    ppermute x1, waiting for transfers between devices, on_device(): other = lax.ppermute(tokens, MP, SWAP)  8.95 us
    all_to_all x1, starting transfers between devices, on_device(): embs = lax.all_to_all(sent, group, split_axis=0, concat_axis=0, tiled=True)  8.74 us
    ppermute x3, starting transfers between devices, on_device(): grad_image += lax.ppermute(part, 'zh', shift(4, -k - 1)).astype(F32)  8.45 us
    all_to_all x1, waiting for transfers between devices, on_device(): embs = lax.all_to_all(sent, group, split_axis=0, concat_axis=0, tiled=True)  8.4 us
    all_to_all x1, waiting for transfers between devices, on_device(): lax.all_to_all(gt, ('y', 'xl', 'xh'), split_axis=0, concat_axis=0, tiled=...  7.06 us
  transfers between devices with their start and end apart: 13, of which 9 were waited for; matrix products, arithmetic and copies ran while one was open for 5% of the time, Pallas kernels for 11%

profile of v5, /device:TPU:1, one launch (start us, length us, event | category | flops | bytes accessed | tf_op | source)
XLA Modules:
  0.0 119.0 jit_solution(6108383555964655113)
XLA Ops:
  0.6 0.0 copy-start
  0.6 3.7 %collective-permute-start = (bf16[1024,512]{1,0:T(8,128)(2,1)}, bf16[1024,512]{1,0:T(8,128)(2,1)}, u32[]{:S(2)}, u32[]{:S(2)}) collective-permute-start(bf16[1024,512]{1,0:T(8,128)(2,1)} %tokens.1), channel_id=1, source_target_pairs={{0,1},{1,0},{2,3},{3,2},{4,5},{5,4},{6,7},{7,6},{8,9},{9,8},{10,11... | collective-permute-start | bytes 3145736 | tf_op jit(solution)/shard_map/ppermute | solution.py:196
  4.3 0.7 fusion.6
  5.0 0.1 copy.17
  5.1 1.1 fusion
  6.2 1.1 fusion.1
  7.3 6.1 %collective-permute-start.4 = (bf16[128,1152]{1,0:T(8,128)(2,1)S(1)}, bf16[128,1152]{1,0:T(8,128)(2,1)S(1)}, u32[]{:S(2)}, u32[]{:S(2)}) collective-permute-start(bf16[128,1152]{1,0:T(8,128)(2,1)S(1)} %pad_maximum_fusion.1), channel_id=1, source_target_pairs={{0,192},{64,0},{128,64},{192,128},{1,193},{65,1},{129,65},{193,129... | collective-permute-start | bytes 884744 | tf_op jit(solution)/shard_map/ppermute | solution.py:203
  13.4 1.0 collective-permute-start.3
  14.4 2.3 %collective-permute-start.2 = (bf16[128,1152]{1,0:T(8,128)(2,1)S(1)}, bf16[128,1152]{1,0:T(8,128)(2,1)S(1)}, u32[]{:S(2)}, u32[]{:S(2)}) collective-permute-start(bf16[128,1152]{1,0:T(8,128)(2,1)S(1)} %pad_maximum_fusion.1), channel_id=1, source_target_pairs={{0,64},{64,128},{128,192},{192,0},{1,65},{65,129},{129,193},{193,1... | collective-permute-start | bytes 884744 | tf_op jit(solution)/shard_map/ppermute | solution.py:203
  16.7 0.8 convert_reduce_fusion.1
  17.5 9.0 %collective-permute-done.arrived = bf16[1024,512]{1,0:T(8,128)(2,1)} collective-permute-done((bf16[1024,512]{1,0:T(8,128)(2,1)}, bf16[1024,512]{1,0:T(8,128)(2,1)}, u32[]{:S(2)}, u32[]{:S(2)}) %collective-permute-start) | collective-permute-done | bytes 1048608 | tf_op jit(solution)/shard_map/ppermute | solution.py:196
  26.4 11.6 %shard_map.121 = (f32[32,1024]{1,0:T(8,128)}, f32[32,1024]{1,0:T(8,128)}) custom-call(s32[1]{0:T(128)} %bitcast.1.low, s32[1,1024]{1,0:T(1,128)} %slot.1, bf16[1024,512]{1,0:T(8,128)(2,1)} %tokens.1, bf16[1024,512]{1,0:T(8,128)(2,1)} %collective-permute-done.arrived, f32[1,1024]{1,0:T(1,128)} %bitcast.16, bf16[1024,2048]{1,0:T(8,128)(2,1)} %fc_in.1, ...), custom_call_target="tpu_custom_call" | custom-call | flops 10000000000 | bytes 1000 | tf_op jit(solution)/shard_map/pallas_call | solution.py:179
  38.0 0.0 copy-start.4
  38.0 3.8 %collective-permute-start.1 = (f32[32,1024]{1,0:T(8,128)}, f32[32,1024]{1,0:T(8,128)S(1)}, u32[]{:S(2)}, u32[]{:S(2)}) collective-permute-start(f32[32,1024]{1,0:T(8,128)} %get-tuple-element.20), channel_id=1, source_target_pairs={{0,1},{1,0},{2,3},{3,2},{4,5},{5,4},{6,7},{7,6},{8,9},{9,8},{10,11... | collective-permute-start | bytes 393224 | tf_op jit(solution)/shard_map/ppermute | solution.py:226
  41.8 0.0 collective-permute-done.4
  41.9 0.0 collective-permute-done.3
  41.9 0.1 pad_maximum_fusion.img.img_b
  42.0 2.4 %collective-permute-done.1 = f32[32,1024]{1,0:T(8,128)S(1)} collective-permute-done((f32[32,1024]{1,0:T(8,128)}, f32[32,1024]{1,0:T(8,128)S(1)}, u32[]{:S(2)}, u32[]{:S(2)}) %collective-permute-start.1) | collective-permute-done | bytes 131104 | tf_op jit(solution)/shard_map/ppermute | solution.py:226
  44.5 0.3 fusion.7
  44.8 1.1 broadcast_in_dim.5
  45.9 8.7 %all-to-all-start = ((bf16[32,32,512]{2,1,0:T(8,128)(2,1)}), bf16[32,32,512]{2,1,0:T(8,128)(2,1)}, u32[]{:S(2)}, u32[]{:S(2)}) async-start(bf16[32,32,512]{2,1,0:T(8,128)(2,1)} %broadcast_in_dim.5), calls=%async_computation | async-start | bytes 2097152 | tf_op jit(solution)/shard_map/all_to_all | solution.py:233
  54.7 3.2 %collective-permute-start.5 = (bf16[512,1152]{1,0:T(8,128)(2,1)S(1)}, bf16[512,1152]{1,0:T(8,128)(2,1)S(1)}, u32[]{:S(2)}, u32[]{:S(2)}) collective-permute-start(bf16[512,1152]{1,0:T(8,128)(2,1)S(1)} %pad_maximum_fusion.img.img_b), channel_id=1, source_target_pairs={{0,2},{2,0},{1,3},{3,1},{4,6},{6,4},{5,7},{7,5},{8,10},{10,8},{9,1... | collective-permute-start | bytes 3538952 | tf_op jit(solution)/shard_map/ppermute | solution.py:236
  59.2 0.1 multiply_add_fusion
  59.3 0.1 reshape.112.columns
  59.4 0.1 pad_maximum_fusion.2.scal
  59.5 0.9 collective-permute-done.5.img.img_a
  60.4 8.4 %all-to-all-done = bf16[32,32,512]{2,1,0:T(8,128)(2,1)} async-done(((bf16[32,32,512]{2,1,0:T(8,128)(2,1)}), bf16[32,32,512]{2,1,0:T(8,128)(2,1)}, u32[]{:S(2)}, u32[]{:S(2)}) %all-to-all-start) | async-done | bytes 1048608 | tf_op jit(solution)/shard_map/all_to_all | solution.py:233
  68.8 3.5 %shard_map.122 = (bf16[32,512]{1,0:T(8,128)(2,1)}, bf16[512,1024]{1,0:T(8,128)(2,1)S(1)}, bf16[512,512]{1,0:T(8,128)(2,1)S(1)}, bf16[512,1024]{1,0:T(8,128)(2,1)S(1)}) custom-call(f32[2]{0:T(128)S(1)} %pad_maximum_fusion.2.scal, s32[1]{0:T(128)} %bitcast.place, s32[1,512]{1,0:T(1,128)S(1)} %reshape.112.columns, bf16[16,2,32,512]{3,2,1,0:T(8,128)(2,1)} %bitcast.6.emb, ...), custom_call_target="tpu_custom_call" | custom-call | flops 1000 | bytes 1000 | tf_op jit(solution)/shard_map/pallas_call | solution.py:179
  72.2 4.4 %collective-permute-start.6 = (bf16[512,1024]{1,0:T(8,128)(2,1)S(1)}, bf16[512,1024]{1,0:T(8,128)(2,1)S(1)}, u32[]{:S(2)}, u32[]{:S(2)}) collective-permute-start(bf16[512,1024]{1,0:T(8,128)(2,1)S(1)} %get-tuple-element.25), channel_id=1, source_target_pairs={{0,2},{2,0},{1,3},{3,1},{4,6},{6,4},{5,7},{7,5},{8,10},{10,8},{9,1... | collective-permute-start | bytes 3145736 | tf_op jit(solution)/shard_map/ppermute | solution.py:254
  76.7 1.5 %shard_map.123.weight.weight_b = bf16[512,512]{1,0:T(8,128)(2,1)S(1)} custom-call(f32[2]{0:T(128)S(1)} %pad_maximum_fusion.2.scal, s32[1,512]{1,0:T(1,128)S(1)} %reshape.112.columns, bf16[512,1024]{1,0:T(8,128)(2,1)S(1)} %get-tuple-element.26.texts, bf16[512,1152]{1,0:T(8,128)(2,1)S(1)} %pad_maximum_fusion.img.img_b), custom_call_target="tpu_custom_call" | custom-call | flops 1000 | bytes 1000 | tf_op jit(solution)/shard_map/pallas_call | solution.py:179
  78.1 0.8 collective-permute-done.6.got
  79.0 0.7 shard_map.124
  79.7 0.0 copy-start.2
  79.7 0.7 copy-done.2
  80.4 3.5 %shard_map.125 = bf16[16,2,32,512]{3,2,1,0:T(8,128)(2,1)} custom-call(bf16[512,512]{1,0:T(8,128)(2,1)S(1)} %get-tuple-element.33.weight_a, bf16[512,1152]{1,0:T(8,128)(2,1)S(1)} %collective-permute-done.5.img.img_a, bf16[512,512]{1,0:T(8,128)(2,1)S(1)} %shard_map.123.weight.weight_b, bf16[512,1152]{1,0:T(8,128)(2,1)} %copy-done.1), custom_call_target="tpu_custom_call" | custom-call | flops 1000 | bytes 1000 | tf_op jit(solution)/shard_map/pallas_call | solution.py:179
  83.9 3.7 %all-to-all-start.1 = ((bf16[16,2,32,512]{3,2,1,0:T(8,128)(2,1)}), bf16[16,2,32,512]{3,2,1,0:T(8,128)(2,1)S(1)}, u32[]{:S(2)}, u32[]{:S(2)}) async-start(bf16[16,2,32,512]{3,2,1,0:T(8,128)(2,1)} %shard_map.125), calls=%async_computation.1 | async-start | bytes 2097152 | tf_op jit(solution)/shard_map/all_to_all | solution.py:279
  87.6 5.2 %collective-permute-start.7 = (bf16[128,1024]{1,0:T(8,128)(2,1)S(1)}, bf16[128,1024]{1,0:T(8,128)(2,1)S(1)}, u32[]{:S(2)}, u32[]{:S(2)}) collective-permute-start(bf16[128,1024]{1,0:T(8,128)(2,1)S(1)} %get-tuple-element.30), channel_id=1, source_target_pairs={{0,192},{64,0},{128,64},{192,128},{1,193},{65,1},{129,65},{193,129... | collective-permute-start | bytes 786440 | tf_op jit(solution)/shard_map/ppermute | solution.py:270
  92.8 1.2 collective-permute-start.8
  93.9 2.1 %collective-permute-start.9 = (bf16[128,1024]{1,0:T(8,128)(2,1)S(1)}, bf16[128,1024]{1,0:T(8,128)(2,1)}, u32[]{:S(2)}, u32[]{:S(2)}) collective-permute-start(bf16[128,1024]{1,0:T(8,128)(2,1)S(1)} %get-tuple-element.32), channel_id=1, source_target_pairs={{0,64},{64,128},{128,192},{192,0},{1,65},{65,129},{129,193},{193,1... | collective-permute-start | bytes 786440 | tf_op jit(solution)/shard_map/ppermute | solution.py:270
  96.0 7.1 %all-to-all-done.1 = bf16[16,2,32,512]{3,2,1,0:T(8,128)(2,1)S(1)} async-done(((bf16[16,2,32,512]{3,2,1,0:T(8,128)(2,1)}), bf16[16,2,32,512]{3,2,1,0:T(8,128)(2,1)S(1)}, u32[]{:S(2)}, u32[]{:S(2)}) %all-to-all-start.1) | async-done | bytes 1048608 | tf_op jit(solution)/shard_map/all_to_all | solution.py:279
  103.1 0.1 convert_reduce_fusion
  103.3 0.4 collective-permute-start.10
  103.6 8.0 %collective-permute-done.8 = bf16[128,1024]{1,0:T(8,128)(2,1)} collective-permute-done((bf16[128,1024]{1,0:T(8,128)(2,1)}, bf16[128,1024]{1,0:T(8,128)(2,1)}, u32[]{:S(2)}, u32[]{:S(2)}) %collective-permute-start.8) | collective-permute-done | bytes 262176 | tf_op jit(solution)/shard_map/ppermute | solution.py:270
  111.6 4.5 %collective-permute-done.9 = bf16[128,1024]{1,0:T(8,128)(2,1)} collective-permute-done((bf16[128,1024]{1,0:T(8,128)(2,1)S(1)}, bf16[128,1024]{1,0:T(8,128)(2,1)}, u32[]{:S(2)}, u32[]{:S(2)}) %collective-permute-start.9) | collective-permute-done | bytes 262176 | tf_op jit(solution)/shard_map/ppermute | solution.py:270
  116.1 0.0 collective-permute-done.7
  116.1 2.0 %convert_add_fusion = f32[128,1024]{1,0:T(8,128)} fusion(bf16[128,1024]{1,0:T(8,128)(2,1)} %collective-permute-done.9, bf16[128,1024]{1,0:T(8,128)(2,1)} %collective-permute-done.8, f32[128,1024]{1,0:T(8,128)S(1)} %get-tuple-element.29, bf16[128,1024]{1,0:T(8,128)(2,1)S(1)} %collective-permute-done.7), kind=kLoop, calls=%fused_computation.6 | loop fusion | flops 786432 | bytes 1835008 | tf_op jit(solution)/shard_map/add | solution.py:270
  118.1 0.2 collective-permute-done.10
  118.3 0.6 bitcast_add_fusion
  (14 shorter events, 0.1 us)
Async XLA Ops:
  0.6 43.8 %copy-start = (bf16[1024,512]{1,0:T(8,128)(2,1)S(1)}, bf16[1024,512]{1,0:T(8,128)(2,1)}, u32[]{:S(2)}) copy-start(bf16[1024,512]{1,0:T(8,128)(2,1)} %param.14) | copy-start | bytes 3145732
  0.6 25.8 %collective-permute-start = (bf16[1024,512]{1,0:T(8,128)(2,1)}, bf16[1024,512]{1,0:T(8,128)(2,1)}, u32[]{:S(2)}, u32[]{:S(2)}) collective-permute-start(bf16[1024,512]{1,0:T(8,128)(2,1)} %tokens.1), channel_id=1, source_target_pairs={{0,1},{1,0},{2,3},{3,2},{4,5},{5,4},{6,7},{7,6},{8,9},{9,8},{10,11... | collective-permute-start | bytes 3145736 | tf_op jit(solution)/shard_map/ppermute | solution.py:196
  7.3 34.5 %collective-permute-start.4 = (bf16[128,1152]{1,0:T(8,128)(2,1)S(1)}, bf16[128,1152]{1,0:T(8,128)(2,1)S(1)}, u32[]{:S(2)}, u32[]{:S(2)}) collective-permute-start(bf16[128,1152]{1,0:T(8,128)(2,1)S(1)} %pad_maximum_fusion.1), channel_id=1, source_target_pairs={{0,192},{64,0},{128,64},{192,128},{1,193},{65,1},{129,65},{193,129... | collective-permute-start | bytes 884744 | tf_op jit(solution)/shard_map/ppermute | solution.py:203
  13.4 28.4 %collective-permute-start.3 = (bf16[128,1152]{1,0:T(8,128)(2,1)S(1)}, bf16[128,1152]{1,0:T(8,128)(2,1)S(1)}, u32[]{:S(2)}, u32[]{:S(2)}) collective-permute-start(bf16[128,1152]{1,0:T(8,128)(2,1)S(1)} %pad_maximum_fusion.1), channel_id=1, source_target_pairs={{0,128},{64,192},{128,0},{192,64},{1,129},{65,193},{129,1},{193,65... | collective-permute-start | bytes 884744 | tf_op jit(solution)/shard_map/ppermute | solution.py:203
  14.4 27.4 %collective-permute-start.2 = (bf16[128,1152]{1,0:T(8,128)(2,1)S(1)}, bf16[128,1152]{1,0:T(8,128)(2,1)S(1)}, u32[]{:S(2)}, u32[]{:S(2)}) collective-permute-start(bf16[128,1152]{1,0:T(8,128)(2,1)S(1)} %pad_maximum_fusion.1), channel_id=1, source_target_pairs={{0,64},{64,128},{128,192},{192,0},{1,65},{65,129},{129,193},{193,1... | collective-permute-start | bytes 884744 | tf_op jit(solution)/shard_map/ppermute | solution.py:203
  38.0 6.4 %copy-start.4 = (f32[32,1024]{1,0:T(8,128)S(1)}, f32[32,1024]{1,0:T(8,128)}, u32[]{:S(2)}) copy-start(f32[32,1024]{1,0:T(8,128)} %get-tuple-element.20) | copy-start | bytes 393220
  38.0 6.4 %copy-start.3 = (f32[32,1024]{1,0:T(8,128)S(1)}, f32[32,1024]{1,0:T(8,128)}, u32[]{:S(2)}) copy-start(f32[32,1024]{1,0:T(8,128)} %get-tuple-element.19) | copy-start | bytes 393220
  38.0 6.4 %collective-permute-start.1 = (f32[32,1024]{1,0:T(8,128)}, f32[32,1024]{1,0:T(8,128)S(1)}, u32[]{:S(2)}, u32[]{:S(2)}) collective-permute-start(f32[32,1024]{1,0:T(8,128)} %get-tuple-element.20), channel_id=1, source_target_pairs={{0,1},{1,0},{2,3},{3,2},{4,5},{5,4},{6,7},{7,6},{8,9},{9,8},{10,11... | collective-permute-start | bytes 393224 | tf_op jit(solution)/shard_map/ppermute | solution.py:226
  42.0 34.7 %copy-start.1 = (bf16[512,1152]{1,0:T(8,128)(2,1)}, bf16[512,1152]{1,0:T(8,128)(2,1)S(1)}, u32[]{:S(2)}) copy-start(bf16[512,1152]{1,0:T(8,128)(2,1)S(1)} %pad_maximum_fusion.img.img_b) | copy-start | bytes 3538948
  45.9 22.9 %all-to-all-start = ((bf16[32,32,512]{2,1,0:T(8,128)(2,1)}), bf16[32,32,512]{2,1,0:T(8,128)(2,1)}, u32[]{:S(2)}, u32[]{:S(2)}) async-start(bf16[32,32,512]{2,1,0:T(8,128)(2,1)} %broadcast_in_dim.5), calls=%async_computation | async-start | bytes 2097152 | tf_op jit(solution)/shard_map/all_to_all | solution.py:233
  54.7 5.7 %collective-permute-start.5 = (bf16[512,1152]{1,0:T(8,128)(2,1)S(1)}, bf16[512,1152]{1,0:T(8,128)(2,1)S(1)}, u32[]{:S(2)}, u32[]{:S(2)}) collective-permute-start(bf16[512,1152]{1,0:T(8,128)(2,1)S(1)} %pad_maximum_fusion.img.img_b), channel_id=1, source_target_pairs={{0,2},{2,0},{1,3},{3,1},{4,6},{6,4},{5,7},{7,5},{8,10},{10,8},{9,1... | collective-permute-start | bytes 3538952 | tf_op jit(solution)/shard_map/ppermute | solution.py:236
  72.2 6.7 %collective-permute-start.6 = (bf16[512,1024]{1,0:T(8,128)(2,1)S(1)}, bf16[512,1024]{1,0:T(8,128)(2,1)S(1)}, u32[]{:S(2)}, u32[]{:S(2)}) collective-permute-start(bf16[512,1024]{1,0:T(8,128)(2,1)S(1)} %get-tuple-element.25), channel_id=1, source_target_pairs={{0,2},{2,0},{1,3},{3,1},{4,6},{6,4},{5,7},{7,5},{8,10},{10,8},{9,1... | collective-permute-start | bytes 3145736 | tf_op jit(solution)/shard_map/ppermute | solution.py:254
  79.7 0.7 copy-start.2
  83.9 19.2 %all-to-all-start.1 = ((bf16[16,2,32,512]{3,2,1,0:T(8,128)(2,1)}), bf16[16,2,32,512]{3,2,1,0:T(8,128)(2,1)S(1)}, u32[]{:S(2)}, u32[]{:S(2)}) async-start(bf16[16,2,32,512]{3,2,1,0:T(8,128)(2,1)} %shard_map.125), calls=%async_computation.1 | async-start | bytes 2097152 | tf_op jit(solution)/shard_map/all_to_all | solution.py:279
  87.6 28.6 %collective-permute-start.7 = (bf16[128,1024]{1,0:T(8,128)(2,1)S(1)}, bf16[128,1024]{1,0:T(8,128)(2,1)S(1)}, u32[]{:S(2)}, u32[]{:S(2)}) collective-permute-start(bf16[128,1024]{1,0:T(8,128)(2,1)S(1)} %get-tuple-element.30), channel_id=1, source_target_pairs={{0,192},{64,0},{128,64},{192,128},{1,193},{65,1},{129,65},{193,129... | collective-permute-start | bytes 786440 | tf_op jit(solution)/shard_map/ppermute | solution.py:270
  92.8 18.9 %collective-permute-start.8 = (bf16[128,1024]{1,0:T(8,128)(2,1)}, bf16[128,1024]{1,0:T(8,128)(2,1)}, u32[]{:S(2)}, u32[]{:S(2)}) collective-permute-start(bf16[128,1024]{1,0:T(8,128)(2,1)} %copy-done.2), channel_id=1, source_target_pairs={{0,128},{64,192},{128,0},{192,64},{1,129},{65,193},{129,1},{193,65... | collective-permute-start | bytes 786440 | tf_op jit(solution)/shard_map/ppermute | solution.py:270
  93.9 22.2 %collective-permute-start.9 = (bf16[128,1024]{1,0:T(8,128)(2,1)S(1)}, bf16[128,1024]{1,0:T(8,128)(2,1)}, u32[]{:S(2)}, u32[]{:S(2)}) collective-permute-start(bf16[128,1024]{1,0:T(8,128)(2,1)S(1)} %get-tuple-element.32), channel_id=1, source_target_pairs={{0,64},{64,128},{128,192},{192,0},{1,65},{65,129},{129,193},{193,1... | collective-permute-start | bytes 786440 | tf_op jit(solution)/shard_map/ppermute | solution.py:270
  103.3 15.1 %collective-permute-start.10 = (f32[32,512]{1,0:T(8,128)S(1)}, f32[32,512]{1,0:T(8,128)S(1)}, u32[]{:S(2)}, u32[]{:S(2)}) collective-permute-start(f32[32,512]{1,0:T(8,128)S(1)} %select_bitcast_fusion), channel_id=1, source_target_pairs={{0,32},{32,0},{1,33},{33,1},{2,34},{34,2},{3,35},{35,3},{4,36},{36... | collective-permute-start | bytes 196616 | tf_op jit(solution)/shard_map/ppermute | solution.py:284

commit v6 on v4

--- a/solution.py
+++ b/solution.py
@@ -13,8 +13,10 @@
 GELU_A = 0.7978845608028654
 GELU_B = GELU_A * 0.044715
 PAD = 128
-IMAGE_LIMIT = 54
-TEXT_LIMIT = 20
+FIRST_LIMIT = 20
+SECOND_LIMIT = 20
+IMAGE_LIMIT = 20
+TEXT_LIMIT = 50
 AXES = ("zh", "zl", "xl", "y", "core", "xh")
 SIZES = (4, 2, 2, 4, 2, 2)
 DP = ("zh", "zl", "xl", "y", "core")
@@ -247,10 +249,12 @@
         (scal, place, columns, embs, emb, img_other),
         [(emb.shape, BF), ((n, e), BF), ((images_half, n), BF), ((images_half, e), BF)],
         2,
+        limit=FIRST_LIMIT,
     )
     gi_got = lax.ppermute(gi_send, "core", SWAP)
     (weight_mine,) = call(
-        second_kernel, (scal, columns, texts, img_mine), [((images_half, n), BF)], 1
+        second_kernel, (scal, columns, texts, img_mine), [((images_half, n), BF)], 1,
+        limit=SECOND_LIMIT,
     )
 
     gi_got, weight_mine = lax.optimization_barrier((gi_got, weight_mine))

time: 120 us -> 118 us (0.983)
  local copies, waits for them, and re-layouts: 5.24 us -> 3.28 us
    unnamed x21 -> x15, local copies, waits for them, and re-layouts: 2.92 us -> 0.87 us
  transfers between devices with their start and end apart: 11 -> 11, of which waited for: 8 -> 9; matrix products, arithmetic and copies ran while one was open for 5% -> 6% of each run, Pallas kernels for 10% -> 10%
where the time goes in v6:
time: 118 us
  starting transfers between devices  43.5 us (37%)
  waiting for transfers between devices  42.8 us (36%)
  Pallas kernels  19.5 us (17%)
  other arithmetic  5.98 us (5%)
  local copies, waits for them, and re-layouts  3.28 us (3%)
  between operations  2.09 us (2%)
    pallas_call x5, Pallas kernels, call(): pl.pallas_call(kernel, in_specs=in_specs, out_specs=[pl.BlockSpec(memory_...  19.5 us
    ppermute x3, waiting for transfers between devices, on_device(): grad_image += lax.ppermute(part, 'zh', shift(4, -k - 1)).astype(F32)  11.2 us
    ppermute x1, waiting for transfers between devices, on_device(): other = lax.ppermute(tokens, MP, SWAP)  9.79 us
    all_to_all x1, waiting for transfers between devices, on_device(): embs = lax.all_to_all(sent, group, split_axis=0, concat_axis=0, tiled=True)  9.23 us
    all_to_all x1, starting transfers between devices, on_device(): embs = lax.all_to_all(sent, group, split_axis=0, concat_axis=0, tiled=True)  8.72 us
    all_to_all x1, starting transfers between devices, on_device(): lax.all_to_all(jnp.broadcast_to(img[None], (4,) + img.shape), 'zh', split...  8.18 us
    ppermute x3, starting transfers between devices, on_device(): grad_image += lax.ppermute(part, 'zh', shift(4, -k - 1)).astype(F32)  8.16 us
    all_to_all x1, waiting for transfers between devices, on_device(): lax.all_to_all(gt, ('y', 'xl', 'xh'), split_axis=0, concat_axis=0, tiled=...  7.34 us
  transfers between devices with their start and end apart: 11, of which 9 were waited for; matrix products, arithmetic and copies ran while one was open for 6% of the time, Pallas kernels for 10%

profile of v6, /device:TPU:1, one launch (start us, length us, event | category | flops | bytes accessed | tf_op | source)
XLA Modules:
  0.0 117.5 jit_solution(18372959898308044084)
XLA Ops:
  0.6 0.0 copy-start
  0.6 3.7 %collective-permute-start = (bf16[1024,512]{1,0:T(8,128)(2,1)}, bf16[1024,512]{1,0:T(8,128)(2,1)}, u32[]{:S(2)}, u32[]{:S(2)}) collective-permute-start(bf16[1024,512]{1,0:T(8,128)(2,1)} %tokens.1), channel_id=1, source_target_pairs={{0,1},{1,0},{2,3},{3,2},{4,5},{5,4},{6,7},{7,6},{8,9},{9,8},{10,11... | collective-permute-start | bytes 3145736 | tf_op jit(solution)/shard_map/ppermute | solution.py:197
  4.3 1.1 fusion.1
  5.4 0.7 fusion.8
  6.1 0.1 copy.15
  6.2 1.1 fusion.2
  7.3 0.0 copy-start.2
  7.3 0.0 copy-start.3
  7.3 0.0 copy-start.6
  7.4 1.1 broadcast_in_dim.8
  8.5 8.2 %all-to-all-start.1 = ((bf16[4,128,1152]{2,1,0:T(8,128)(2,1)}), bf16[4,128,1152]{2,1,0:T(8,128)(2,1)S(1)}, u32[]{:S(2)}, u32[]{:S(2)}) async-start(bf16[4,128,1152]{2,1,0:T(8,128)(2,1)} %broadcast_in_dim.8), calls=%async_computation.1 | async-start | bytes 2359296 | tf_op jit(solution)/shard_map/all_to_all | solution.py:203
  16.7 9.8 %collective-permute-done.arrived = bf16[1024,512]{1,0:T(8,128)(2,1)} collective-permute-done((bf16[1024,512]{1,0:T(8,128)(2,1)}, bf16[1024,512]{1,0:T(8,128)(2,1)}, u32[]{:S(2)}, u32[]{:S(2)}) %collective-permute-start) | collective-permute-done | bytes 1048608 | tf_op jit(solution)/shard_map/ppermute | solution.py:197
  26.4 0.0 copy-done.2
  26.5 10.1 %shard_map.121 = (f32[32,1024]{1,0:T(8,128)S(1)}, f32[32,1024]{1,0:T(8,128)S(1)}) custom-call(s32[1]{0:T(128)} %bitcast.1.low, s32[1,1024]{1,0:T(1,128)S(1)} %copy-done.2, bf16[1024,512]{1,0:T(8,128)(2,1)S(1)} %copy-done.3, bf16[1024,512]{1,0:T(8,128)(2,1)} %collective-permute-done.arrived, f32[1,1024]{1,0:T(1,128)S(1)} %bitcast.20, ...), custom_call_target="tpu_custom_call" | custom-call | flops 10000000000 | bytes 1000 | tf_op jit(solution)/shard_map/pallas_call | solution.py:180
  36.5 3.8 %collective-permute-start.1 = (f32[32,1024]{1,0:T(8,128)S(1)}, f32[32,1024]{1,0:T(8,128)S(1)}, u32[]{:S(2)}, u32[]{:S(2)}) collective-permute-start(f32[32,1024]{1,0:T(8,128)S(1)} %get-tuple-element.18), channel_id=1, source_target_pairs={{0,1},{1,0},{2,3},{3,2},{4,5},{5,4},{6,7},{7,6},{8,9},{9,8},{10,11... | collective-permute-start | bytes 393224 | tf_op jit(solution)/shard_map/ppermute | solution.py:227
  40.4 0.1 convert_reduce_fusion.1
  40.5 2.5 %collective-permute-done.1 = f32[32,1024]{1,0:T(8,128)S(1)} collective-permute-done((f32[32,1024]{1,0:T(8,128)S(1)}, f32[32,1024]{1,0:T(8,128)S(1)}, u32[]{:S(2)}, u32[]{:S(2)}) %collective-permute-start.1) | collective-permute-done | bytes 131104 | tf_op jit(solution)/shard_map/ppermute | solution.py:227
  43.0 0.3 fusion.9
  43.4 0.0 all-to-all-done.1
  43.4 1.2 %broadcast_in_dim.7 = bf16[32,32,512]{2,1,0:T(8,128)(2,1)} broadcast(bf16[32,512]{1,0:T(8,128)(2,1)S(1)} %get-tuple-element.33), dimensions={1,2} | broadcast | bytes 1081344 | tf_op jit(solution)/shard_map/broadcast_in_dim | solution.py:230
  44.6 8.7 %all-to-all-start = ((bf16[32,32,512]{2,1,0:T(8,128)(2,1)}), bf16[32,32,512]{2,1,0:T(8,128)(2,1)}, u32[]{:S(2)}, u32[]{:S(2)}) async-start(bf16[32,32,512]{2,1,0:T(8,128)(2,1)} %broadcast_in_dim.7), calls=%async_computation | async-start | bytes 2097152 | tf_op jit(solution)/shard_map/all_to_all | solution.py:233
  53.3 2.8 %collective-permute-start.2 = (bf16[512,1152]{1,0:T(8,128)(2,1)S(1)}, bf16[512,1152]{1,0:T(8,128)(2,1)S(1)}, u32[]{:S(2)}, u32[]{:S(2)}) collective-permute-start(bf16[512,1152]{1,0:T(8,128)(2,1)S(1)} %bitcast.16), channel_id=1, source_target_pairs={{0,2},{2,0},{1,3},{3,1},{4,6},{6,4},{5,7},{7,5},{8,10},{10,8},{9,1... | collective-permute-start | bytes 3538952 | tf_op jit(solution)/shard_map/ppermute | solution.py:236
  57.4 0.1 multiply_add_fusion
  57.5 0.1 reshape.117.columns
  57.6 0.1 pad_maximum_fusion.scal
  57.6 0.9 collective-permute-done.2.img.img_a
  58.6 9.2 %all-to-all-done = bf16[32,32,512]{2,1,0:T(8,128)(2,1)} async-done(((bf16[32,32,512]{2,1,0:T(8,128)(2,1)}), bf16[32,32,512]{2,1,0:T(8,128)(2,1)}, u32[]{:S(2)}, u32[]{:S(2)}) %all-to-all-start) | async-done | bytes 1048608 | tf_op jit(solution)/shard_map/all_to_all | solution.py:233
  67.8 3.5 %shard_map.122 = (bf16[32,512]{1,0:T(8,128)(2,1)}, bf16[512,1024]{1,0:T(8,128)(2,1)S(1)}, bf16[512,512]{1,0:T(8,128)(2,1)S(1)}, bf16[512,1024]{1,0:T(8,128)(2,1)S(1)}) custom-call(f32[2]{0:T(128)S(1)} %pad_maximum_fusion.scal, s32[1]{0:T(128)} %bitcast.place, s32[1,512]{1,0:T(1,128)S(1)} %reshape.117.columns, bf16[16,2,32,512]{3,2,1,0:T(8,128)(2,1)} %bitcast.4.emb, ...), custom_call_target="tpu_custom_call" | custom-call | flops 1000 | bytes 1000 | tf_op jit(solution)/shard_map/pallas_call | solution.py:180
  71.2 4.1 %collective-permute-start.3 = (bf16[512,1024]{1,0:T(8,128)(2,1)S(1)}, bf16[512,1024]{1,0:T(8,128)(2,1)S(1)}, u32[]{:S(2)}, u32[]{:S(2)}) collective-permute-start(bf16[512,1024]{1,0:T(8,128)(2,1)S(1)} %get-tuple-element.21), channel_id=1, source_target_pairs={{0,2},{2,0},{1,3},{3,1},{4,6},{6,4},{5,7},{7,5},{8,10},{10,8},{9,1... | collective-permute-start | bytes 3145736 | tf_op jit(solution)/shard_map/ppermute | solution.py:254
  75.3 1.5 %shard_map.123.weight.weight_b = bf16[512,512]{1,0:T(8,128)(2,1)S(1)} custom-call(f32[2]{0:T(128)S(1)} %pad_maximum_fusion.scal, s32[1,512]{1,0:T(1,128)S(1)} %reshape.117.columns, bf16[512,1024]{1,0:T(8,128)(2,1)S(1)} %get-tuple-element.22.texts, bf16[512,1152]{1,0:T(8,128)(2,1)S(1)} %bitcast.17), custom_call_target="tpu_custom_call" | custom-call | flops 1000 | bytes 1000 | tf_op jit(solution)/shard_map/pallas_call | solution.py:180
  76.8 0.8 collective-permute-done.3.got
  77.6 0.9 shard_map.124
  78.5 0.0 copy-start.4
  78.5 0.7 copy-done.4
  79.2 3.5 %shard_map.125 = bf16[16,2,32,512]{3,2,1,0:T(8,128)(2,1)} custom-call(bf16[512,512]{1,0:T(8,128)(2,1)S(1)} %get-tuple-element.29.weight_a, bf16[512,1152]{1,0:T(8,128)(2,1)S(1)} %collective-permute-done.2.img.img_a, bf16[512,512]{1,0:T(8,128)(2,1)S(1)} %shard_map.123.weight.weight_b, bf16[512,1152]{1,0:T(8,128)(2,1)} %bitcast.18), custom_call_target="tpu_custom_call" | custom-call | flops 1000 | bytes 1000 | tf_op jit(solution)/shard_map/pallas_call | solution.py:180
  82.8 3.8 %all-to-all-start.2 = ((bf16[16,2,32,512]{3,2,1,0:T(8,128)(2,1)}), bf16[16,2,32,512]{3,2,1,0:T(8,128)(2,1)S(1)}, u32[]{:S(2)}, u32[]{:S(2)}) async-start(bf16[16,2,32,512]{3,2,1,0:T(8,128)(2,1)} %shard_map.125), calls=%async_computation.2 | async-start | bytes 2097152 | tf_op jit(solution)/shard_map/all_to_all | solution.py:279
  86.6 4.9 %collective-permute-start.4 = (bf16[128,1024]{1,0:T(8,128)(2,1)S(1)}, bf16[128,1024]{1,0:T(8,128)(2,1)}, u32[]{:S(2)}, u32[]{:S(2)}) collective-permute-start(bf16[128,1024]{1,0:T(8,128)(2,1)S(1)} %get-tuple-element.26), channel_id=1, source_target_pairs={{0,192},{64,0},{128,64},{192,128},{1,193},{65,1},{129,65},{193,129... | collective-permute-start | bytes 786440 | tf_op jit(solution)/shard_map/ppermute | solution.py:270
  91.5 1.1 collective-permute-start.5
  92.6 2.1 %collective-permute-start.6 = (bf16[128,1024]{1,0:T(8,128)(2,1)S(1)}, bf16[128,1024]{1,0:T(8,128)(2,1)}, u32[]{:S(2)}, u32[]{:S(2)}) collective-permute-start(bf16[128,1024]{1,0:T(8,128)(2,1)S(1)} %get-tuple-element.28), channel_id=1, source_target_pairs={{0,64},{64,128},{128,192},{192,0},{1,65},{65,129},{129,193},{193,1... | collective-permute-start | bytes 786440 | tf_op jit(solution)/shard_map/ppermute | solution.py:270
  94.7 7.3 %all-to-all-done.2 = bf16[16,2,32,512]{3,2,1,0:T(8,128)(2,1)S(1)} async-done(((bf16[16,2,32,512]{3,2,1,0:T(8,128)(2,1)}), bf16[16,2,32,512]{3,2,1,0:T(8,128)(2,1)S(1)}, u32[]{:S(2)}, u32[]{:S(2)}) %all-to-all-start.2) | async-done | bytes 1048608 | tf_op jit(solution)/shard_map/all_to_all | solution.py:279
  102.1 0.1 convert_reduce_fusion
  102.2 0.4 collective-permute-start.7
  102.6 7.2 %collective-permute-done.5 = bf16[128,1024]{1,0:T(8,128)(2,1)} collective-permute-done((bf16[128,1024]{1,0:T(8,128)(2,1)S(1)}, bf16[128,1024]{1,0:T(8,128)(2,1)}, u32[]{:S(2)}, u32[]{:S(2)}) %collective-permute-start.5) | collective-permute-done | bytes 262176 | tf_op jit(solution)/shard_map/ppermute | solution.py:270
  109.8 4.0 %collective-permute-done.6 = bf16[128,1024]{1,0:T(8,128)(2,1)} collective-permute-done((bf16[128,1024]{1,0:T(8,128)(2,1)S(1)}, bf16[128,1024]{1,0:T(8,128)(2,1)}, u32[]{:S(2)}, u32[]{:S(2)}) %collective-permute-start.6) | collective-permute-done | bytes 262176 | tf_op jit(solution)/shard_map/ppermute | solution.py:270
  113.8 0.0 collective-permute-done.4
  113.9 2.0 %convert_add_fusion = f32[128,1024]{1,0:T(8,128)} fusion(bf16[128,1024]{1,0:T(8,128)(2,1)} %collective-permute-done.6, bf16[128,1024]{1,0:T(8,128)(2,1)} %collective-permute-done.5, f32[128,1024]{1,0:T(8,128)S(1)} %get-tuple-element.25, bf16[128,1024]{1,0:T(8,128)(2,1)} %collective-permute-done.4), kind=kLoop, calls=%fused_computation.7 | loop fusion | flops 786432 | bytes 1835008 | tf_op jit(solution)/shard_map/add | solution.py:270
  115.9 1.0 collective-permute-done.7
  116.9 0.6 bitcast_add_fusion
  (12 shorter events, 0.1 us)
Async XLA Ops:
  0.6 42.4 %copy-start = (bf16[1024,512]{1,0:T(8,128)(2,1)S(1)}, bf16[1024,512]{1,0:T(8,128)(2,1)}, u32[]{:S(2)}) copy-start(bf16[1024,512]{1,0:T(8,128)(2,1)} %param.14) | copy-start | bytes 3145732
  0.6 25.8 %collective-permute-start = (bf16[1024,512]{1,0:T(8,128)(2,1)}, bf16[1024,512]{1,0:T(8,128)(2,1)}, u32[]{:S(2)}, u32[]{:S(2)}) collective-permute-start(bf16[1024,512]{1,0:T(8,128)(2,1)} %tokens.1), channel_id=1, source_target_pairs={{0,1},{1,0},{2,3},{3,2},{4,5},{5,4},{6,7},{7,6},{8,9},{9,8},{10,11... | collective-permute-start | bytes 3145736 | tf_op jit(solution)/shard_map/ppermute | solution.py:197
  7.3 19.2 %copy-start.2 = (s32[1,1024]{1,0:T(1,128)S(1)}, s32[1,1024]{1,0:T(1,128)}, u32[]{:S(2)}) copy-start(s32[1,1024]{1,0:T(1,128)} %slot.1) | copy-start | bytes 12292
  7.3 19.2 %copy-start.3 = (bf16[1024,512]{1,0:T(8,128)(2,1)S(1)}, bf16[1024,512]{1,0:T(8,128)(2,1)}, u32[]{:S(2)}) copy-start(bf16[1024,512]{1,0:T(8,128)(2,1)} %tokens.1) | copy-start | bytes 3145732
  7.3 19.1 %copy-start.6 = (f32[1024]{0:T(1024)S(1)}, f32[1024]{0:T(1024)}, u32[]{:S(2)}) copy-start(f32[1024]{0:T(1024)} %param.11) | copy-start | bytes 12292
  8.5 34.9 %all-to-all-start.1 = ((bf16[4,128,1152]{2,1,0:T(8,128)(2,1)}), bf16[4,128,1152]{2,1,0:T(8,128)(2,1)S(1)}, u32[]{:S(2)}, u32[]{:S(2)}) async-start(bf16[4,128,1152]{2,1,0:T(8,128)(2,1)} %broadcast_in_dim.8), calls=%async_computation.1 | async-start | bytes 2359296 | tf_op jit(solution)/shard_map/all_to_all | solution.py:203
  36.5 6.5 %collective-permute-start.1 = (f32[32,1024]{1,0:T(8,128)S(1)}, f32[32,1024]{1,0:T(8,128)S(1)}, u32[]{:S(2)}, u32[]{:S(2)}) collective-permute-start(f32[32,1024]{1,0:T(8,128)S(1)} %get-tuple-element.18), channel_id=1, source_target_pairs={{0,1},{1,0},{2,3},{3,2},{4,5},{5,4},{6,7},{7,6},{8,9},{9,8},{10,11... | collective-permute-start | bytes 393224 | tf_op jit(solution)/shard_map/ppermute | solution.py:227
  43.4 31.9 %copy-start.1 = (bf16[4,128,1152]{2,1,0:T(8,128)(2,1)}, bf16[4,128,1152]{2,1,0:T(8,128)(2,1)S(1)}, u32[]{:S(2)}) copy-start(bf16[4,128,1152]{2,1,0:T(8,128)(2,1)S(1)} %all-to-all-done.1) | copy-start | bytes 3538948
  44.6 23.2 %all-to-all-start = ((bf16[32,32,512]{2,1,0:T(8,128)(2,1)}), bf16[32,32,512]{2,1,0:T(8,128)(2,1)}, u32[]{:S(2)}, u32[]{:S(2)}) async-start(bf16[32,32,512]{2,1,0:T(8,128)(2,1)} %broadcast_in_dim.7), calls=%async_computation | async-start | bytes 2097152 | tf_op jit(solution)/shard_map/all_to_all | solution.py:233
  53.3 5.2 %collective-permute-start.2 = (bf16[512,1152]{1,0:T(8,128)(2,1)S(1)}, bf16[512,1152]{1,0:T(8,128)(2,1)S(1)}, u32[]{:S(2)}, u32[]{:S(2)}) collective-permute-start(bf16[512,1152]{1,0:T(8,128)(2,1)S(1)} %bitcast.16), channel_id=1, source_target_pairs={{0,2},{2,0},{1,3},{3,1},{4,6},{6,4},{5,7},{7,5},{8,10},{10,8},{9,1... | collective-permute-start | bytes 3538952 | tf_op jit(solution)/shard_map/ppermute | solution.py:236
  71.2 6.4 %collective-permute-start.3 = (bf16[512,1024]{1,0:T(8,128)(2,1)S(1)}, bf16[512,1024]{1,0:T(8,128)(2,1)S(1)}, u32[]{:S(2)}, u32[]{:S(2)}) collective-permute-start(bf16[512,1024]{1,0:T(8,128)(2,1)S(1)} %get-tuple-element.21), channel_id=1, source_target_pairs={{0,2},{2,0},{1,3},{3,1},{4,6},{6,4},{5,7},{7,5},{8,10},{10,8},{9,1... | collective-permute-start | bytes 3145736 | tf_op jit(solution)/shard_map/ppermute | solution.py:254
  78.5 0.7 copy-start.4
  82.8 8.7 %copy-start.5 = (bf16[128,1024]{1,0:T(8,128)(2,1)S(1)}, bf16[128,1024]{1,0:T(8,128)(2,1)}, u32[]{:S(2)}) copy-start(bf16[128,1024]{1,0:T(8,128)(2,1)} %copy-done.4) | copy-start | bytes 786436
  82.8 19.3 %all-to-all-start.2 = ((bf16[16,2,32,512]{3,2,1,0:T(8,128)(2,1)}), bf16[16,2,32,512]{3,2,1,0:T(8,128)(2,1)S(1)}, u32[]{:S(2)}, u32[]{:S(2)}) async-start(bf16[16,2,32,512]{3,2,1,0:T(8,128)(2,1)} %shard_map.125), calls=%async_computation.2 | async-start | bytes 2097152 | tf_op jit(solution)/shard_map/all_to_all | solution.py:279
  86.6 27.3 %collective-permute-start.4 = (bf16[128,1024]{1,0:T(8,128)(2,1)S(1)}, bf16[128,1024]{1,0:T(8,128)(2,1)}, u32[]{:S(2)}, u32[]{:S(2)}) collective-permute-start(bf16[128,1024]{1,0:T(8,128)(2,1)S(1)} %get-tuple-element.26), channel_id=1, source_target_pairs={{0,192},{64,0},{128,64},{192,128},{1,193},{65,1},{129,65},{193,129... | collective-permute-start | bytes 786440 | tf_op jit(solution)/shard_map/ppermute | solution.py:270
  91.5 18.3 %collective-permute-start.5 = (bf16[128,1024]{1,0:T(8,128)(2,1)S(1)}, bf16[128,1024]{1,0:T(8,128)(2,1)}, u32[]{:S(2)}, u32[]{:S(2)}) collective-permute-start(bf16[128,1024]{1,0:T(8,128)(2,1)S(1)} %copy-done.5), channel_id=1, source_target_pairs={{0,128},{64,192},{128,0},{192,64},{1,129},{65,193},{129,1},{193,65... | collective-permute-start | bytes 786440 | tf_op jit(solution)/shard_map/ppermute | solution.py:270
  92.6 21.2 %collective-permute-start.6 = (bf16[128,1024]{1,0:T(8,128)(2,1)S(1)}, bf16[128,1024]{1,0:T(8,128)(2,1)}, u32[]{:S(2)}, u32[]{:S(2)}) collective-permute-start(bf16[128,1024]{1,0:T(8,128)(2,1)S(1)} %get-tuple-element.28), channel_id=1, source_target_pairs={{0,64},{64,128},{128,192},{192,0},{1,65},{65,129},{129,193},{193,1... | collective-permute-start | bytes 786440 | tf_op jit(solution)/shard_map/ppermute | solution.py:270
  102.2 14.6 %collective-permute-start.7 = (f32[32,512]{1,0:T(8,128)S(1)}, f32[32,512]{1,0:T(8,128)S(1)}, u32[]{:S(2)}, u32[]{:S(2)}) collective-permute-start(f32[32,512]{1,0:T(8,128)S(1)} %select_bitcast_fusion), channel_id=1, source_target_pairs={{0,32},{32,0},{1,33},{33,1},{2,34},{34,2},{3,35},{35,3},{4,36},{36... | collective-permute-start | bytes 196616 | tf_op jit(solution)/shard_map/ppermute | solution.py:284

commit v7 on v6

--- a/solution.py
+++ b/solution.py
@@ -34,6 +34,19 @@
 
 def shift(n, k):
     return [(i, (i + k) % n) for i in range(n)]
+
+
+def prepare_kernel(images, labels, out):
+    e = images.shape[1]
+    rows = images[...].astype(F32)
+    img = (rows * lax.rsqrt(jnp.sum(rows * rows, axis=1, keepdims=True) + 1e-06)).astype(BF)
+    place = lax.broadcasted_iota(jnp.int32, (images.shape[0], PAD), 1)
+    mark = labels[...]
+    code = jnp.where(place == 0, mark >> 6, jnp.where(place == 1, mark & 63, 0))
+    code = code.astype(F32).astype(BF)
+    for i in range(out.shape[0]):
+        out[i, :, :e] = img
+        out[i, :, e:] = code
 
 
 def mlp_kernel(
@@ -196,13 +209,13 @@
 
     other = lax.ppermute(tokens, MP, SWAP)
 
-    imgs = images.astype(F32)
-    img = (imgs * lax.rsqrt(jnp.sum(imgs * imgs, axis=1, keepdims=True) + 1e-06)).astype(BF)
-    code = jnp.stack([labels // 64, labels % 64], axis=1).astype(F32).astype(BF)
-    img = jnp.concatenate([img, jnp.pad(code, ((0, 0), (0, PAD - 2)))], axis=1)
-    img_mine = lax.all_to_all(
-        jnp.broadcast_to(img[None], (4,) + img.shape), "zh", split_axis=0, concat_axis=0, tiled=True
-    ).reshape(4 * IMG_ROWS, -1)
+    (img_sent,) = call(
+        prepare_kernel,
+        (images, labels[:, None]),
+        [((4,) + (images.shape[0], images.shape[1] + PAD), BF)],
+    )
+    img_mine = lax.all_to_all(img_sent, "zh", split_axis=0, concat_axis=0, tiled=True)
+    img_mine = img_mine.reshape(4 * IMG_ROWS, -1)
 
     members = slots[0][None, :] == jnp.arange(CAP_DEV, dtype=jnp.int32)[:, None]
     counts = jnp.sum(members.astype(F32), axis=1)

time: 118 us -> 118 us (level)
  other arithmetic: 5.98 us -> 3.12 us
  waiting for transfers between devices: 42.8 us -> 44.1 us
  Pallas kernels: 19.5 us -> 20.7 us
    ppermute x1, waiting for transfers between devices: 9.79 us -> 11 us  [on_device(): other = lax.ppermute(tokens, MP, SWAP)]
    pallas_call x5 -> x6, Pallas kernels: 19.5 us -> 20.7 us  [call(): pl.pallas_call(kernel, in_specs=in_specs, out_specs=[pl.BlockSpec(memory_...]
  transfers between devices with their start and end apart: 11 -> 11, of which waited for: 9 -> 9; matrix products, arithmetic and copies ran while one was open for 6% -> 3% of each run, Pallas kernels for 10% -> 11%
where the time goes in v7:
time: 118 us
  waiting for transfers between devices  44.1 us (37%)
  starting transfers between devices  43.5 us (37%)
  Pallas kernels  20.7 us (18%)
  local copies, waits for them, and re-layouts  3.71 us (3%)
  other arithmetic  3.12 us (3%)
  between operations  2.07 us (2%)
    pallas_call x6, Pallas kernels, call(): pl.pallas_call(kernel, in_specs=in_specs, out_specs=[pl.BlockSpec(memory_...  20.7 us
    ppermute x3, waiting for transfers between devices, on_device(): grad_image += lax.ppermute(part, 'zh', shift(4, -k - 1)).astype(F32)  11.2 us
    ppermute x1, waiting for transfers between devices, on_device(): other = lax.ppermute(tokens, MP, SWAP)  11 us
    all_to_all x1, waiting for transfers between devices, on_device(): embs = lax.all_to_all(sent, group, split_axis=0, concat_axis=0, tiled=True)  9.25 us
    all_to_all x1, starting transfers between devices, on_device(): embs = lax.all_to_all(sent, group, split_axis=0, concat_axis=0, tiled=True)  8.75 us
    all_to_all x1, starting transfers between devices, on_device(): lax.all_to_all(img_sent, 'zh', split_axis=0, concat_axis=0, tiled=True)  8.18 us
    ppermute x3, starting transfers between devices, on_device(): grad_image += lax.ppermute(part, 'zh', shift(4, -k - 1)).astype(F32)  8.15 us
    all_to_all x1, waiting for transfers between devices, on_device(): lax.all_to_all(gt, ('y', 'xl', 'xh'), split_axis=0, concat_axis=0, tiled=...  7.34 us
  transfers between devices with their start and end apart: 11, of which 9 were waited for; matrix products, arithmetic and copies ran while one was open for 3% of the time, Pallas kernels for 11%

profile of v7, /device:TPU:1, one launch (start us, length us, event | category | flops | bytes accessed | tf_op | source)
XLA Modules:
  0.0 117.5 jit_solution(9076545624400213082)
XLA Ops:
  0.6 0.0 copy-start
  0.6 0.0 copy-start.3
  0.7 0.0 copy-start.7
  0.7 3.7 %collective-permute-start = (bf16[1024,512]{1,0:T(8,128)(2,1)}, bf16[1024,512]{1,0:T(8,128)(2,1)}, u32[]{:S(2)}, u32[]{:S(2)}) collective-permute-start(bf16[1024,512]{1,0:T(8,128)(2,1)} %tokens.1), channel_id=1, source_target_pairs={{0,1},{1,0},{2,3},{3,2},{4,5},{5,4},{6,7},{7,6},{8,9},{9,8},{10,11... | collective-permute-start | bytes 3145736 | tf_op jit(solution)/shard_map/ppermute | solution.py:210
  4.3 0.8 copy.14.labels
  5.1 0.9 copy-done.2
  6.0 1.2 %shard_map.122 = bf16[4,128,1152]{2,1,0:T(8,128)(2,1)} custom-call(bf16[128,1024]{1,0:T(8,128)(2,1)S(1)} %copy-done.2, s32[128,1]{1,0:T(8,128)S(1)} %copy.14.labels), custom_call_target="tpu_custom_call" | custom-call | flops 1000 | bytes 1000 | tf_op jit(solution)/shard_map/pallas_call | solution.py:193
  7.3 8.2 %all-to-all-start.1 = ((bf16[4,128,1152]{2,1,0:T(8,128)(2,1)}), bf16[4,128,1152]{2,1,0:T(8,128)(2,1)S(1)}, u32[]{:S(2)}, u32[]{:S(2)}) async-start(bf16[4,128,1152]{2,1,0:T(8,128)(2,1)} %shard_map.122), calls=%async_computation.1 | async-start | bytes 2359296 | tf_op jit(solution)/shard_map/all_to_all | solution.py:217
  15.5 11.0 %collective-permute-done.arrived = bf16[1024,512]{1,0:T(8,128)(2,1)} collective-permute-done((bf16[1024,512]{1,0:T(8,128)(2,1)}, bf16[1024,512]{1,0:T(8,128)(2,1)}, u32[]{:S(2)}, u32[]{:S(2)}) %collective-permute-start) | collective-permute-done | bytes 1048608 | tf_op jit(solution)/shard_map/ppermute | solution.py:210
  26.5 0.0 copy-done.3
  26.5 0.0 copy-done.7
  26.5 0.0 copy-done.4
  26.5 10.1 %shard_map.121 = (f32[32,1024]{1,0:T(8,128)S(1)}, f32[32,1024]{1,0:T(8,128)S(1)}) custom-call(s32[1]{0:T(128)} %bitcast.1.low, s32[1,1024]{1,0:T(1,128)S(1)} %copy-done.3, bf16[1024,512]{1,0:T(8,128)(2,1)S(1)} %copy-done.4, bf16[1024,512]{1,0:T(8,128)(2,1)} %collective-permute-done.arrived, f32[1,1024]{1,0:T(1,128)S(1)} %bitcast.17, ...), custom_call_target="tpu_custom_call" | custom-call | flops 10000000000 | bytes 1000 | tf_op jit(solution)/shard_map/pallas_call | solution.py:193
  36.6 3.8 %collective-permute-start.1 = (f32[32,1024]{1,0:T(8,128)S(1)}, f32[32,1024]{1,0:T(8,128)S(1)}, u32[]{:S(2)}, u32[]{:S(2)}) collective-permute-start(f32[32,1024]{1,0:T(8,128)S(1)} %get-tuple-element.18), channel_id=1, source_target_pairs={{0,1},{1,0},{2,3},{3,2},{4,5},{5,4},{6,7},{7,6},{8,9},{9,8},{10,11... | collective-permute-start | bytes 393224 | tf_op jit(solution)/shard_map/ppermute | solution.py:240
  40.4 0.1 convert_reduce_fusion.1
  40.5 2.5 %collective-permute-done.1 = f32[32,1024]{1,0:T(8,128)S(1)} collective-permute-done((f32[32,1024]{1,0:T(8,128)S(1)}, f32[32,1024]{1,0:T(8,128)S(1)}, u32[]{:S(2)}, u32[]{:S(2)}) %collective-permute-start.1) | collective-permute-done | bytes 131104 | tf_op jit(solution)/shard_map/ppermute | solution.py:240
  43.0 0.3 fusion.2
  43.3 0.0 all-to-all-done.1
  43.4 1.2 %broadcast_in_dim.7 = bf16[32,32,512]{2,1,0:T(8,128)(2,1)} broadcast(bf16[32,512]{1,0:T(8,128)(2,1)S(1)} %get-tuple-element.31), dimensions={1,2} | broadcast | bytes 1081344 | tf_op jit(solution)/shard_map/broadcast_in_dim | solution.py:243
  44.6 8.8 %all-to-all-start = ((bf16[32,32,512]{2,1,0:T(8,128)(2,1)}), bf16[32,32,512]{2,1,0:T(8,128)(2,1)}, u32[]{:S(2)}, u32[]{:S(2)}) async-start(bf16[32,32,512]{2,1,0:T(8,128)(2,1)} %broadcast_in_dim.7), calls=%async_computation | async-start | bytes 2097152 | tf_op jit(solution)/shard_map/all_to_all | solution.py:246
  53.3 2.8 %collective-permute-start.2 = (bf16[512,1152]{1,0:T(8,128)(2,1)S(1)}, bf16[512,1152]{1,0:T(8,128)(2,1)S(1)}, u32[]{:S(2)}, u32[]{:S(2)}) collective-permute-start(bf16[512,1152]{1,0:T(8,128)(2,1)S(1)} %bitcast.13), channel_id=1, source_target_pairs={{0,2},{2,0},{1,3},{3,1},{4,6},{6,4},{5,7},{7,5},{8,10},{10,8},{9,1... | collective-permute-start | bytes 3538952 | tf_op jit(solution)/shard_map/ppermute | solution.py:249
  57.4 0.1 multiply_add_fusion
  57.5 0.1 reshape.110.columns
  57.6 0.1 pad_maximum_fusion.scal
  57.6 0.9 collective-permute-done.2.img.img_a
  58.6 9.2 %all-to-all-done = bf16[32,32,512]{2,1,0:T(8,128)(2,1)} async-done(((bf16[32,32,512]{2,1,0:T(8,128)(2,1)}), bf16[32,32,512]{2,1,0:T(8,128)(2,1)}, u32[]{:S(2)}, u32[]{:S(2)}) %all-to-all-start) | async-done | bytes 1048608 | tf_op jit(solution)/shard_map/all_to_all | solution.py:246
  67.8 3.5 %shard_map.123 = (bf16[32,512]{1,0:T(8,128)(2,1)}, bf16[512,1024]{1,0:T(8,128)(2,1)S(1)}, bf16[512,512]{1,0:T(8,128)(2,1)S(1)}, bf16[512,1024]{1,0:T(8,128)(2,1)S(1)}) custom-call(f32[2]{0:T(128)S(1)} %pad_maximum_fusion.scal, s32[1]{0:T(128)} %bitcast.place, s32[1,512]{1,0:T(1,128)S(1)} %reshape.110.columns, bf16[16,2,32,512]{3,2,1,0:T(8,128)(2,1)} %bitcast.4.emb, ...), custom_call_target="tpu_custom_call" | custom-call | flops 1000 | bytes 1000 | tf_op jit(solution)/shard_map/pallas_call | solution.py:193
  71.3 4.1 %collective-permute-start.3 = (bf16[512,1024]{1,0:T(8,128)(2,1)S(1)}, bf16[512,1024]{1,0:T(8,128)(2,1)S(1)}, u32[]{:S(2)}, u32[]{:S(2)}) collective-permute-start(bf16[512,1024]{1,0:T(8,128)(2,1)S(1)} %get-tuple-element.21), channel_id=1, source_target_pairs={{0,2},{2,0},{1,3},{3,1},{4,6},{6,4},{5,7},{7,5},{8,10},{10,8},{9,1... | collective-permute-start | bytes 3145736 | tf_op jit(solution)/shard_map/ppermute | solution.py:267
  75.3 1.5 %shard_map.124.weight.weight_b = bf16[512,512]{1,0:T(8,128)(2,1)S(1)} custom-call(f32[2]{0:T(128)S(1)} %pad_maximum_fusion.scal, s32[1,512]{1,0:T(1,128)S(1)} %reshape.110.columns, bf16[512,1024]{1,0:T(8,128)(2,1)S(1)} %get-tuple-element.22.texts, bf16[512,1152]{1,0:T(8,128)(2,1)S(1)} %bitcast.14), custom_call_target="tpu_custom_call" | custom-call | flops 1000 | bytes 1000 | tf_op jit(solution)/shard_map/pallas_call | solution.py:193
  76.8 0.8 collective-permute-done.3.got
  77.6 0.9 shard_map.125
  78.6 0.0 copy-start.5
  78.6 0.7 copy-done.5
  79.3 3.5 %shard_map.126 = bf16[16,2,32,512]{3,2,1,0:T(8,128)(2,1)} custom-call(bf16[512,512]{1,0:T(8,128)(2,1)S(1)} %get-tuple-element.29.weight_a, bf16[512,1152]{1,0:T(8,128)(2,1)S(1)} %collective-permute-done.2.img.img_a, bf16[512,512]{1,0:T(8,128)(2,1)S(1)} %shard_map.124.weight.weight_b, bf16[512,1152]{1,0:T(8,128)(2,1)} %bitcast.15), custom_call_target="tpu_custom_call" | custom-call | flops 1000 | bytes 1000 | tf_op jit(solution)/shard_map/pallas_call | solution.py:193
  82.8 3.8 %all-to-all-start.2 = ((bf16[16,2,32,512]{3,2,1,0:T(8,128)(2,1)}), bf16[16,2,32,512]{3,2,1,0:T(8,128)(2,1)S(1)}, u32[]{:S(2)}, u32[]{:S(2)}) async-start(bf16[16,2,32,512]{3,2,1,0:T(8,128)(2,1)} %shard_map.126), calls=%async_computation.2 | async-start | bytes 2097152 | tf_op jit(solution)/shard_map/all_to_all | solution.py:292
  86.6 4.9 %collective-permute-start.4 = (bf16[128,1024]{1,0:T(8,128)(2,1)S(1)}, bf16[128,1024]{1,0:T(8,128)(2,1)}, u32[]{:S(2)}, u32[]{:S(2)}) collective-permute-start(bf16[128,1024]{1,0:T(8,128)(2,1)S(1)} %get-tuple-element.26), channel_id=1, source_target_pairs={{0,192},{64,0},{128,64},{192,128},{1,193},{65,1},{129,65},{193,129... | collective-permute-start | bytes 786440 | tf_op jit(solution)/shard_map/ppermute | solution.py:283
  91.5 0.0 copy-done.6
  91.5 1.2 collective-permute-start.5
  92.6 2.1 %collective-permute-start.6 = (bf16[128,1024]{1,0:T(8,128)(2,1)S(1)}, bf16[128,1024]{1,0:T(8,128)(2,1)}, u32[]{:S(2)}, u32[]{:S(2)}) collective-permute-start(bf16[128,1024]{1,0:T(8,128)(2,1)S(1)} %get-tuple-element.28), channel_id=1, source_target_pairs={{0,64},{64,128},{128,192},{192,0},{1,65},{65,129},{129,193},{193,1... | collective-permute-start | bytes 786440 | tf_op jit(solution)/shard_map/ppermute | solution.py:283
  94.7 7.3 %all-to-all-done.2 = bf16[16,2,32,512]{3,2,1,0:T(8,128)(2,1)S(1)} async-done(((bf16[16,2,32,512]{3,2,1,0:T(8,128)(2,1)}), bf16[16,2,32,512]{3,2,1,0:T(8,128)(2,1)S(1)}, u32[]{:S(2)}, u32[]{:S(2)}) %all-to-all-start.2) | async-done | bytes 1048608 | tf_op jit(solution)/shard_map/all_to_all | solution.py:292
  102.1 0.1 convert_reduce_fusion
  102.2 0.4 collective-permute-start.7
  102.6 7.1 %collective-permute-done.5 = bf16[128,1024]{1,0:T(8,128)(2,1)} collective-permute-done((bf16[128,1024]{1,0:T(8,128)(2,1)S(1)}, bf16[128,1024]{1,0:T(8,128)(2,1)}, u32[]{:S(2)}, u32[]{:S(2)}) %collective-permute-start.5) | collective-permute-done | bytes 262176 | tf_op jit(solution)/shard_map/ppermute | solution.py:283
  109.8 4.1 %collective-permute-done.6 = bf16[128,1024]{1,0:T(8,128)(2,1)} collective-permute-done((bf16[128,1024]{1,0:T(8,128)(2,1)S(1)}, bf16[128,1024]{1,0:T(8,128)(2,1)}, u32[]{:S(2)}, u32[]{:S(2)}) %collective-permute-start.6) | collective-permute-done | bytes 262176 | tf_op jit(solution)/shard_map/ppermute | solution.py:283
  113.9 0.0 collective-permute-done.4
  113.9 2.0 %convert_add_fusion = f32[128,1024]{1,0:T(8,128)} fusion(bf16[128,1024]{1,0:T(8,128)(2,1)} %collective-permute-done.6, bf16[128,1024]{1,0:T(8,128)(2,1)} %collective-permute-done.5, f32[128,1024]{1,0:T(8,128)S(1)} %get-tuple-element.25, bf16[128,1024]{1,0:T(8,128)(2,1)} %collective-permute-done.4), kind=kLoop, calls=%fused_computation.1 | loop fusion | flops 786432 | bytes 1835008 | tf_op jit(solution)/shard_map/add | solution.py:283
  115.9 1.0 collective-permute-done.7
  116.9 0.6 bitcast_add_fusion
  (8 shorter events, 0.0 us)
Async XLA Ops:
  0.6 42.4 %copy-start = (bf16[1024,512]{1,0:T(8,128)(2,1)S(1)}, bf16[1024,512]{1,0:T(8,128)(2,1)}, u32[]{:S(2)}) copy-start(bf16[1024,512]{1,0:T(8,128)(2,1)} %param.14) | copy-start | bytes 3145732
  0.6 25.8 %copy-start.3 = (s32[1,1024]{1,0:T(1,128)S(1)}, s32[1,1024]{1,0:T(1,128)}, u32[]{:S(2)}) copy-start(s32[1,1024]{1,0:T(1,128)} %slot.1) | copy-start | bytes 12292
  0.7 25.8 %copy-start.7 = (f32[1024]{0:T(1024)S(1)}, f32[1024]{0:T(1024)}, u32[]{:S(2)}) copy-start(f32[1024]{0:T(1024)} %param.11) | copy-start | bytes 12292
  0.7 25.8 %collective-permute-start = (bf16[1024,512]{1,0:T(8,128)(2,1)}, bf16[1024,512]{1,0:T(8,128)(2,1)}, u32[]{:S(2)}, u32[]{:S(2)}) collective-permute-start(bf16[1024,512]{1,0:T(8,128)(2,1)} %tokens.1), channel_id=1, source_target_pairs={{0,1},{1,0},{2,3},{3,2},{4,5},{5,4},{6,7},{7,6},{8,9},{9,8},{10,11... | collective-permute-start | bytes 3145736 | tf_op jit(solution)/shard_map/ppermute | solution.py:210
  5.1 0.9 copy-start.2
  6.0 20.4 %copy-start.4 = (bf16[1024,512]{1,0:T(8,128)(2,1)S(1)}, bf16[1024,512]{1,0:T(8,128)(2,1)}, u32[]{:S(2)}) copy-start(bf16[1024,512]{1,0:T(8,128)(2,1)} %tokens.1) | copy-start | bytes 3145732
  7.3 36.1 %all-to-all-start.1 = ((bf16[4,128,1152]{2,1,0:T(8,128)(2,1)}), bf16[4,128,1152]{2,1,0:T(8,128)(2,1)S(1)}, u32[]{:S(2)}, u32[]{:S(2)}) async-start(bf16[4,128,1152]{2,1,0:T(8,128)(2,1)} %shard_map.122), calls=%async_computation.1 | async-start | bytes 2359296 | tf_op jit(solution)/shard_map/all_to_all | solution.py:217
  36.6 6.4 %collective-permute-start.1 = (f32[32,1024]{1,0:T(8,128)S(1)}, f32[32,1024]{1,0:T(8,128)S(1)}, u32[]{:S(2)}, u32[]{:S(2)}) collective-permute-start(f32[32,1024]{1,0:T(8,128)S(1)} %get-tuple-element.18), channel_id=1, source_target_pairs={{0,1},{1,0},{2,3},{3,2},{4,5},{5,4},{6,7},{7,6},{8,9},{9,8},{10,11... | collective-permute-start | bytes 393224 | tf_op jit(solution)/shard_map/ppermute | solution.py:240
  43.4 32.0 %copy-start.1 = (bf16[4,128,1152]{2,1,0:T(8,128)(2,1)}, bf16[4,128,1152]{2,1,0:T(8,128)(2,1)S(1)}, u32[]{:S(2)}) copy-start(bf16[4,128,1152]{2,1,0:T(8,128)(2,1)S(1)} %all-to-all-done.1) | copy-start | bytes 3538948
  44.6 23.2 %all-to-all-start = ((bf16[32,32,512]{2,1,0:T(8,128)(2,1)}), bf16[32,32,512]{2,1,0:T(8,128)(2,1)}, u32[]{:S(2)}, u32[]{:S(2)}) async-start(bf16[32,32,512]{2,1,0:T(8,128)(2,1)} %broadcast_in_dim.7), calls=%async_computation | async-start | bytes 2097152 | tf_op jit(solution)/shard_map/all_to_all | solution.py:246
  53.3 5.2 %collective-permute-start.2 = (bf16[512,1152]{1,0:T(8,128)(2,1)S(1)}, bf16[512,1152]{1,0:T(8,128)(2,1)S(1)}, u32[]{:S(2)}, u32[]{:S(2)}) collective-permute-start(bf16[512,1152]{1,0:T(8,128)(2,1)S(1)} %bitcast.13), channel_id=1, source_target_pairs={{0,2},{2,0},{1,3},{3,1},{4,6},{6,4},{5,7},{7,5},{8,10},{10,8},{9,1... | collective-permute-start | bytes 3538952 | tf_op jit(solution)/shard_map/ppermute | solution.py:249
  71.3 6.4 %collective-permute-start.3 = (bf16[512,1024]{1,0:T(8,128)(2,1)S(1)}, bf16[512,1024]{1,0:T(8,128)(2,1)S(1)}, u32[]{:S(2)}, u32[]{:S(2)}) collective-permute-start(bf16[512,1024]{1,0:T(8,128)(2,1)S(1)} %get-tuple-element.21), channel_id=1, source_target_pairs={{0,2},{2,0},{1,3},{3,1},{4,6},{6,4},{5,7},{7,5},{8,10},{10,8},{9,1... | collective-permute-start | bytes 3145736 | tf_op jit(solution)/shard_map/ppermute | solution.py:267
  78.6 0.7 copy-start.5
  82.8 8.7 %copy-start.6 = (bf16[128,1024]{1,0:T(8,128)(2,1)S(1)}, bf16[128,1024]{1,0:T(8,128)(2,1)}, u32[]{:S(2)}) copy-start(bf16[128,1024]{1,0:T(8,128)(2,1)} %copy-done.5) | copy-start | bytes 786436
  82.8 19.3 %all-to-all-start.2 = ((bf16[16,2,32,512]{3,2,1,0:T(8,128)(2,1)}), bf16[16,2,32,512]{3,2,1,0:T(8,128)(2,1)S(1)}, u32[]{:S(2)}, u32[]{:S(2)}) async-start(bf16[16,2,32,512]{3,2,1,0:T(8,128)(2,1)} %shard_map.126), calls=%async_computation.2 | async-start | bytes 2097152 | tf_op jit(solution)/shard_map/all_to_all | solution.py:292
  86.6 27.3 %collective-permute-start.4 = (bf16[128,1024]{1,0:T(8,128)(2,1)S(1)}, bf16[128,1024]{1,0:T(8,128)(2,1)}, u32[]{:S(2)}, u32[]{:S(2)}) collective-permute-start(bf16[128,1024]{1,0:T(8,128)(2,1)S(1)} %get-tuple-element.26), channel_id=1, source_target_pairs={{0,192},{64,0},{128,64},{192,128},{1,193},{65,1},{129,65},{193,129... | collective-permute-start | bytes 786440 | tf_op jit(solution)/shard_map/ppermute | solution.py:283
  91.5 18.3 %collective-permute-start.5 = (bf16[128,1024]{1,0:T(8,128)(2,1)S(1)}, bf16[128,1024]{1,0:T(8,128)(2,1)}, u32[]{:S(2)}, u32[]{:S(2)}) collective-permute-start(bf16[128,1024]{1,0:T(8,128)(2,1)S(1)} %copy-done.6), channel_id=1, source_target_pairs={{0,128},{64,192},{128,0},{192,64},{1,129},{65,193},{129,1},{193,65... | collective-permute-start | bytes 786440 | tf_op jit(solution)/shard_map/ppermute | solution.py:283
  92.6 21.2 %collective-permute-start.6 = (bf16[128,1024]{1,0:T(8,128)(2,1)S(1)}, bf16[128,1024]{1,0:T(8,128)(2,1)}, u32[]{:S(2)}, u32[]{:S(2)}) collective-permute-start(bf16[128,1024]{1,0:T(8,128)(2,1)S(1)} %get-tuple-element.28), channel_id=1, source_target_pairs={{0,64},{64,128},{128,192},{192,0},{1,65},{65,129},{129,193},{193,1... | collective-permute-start | bytes 786440 | tf_op jit(solution)/shard_map/ppermute | solution.py:283
  102.2 14.6 %collective-permute-start.7 = (f32[32,512]{1,0:T(8,128)S(1)}, f32[32,512]{1,0:T(8,128)S(1)}, u32[]{:S(2)}, u32[]{:S(2)}) collective-permute-start(f32[32,512]{1,0:T(8,128)S(1)} %select_bitcast_fusion), channel_id=1, source_target_pairs={{0,32},{32,0},{1,33},{33,1},{2,34},{34,2},{3,35},{35,3},{4,36},{36... | collective-permute-start | bytes 196616 | tf_op jit(solution)/shard_map/ppermute | solution.py:297
